TPU v7x, 32 devices: a whole 2x2x4 slice. The times are simulated.
32 devices in a mesh: fsdp: 32 (over z, y, x, core).
Axes of the slice: x: 2, y: 2, z: 4, core: 2. Of those that a mesh axis runs over, the one named last changes fastest.
Arguments:
- tokens: bfloat16 [32768, 768], P('fsdp'), may hold values from -6 to 6
- cotangent: bfloat16 [32768, 768], P('fsdp'), may hold values from -6 to 6
- lengths: int32 [32, 4], P('fsdp'), may hold values from 0 to 1024, as said below
- routes: int32 [32768, 1], P('fsdp'), may hold values from 0 to 3; in each aligned block of 1024 rows (0 to 1023, 1024 to 2047, ...) at most 512 rows name the same one
- gain_attn: bfloat16 [768], P('fsdp'), may hold values from 0.5 to 1.5
- w_qkv: bfloat16 [768, 2304], P('fsdp'), may hold values from -0.21875 to 0.21875
- w_out: bfloat16 [768, 768], P('fsdp'), may hold values from -1.75 to 1.75
- table: bfloat16 [32, 12], replicated, may hold values from -4 to 4
- gain_ffn: bfloat16 [768], P('fsdp'), may hold values from 0.5 to 1.5
- router: bfloat16 [768, 4], P('fsdp'), may hold values from -0.21875 to 0.21875
- expert_up: bfloat16 [3072, 4, 768], P('fsdp'), may hold values from -0.21875 to 0.21875
- expert_down: bfloat16 [3072, 4, 768], P('fsdp'), may hold values from -0.4375 to 0.4375
Outputs:
- output: bfloat16 [32768, 768], P('fsdp')
- grad_tokens: bfloat16 [32768, 768], P('fsdp')
- grad_gain_attn: float32 [768], P('fsdp')
- grad_w_qkv: float32 [768, 2304], P('fsdp')
- grad_w_out: float32 [768, 768], P('fsdp')
- grad_table: float32 [32, 12], replicated
- grad_gain_ffn: float32 [768], P('fsdp')
- grad_router: float32 [768, 4], P('fsdp')
- grad_up: float32 [3072, 4, 768], P('fsdp')
- grad_down: float32 [3072, 4, 768], P('fsdp')
Inputs may be any that keep to these rules, and one draw needn't show every extreme that they name: `lengths`: each row sums to 1024; some row is one sequence of 1024 tokens. `routes`: among the 1024 rows of one device no expert is named more than 512 times, a bound that some block reaches.
All inputs are finite; a program needn't handle non-finite values.
Results may differ from a plain program's by a relative error of at most 0.015.
Values may be sent and summed in bfloat16 or wider, within the bound.
No kernel may reach another device: no remote copies, remote signals or barrier semaphores. Data moves between devices by JAX's collectives and lax.ppermute only.
A program may use at most 448 MiB of HBM per device.

v0:
```python
import jax
import jax.numpy as jnp
from jax import lax
from jax.sharding import PartitionSpec as P

D = 768
HEADS = 12
HEAD_DIM = 64
BUCKETS = 32
EXPERTS = 4
TOK_DEV = 1024
CAP = 512


norm_eps = 1e-06
masked_fill = -1e30
far_steps = (12, 16, 23, 32, 46, 64, 91)


def bucket_of(offset):
    distance = jnp.abs(offset)
    far_bucket = 8 + sum(((distance >= step).astype(jnp.int32) for step in far_steps))
    return jnp.where(distance < 8, distance, far_bucket) + 16 * (offset > 0).astype(jnp.int32)


def rms_norm(values, gain):
    return values * lax.rsqrt(jnp.mean(values * values, axis=-1, keepdims=True) + norm_eps) * gain


def body(
    tokens,
    cotangent,
    lengths,
    routes,
    gain_attn,
    w_qkv,
    w_out,
    table,
    gain_ffn,
    router,
    expert_up,
    expert_down,
):
    params = (
        lax.all_gather(gain_attn, "fsdp", axis=0, tiled=True),
        lax.all_gather(w_qkv, "fsdp", axis=0, tiled=True),
        lax.all_gather(w_out, "fsdp", axis=0, tiled=True),
        lax.all_gather(gain_ffn, "fsdp", axis=0, tiled=True),
        lax.all_gather(router, "fsdp", axis=0, tiled=True),
    )
    tokens_f = tokens.astype(jnp.float32)
    gain_first = params[0].astype(jnp.float32)
    normed = rms_norm(tokens_f, gain_first).astype(jnp.bfloat16)
    qkv_rows = jnp.dot(normed, params[1], preferred_element_type=jnp.float32).astype(jnp.bfloat16)
    queries = qkv_rows[:, :D].reshape(TOK_DEV, HEADS, HEAD_DIM)
    key_rows = qkv_rows[:, D : 2 * D].reshape(TOK_DEV, HEADS, HEAD_DIM)
    value_rows = qkv_rows[:, 2 * D :].reshape(TOK_DEV, HEADS, HEAD_DIM)
    ends = jnp.cumsum(lengths[0])
    places = lax.iota(jnp.int32, TOK_DEV)
    doc_ids = jnp.sum((places[:, None] >= ends[None, :]).astype(jnp.int32), axis=1)
    bucket_ids = lax.iota(jnp.int32, BUCKETS)
    block_rows = min(512, TOK_DEV)
    block_count = TOK_DEV // block_rows

    def block_scores(first):
        rows_at = first + lax.iota(jnp.int32, block_rows)
        buckets = bucket_of(places[None, :] - rows_at[:, None])
        onehot = (buckets[:, :, None] == bucket_ids[None, None, :]).astype(jnp.bfloat16)
        raw = (
            jnp.einsum(
                "qhd,khd->hqk",
                queries[first : first + block_rows],
                key_rows,
                preferred_element_type=jnp.float32,
            )
            * 0.125
        )
        same_doc = doc_ids[first : first + block_rows, None] == doc_ids[None, :]
        bias = jnp.einsum("qkb,bh->hqk", onehot, table, preferred_element_type=jnp.float32)
        scores = raw + bias
        return (jnp.where(same_doc[None], scores, masked_fill), onehot)

    mixed_blocks = []
    log_totals = []
    for block_index in range(block_count):
        masked, unused_onehot = block_scores(block_index * block_rows)
        top = jnp.max(masked, axis=-1, keepdims=True)
        expo = jnp.exp(masked - top)
        total = jnp.sum(expo, axis=-1, keepdims=True)
        probs_low = (expo / total).astype(jnp.bfloat16)
        mixed_blocks.append(
            jnp.einsum("hqk,khd->qhd", probs_low, value_rows, preferred_element_type=jnp.float32)
        )
        log_totals.append(top + jnp.log(total))
    mixed = jnp.concatenate(mixed_blocks, axis=0).reshape(TOK_DEV, D).astype(jnp.bfloat16)
    attended = tokens_f + jnp.dot(mixed, params[2], preferred_element_type=jnp.float32)
    gain_second = params[3].astype(jnp.float32)
    normed_ffn = rms_norm(attended, gain_second).astype(jnp.bfloat16)
    logits = jnp.dot(normed_ffn, params[4], preferred_element_type=jnp.float32)
    probs_route = jax.nn.softmax(logits, axis=-1)
    route = routes[:, 0]
    chosen = (route[:, None] == lax.iota(jnp.int32, EXPERTS)[None, :]).astype(jnp.int32)
    rank = jnp.sum((jnp.cumsum(chosen, axis=0) - chosen) * chosen, axis=1)
    slot = route * CAP + rank
    route_hot = chosen.astype(jnp.float32)
    gate_value = jnp.sum(probs_route * route_hot, axis=1, keepdims=True)
    dispatched = (
        jnp.zeros((EXPERTS * CAP, D), jnp.bfloat16)
        .at[slot]
        .set(normed_ffn)
        .reshape(EXPERTS, CAP, D)
    )
    up_piece = lax.all_gather(expert_up, "fsdp", axis=0, tiled=True)
    down_piece = lax.all_gather(expert_down, "fsdp", axis=0, tiled=True)
    pre_act = jnp.einsum("ecd,fed->ecf", dispatched, up_piece, preferred_element_type=jnp.float32)
    hidden = jax.nn.gelu(pre_act).astype(jnp.bfloat16)
    expert_total = jnp.einsum(
        "ecf,fed->ecd", hidden, down_piece, preferred_element_type=jnp.float32
    )
    expert_tok = expert_total.reshape(EXPERTS * CAP, D)[slot]
    output = (attended + gate_value * expert_tok).astype(jnp.bfloat16)
    upstream = cotangent.astype(jnp.float32)
    grad_gate = jnp.sum(upstream * expert_tok, axis=1, keepdims=True)
    grad_logits = (probs_route * (grad_gate * route_hot - grad_gate * gate_value)).astype(
        jnp.bfloat16
    )
    grad_expert_tok = (gate_value * upstream).astype(jnp.bfloat16)
    grad_dispatched = (
        jnp.zeros((EXPERTS * CAP, D), jnp.bfloat16)
        .at[slot]
        .set(grad_expert_tok)
        .reshape(EXPERTS, CAP, D)
    )
    back_params = (
        lax.all_gather(gain_attn, "fsdp", axis=0, tiled=True),
        lax.all_gather(w_qkv, "fsdp", axis=0, tiled=True),
        lax.all_gather(w_out, "fsdp", axis=0, tiled=True),
        lax.all_gather(gain_ffn, "fsdp", axis=0, tiled=True),
        lax.all_gather(router, "fsdp", axis=0, tiled=True),
    )
    up_piece = lax.all_gather(expert_up, "fsdp", axis=0, tiled=True)
    down_piece = lax.all_gather(expert_down, "fsdp", axis=0, tiled=True)
    pre_act = jnp.einsum("ecd,fed->ecf", dispatched, up_piece, preferred_element_type=jnp.float32)
    hidden, gelu_pull = jax.vjp(jax.nn.gelu, pre_act)
    grad_hidden = jnp.einsum(
        "ecd,fed->ecf", grad_dispatched, down_piece, preferred_element_type=jnp.float32
    )
    grad_pre = gelu_pull(grad_hidden)[0].astype(jnp.bfloat16)
    grad_rows = jnp.einsum("ecf,fed->ecd", grad_pre, up_piece, preferred_element_type=jnp.float32)
    expert_hidden_store = hidden.astype(jnp.bfloat16)
    grad_rows, hidden_store, grad_pre_store = (grad_rows, expert_hidden_store, grad_pre)
    expert_sums = lax.psum_scatter(
        jnp.concatenate(
            [
                jnp.einsum(
                    "ecf,ecd->fed", grad_pre_store, dispatched, preferred_element_type=jnp.float32
                ),
                jnp.einsum(
                    "ecf,ecd->fed",
                    hidden_store,
                    grad_dispatched,
                    preferred_element_type=jnp.float32,
                ),
            ],
            axis=1,
        ),
        "fsdp",
        scatter_dimension=0,
        tiled=True,
    )
    down_sums = expert_sums[:, EXPERTS:]
    grad_normed_ffn = grad_rows.reshape(EXPERTS * CAP, D)[slot] + jnp.einsum(
        "te,de->td", grad_logits, back_params[4], preferred_element_type=jnp.float32
    )
    unused_second, second_pull = jax.vjp(rms_norm, attended, back_params[3].astype(jnp.float32))
    grad_res_norm, grad_gain_second = second_pull(grad_normed_ffn)
    grad_res = upstream + grad_res_norm
    grad_attn_out = grad_res.astype(jnp.bfloat16)
    grad_w_out = jnp.einsum("td,tf->df", mixed, grad_attn_out, preferred_element_type=jnp.float32)
    grad_mixed = (
        jnp.einsum("tf,df->td", grad_attn_out, back_params[2], preferred_element_type=jnp.float32)
        .astype(jnp.bfloat16)
        .reshape(TOK_DEV, HEADS, HEAD_DIM)
    )
    grad_keys = jnp.zeros((TOK_DEV, HEADS, HEAD_DIM), jnp.float32)
    grad_values = jnp.zeros((TOK_DEV, HEADS, HEAD_DIM), jnp.float32)
    grad_table = jnp.zeros((BUCKETS, HEADS), jnp.float32)
    grad_query_blocks = []
    for block_index in range(block_count):
        first = block_index * block_rows
        masked, onehot = block_scores(first)
        probs = jnp.exp(masked - log_totals[block_index])
        probs_low = probs.astype(jnp.bfloat16)
        grad_block = grad_mixed[first : first + block_rows]
        grad_values = grad_values + jnp.einsum(
            "hqk,qhd->khd", probs_low, grad_block, preferred_element_type=jnp.float32
        )
        grad_probs = jnp.einsum(
            "qhd,khd->hqk", grad_block, value_rows, preferred_element_type=jnp.float32
        )
        grad_scores = (
            probs * (grad_probs - jnp.sum(probs * grad_probs, axis=-1, keepdims=True))
        ).astype(jnp.bfloat16)
        grad_query_blocks.append(
            jnp.einsum("hqk,khd->qhd", grad_scores, key_rows, preferred_element_type=jnp.float32)
            * 0.125
        )
        grad_keys = (
            grad_keys
            + jnp.einsum(
                "hqk,qhd->khd",
                grad_scores,
                queries[first : first + block_rows],
                preferred_element_type=jnp.float32,
            )
            * 0.125
        )
        grad_table = grad_table + jnp.einsum(
            "hqk,qkb->bh", grad_scores, onehot, preferred_element_type=jnp.float32
        )
    grad_queries = jnp.concatenate(grad_query_blocks, axis=0)
    grad_qkv = jnp.concatenate(
        [
            grad_queries.reshape(TOK_DEV, D),
            grad_keys.reshape(TOK_DEV, D),
            grad_values.reshape(TOK_DEV, D),
        ],
        axis=1,
    ).astype(jnp.bfloat16)
    grad_w_qkv = jnp.einsum("td,tf->df", normed, grad_qkv, preferred_element_type=jnp.float32)
    grad_normed = jnp.einsum(
        "tf,df->td", grad_qkv, back_params[1], preferred_element_type=jnp.float32
    )
    unused_first, first_pull = jax.vjp(rms_norm, tokens_f, back_params[0].astype(jnp.float32))
    grad_tok_norm, grad_gain_first = first_pull(grad_normed)
    grad_tokens = (grad_res + grad_tok_norm).astype(jnp.bfloat16)
    grad_router = jnp.einsum(
        "td,te->de", normed_ffn, grad_logits, preferred_element_type=jnp.float32
    )
    up_sums = expert_sums[:, :EXPERTS]
    dense = (
        lax.psum_scatter(grad_gain_first, "fsdp", scatter_dimension=0, tiled=True),
        lax.psum_scatter(grad_w_qkv, "fsdp", scatter_dimension=0, tiled=True),
        lax.psum_scatter(grad_w_out, "fsdp", scatter_dimension=0, tiled=True),
        lax.psum_scatter(grad_gain_second, "fsdp", scatter_dimension=0, tiled=True),
        lax.psum_scatter(grad_router, "fsdp", scatter_dimension=0, tiled=True),
    )
    table_sum = lax.psum(grad_table, "fsdp")
    return (
        output,
        grad_tokens,
        dense[0],
        dense[1],
        dense[2],
        table_sum,
        dense[3],
        dense[4],
        up_sums,
        down_sums,
    )


def solution(mesh):
    in_specs = (
        P("fsdp", None),
        P("fsdp", None),
        P("fsdp", None),
        P("fsdp", None),
        P("fsdp"),
        P("fsdp", None),
        P("fsdp", None),
        P(),
        P("fsdp"),
        P("fsdp", None),
        P("fsdp", None, None),
        P("fsdp", None, None),
    )
    out_specs = (
        P("fsdp", None),
        P("fsdp", None),
        P("fsdp"),
        P("fsdp", None),
        P("fsdp", None),
        P(),
        P("fsdp"),
        P("fsdp", None),
        P("fsdp", None, None),
        P("fsdp", None, None),
    )
    return jax.shard_map(body, mesh=mesh, in_specs=in_specs, out_specs=out_specs, check_vma=False)
```

profile of v0, /device:TPU:0, one launch (start us, length us, event | category | flops | bytes accessed | tf_op | source)
XLA Modules:
  0.0 1521.4 jit_solution(11246120961089510033)
XLA Ops:
  15.8 42.2 %all-reduce.6 = (bf16[768]{0:T(1024)(128)(2,1)S(1)}, bf16[768]{0:T(1024)(128)(2,1)S(1)}) all-reduce(bf16[768]{0:T(1024)(128)(2,1)S(1)} %dynamic-update-slice, bf16[768]{0:T(1024)(128)(2,1)S(1)} %dynamic-update-slice.1), channel_id=1, replica_groups=mesh['fsdp'=32] {'fsdp'}, use_global_device_ids=true, to_apply=%add | all-reduce | flops 1536 | bytes 6144
  77.5 30.3 %copy.117 = f32[512,1024,12]{1,0,2:T(8,128)} copy(f32[512,1024,12]{0,2,1:T(8,128)} %fusion.1) | data formatting | bytes 50331648 | tf_op jit(solution)/shard_map/qkb,bh->hqk/dot_general | solution.py:79
  125.8 31.1 %copy.115 = f32[512,1024,12]{1,0,2:T(8,128)} copy(f32[512,1024,12]{0,2,1:T(8,128)} %fusion.3) | data formatting | bytes 50331648 | tf_op jit(solution)/shard_map/qkb,bh->hqk/dot_general | solution.py:79
  158.6 40.1 %all-gather = bf16[32,24,4]{1,2,0:T(4,128)(2,1)S(1)} all-gather(bf16[1,24,4]{1,2,0:T(4,128)(2,1)S(1)} %bitcast.154), channel_id=1, replica_groups=mesh['fsdp'=32] {'fsdp'}, dimensions={0}, use_global_device_ids=true | all-gather | bytes 6336 | tf_op jit(solution)/shard_map/all_gather | solution.py:49
  248.1 16.9 %fusion.106 = (f32[12,512]{1,0:T(8,128)S(1)}, f32[12,512,1024]{2,1,0:T(8,128)}) fusion(f32[512,1024,12]{1,0,2:T(8,128)} %copy.115, bf16[512,12,64]{0,2,1:T(8,128)(2,1)} %bitcast.127, bf16[1024,12,64]{0,2,1:T(8,128)(2,1)S(1)} %bitcast.118, pred[512,1024]{1,0:T(8,128)(4,1)} %get-tuple-element.74), kind=kOutput, calls=%fused_computation.174 | convolution fusion | flops 830466048 | bytes 53239808 | tf_op jit(solution)/shard_map/qhd,khd->hqk/dot_general | solution.py:70
  314.0 21.9 %fusion.108 = f32[4,512,3072]{2,1,0:T(8,128)} fusion(bf16[4,512,768]{2,1,0:T(8,128)(2,1)} %bitcast.135, bf16[3072,4,768]{2,0,1:T(8,128)(2,1)} %all-gather.10.cloned.1.call-done), kind=kOutput, calls=%fused_computation.176 | convolution fusion | flops 9663676416 | bytes 47185920 | tf_op jit(solution)/shard_map/ecd,fed->ecf/dot_general | solution.py:115
  335.9 46.2 %all-gather.12.cloned.1.call-done = bf16[3072,4,768]{2,0,1:T(8,128)(2,1)} async-done(((bf16[96,4,768]{2,0,1:T(8,128)(2,1)}), bf16[3072,4,768]{2,0,1:T(8,128)(2,1)}) %all-gather.12.cloned.1.call-update) | async-done | bytes 18874384 | tf_op jit(solution)/shard_map/all_gather | solution.py:114
  382.1 21.1 %fusion.98 = f32[4,512,768]{2,1,0:T(8,128)} fusion(bf16[3072,4,768]{2,0,1:T(8,128)(2,1)} %all-gather.12.cloned.1.call-done, f32[4,512,3072]{2,1,0:T(8,128)} %fusion.108), kind=kOutput, calls=%fused_computation.167 | convolution fusion | flops 9720299520 | bytes 50331648 | tf_op jit(solution)/shard_map/ecf,fed->ecd/dot_general | solution.py:117
  430.7 24.9 %convolution_bitcast_fusion = f32[3072,4,768]{0,2,1:T(8,128)} fusion(bf16[4,512,768]{2,1,0:T(8,128)(2,1)S(1)} %bitcast.137, f32[4,512,3072]{2,1,0:T(8,128)} %fusion.108), kind=kOutput, calls=%fused_computation.43 | convolution fusion | flops 9720299520 | bytes 66060288 | tf_op jit(solution)/shard_map/ecf,ecd->fed/dot_general | solution.py:158
  455.6 29.3 %fusion.14 = bf16[4,512,3072]{2,1,0:T(8,128)(2,1)} fusion(f32[4,512,3072]{2,1,0:T(8,128)} %fusion.108, bf16[4,512,768]{2,1,0:T(8,128)(2,1)} %bitcast.138, bf16[3072,4,768]{2,0,1:T(8,128)(2,1)} %all-gather.12.cloned.1.call-done), kind=kOutput, calls=%fused_computation.23 | convolution fusion | flops 9789505536 | bytes 59768832 | tf_op jit(solution)/shard_map/ecd,fed->ecf/dot_general | solution.py:145
  484.9 20.8 %convolution_bitcast_fusion.1 = f32[3072,4,768]{0,2,1:T(8,128)} fusion(bf16[4,512,768]{2,1,0:T(8,128)(2,1)S(1)} %bitcast.136, bf16[4,512,3072]{2,1,0:T(8,128)(2,1)} %fusion.14), kind=kOutput, calls=%fused_computation.44 | convolution fusion | flops 9663676416 | bytes 53477376 | tf_op jit(solution)/shard_map/ecf,ecd->fed/dot_general | solution.py:155
  505.7 49.1 %pad_maximum_fusion = f32[3072,8,768]{0,2,1:T(8,128)} fusion(f32[3072,4,768]{0,2,1:T(8,128)} %convolution_bitcast_fusion, f32[3072,4,768]{0,2,1:T(8,128)} %convolution_bitcast_fusion.1), kind=kLoop, calls=%fused_computation.4 | loop fusion | flops 18874368 | bytes 150994944 | tf_op jit(solution)/shard_map/concatenate | solution.py:153
  554.8 74.9 %copy.134 = f32[3072,8,768]{2,1,0:T(8,128)} copy(f32[3072,8,768]{0,2,1:T(8,128)} %pad_maximum_fusion) | data formatting | bytes 150994944 | tf_op jit(solution)/shard_map/concatenate | solution.py:153
  630.6 22.9 %fusion.109 = f32[4,512,768]{2,1,0:T(8,128)} fusion(bf16[4,512,3072]{2,1,0:T(8,128)(2,1)} %fusion.14, bf16[3072,4,768]{2,0,1:T(8,128)(2,1)} %all-gather.10.cloned.1.call-done), kind=kOutput, calls=%fused_computation.177 | convolution fusion | flops 9663676416 | bytes 37748736 | tf_op jit(solution)/shard_map/ecf,fed->ecd/dot_general | solution.py:149
  680.8 24.3 %multiply_reduce_fusion.1 = (f32[12,512]{1,0:T(8,128)S(1)}, f32[12,512,1024]{2,1,0:T(8,128)}) fusion(f32[12,512,1024]{2,1,0:T(8,128)} %get-tuple-element.81, f32[12,512]{1,0:T(8,128)S(1)} %log_add_fusion.1, bf16[512,12,64]{0,2,1:T(8,128)(2,1)S(1)} %bitcast.129, bf16[1024,12,64]{0,2,1:T(8,128)(2,1)S(1)} %bitcast.124), kind=kOutput, calls=%fused_computation.32 | convolution fusion | flops 824174592 | bytes 52740096 | tf_op jit(solution)/shard_map/qhd,khd->hqk/dot_general | solution.py:198
  705.1 24.7 %multiply_convert_fusion.1 = bf16[12,512,1024]{2,1,0:T(8,128)(2,1)S(1)} fusion(f32[12,512,1024]{2,1,0:T(8,128)} %get-tuple-element.88, f32[12,512,1024]{2,1,0:T(8,128)} %get-tuple-element.81, f32[12,512]{1,0:T(8,128)S(1)} %get-tuple-element.87, f32[12,512]{1,0:T(8,128)S(1)} %log_add_fusion.1), kind=kLoop, calls=%fused_computation.31 | loop fusion | flops 25165824 | bytes 62963712 | tf_op jit(solution)/shard_map/convert_element_type | solution.py:203
  744.1 17.7 %multiply_reduce_fusion = (f32[12,512]{1,0:T(8,128)S(1)}, f32[12,512,1024]{2,1,0:T(8,128)}) fusion(f32[12,512,1024]{2,1,0:T(8,128)} %get-tuple-element.79, f32[12,512]{1,0:T(8,128)S(1)} %log_add_fusion, bf16[512,12,64]{0,2,1:T(8,128)(2,1)} %bitcast.131, bf16[1024,12,64]{0,2,1:T(8,128)(2,1)} %bitcast.123), kind=kOutput, calls=%fused_computation.29 | convolution fusion | flops 824174592 | bytes 52740096 | tf_op jit(solution)/shard_map/qhd,khd->hqk/dot_general | solution.py:198
  761.9 17.6 %multiply_convert_fusion = bf16[12,512,1024]{2,1,0:T(8,128)(2,1)S(1)} fusion(f32[12,512,1024]{2,1,0:T(8,128)} %get-tuple-element.90, f32[12,512,1024]{2,1,0:T(8,128)} %get-tuple-element.79, f32[12,512]{1,0:T(8,128)S(1)} %get-tuple-element.89, f32[12,512]{1,0:T(8,128)S(1)} %log_add_fusion), kind=kLoop, calls=%fused_computation.28 | loop fusion | flops 25165824 | bytes 62963712 | tf_op jit(solution)/shard_map/convert_element_type | solution.py:203
  832.6 23.3 %copy.130 = bf16[12,512,1024]{1,0,2:T(8,128)(2,1)} copy(bf16[12,512,1024]{2,1,0:T(8,128)(2,1)} %copy-done.3) | data formatting | bytes 25165824 | tf_op jit(solution)/shard_map/convert_element_type | solution.py:203
  855.9 23.3 %copy.131 = bf16[12,512,1024]{1,0,2:T(8,128)(2,1)} copy(bf16[12,512,1024]{2,1,0:T(8,128)(2,1)} %copy-done.2) | data formatting | bytes 25165824 | tf_op jit(solution)/shard_map/convert_element_type | solution.py:203
  918.4 40.1 %all-reduce.5 = (f32[768]{0:T(1024)S(1)}, f32[32,12]{0,1:T(8,128)}, f32[768]{0:T(1024)S(1)}, f32[768,4]{0,1:T(4,128)S(1)}) all-reduce(f32[768]{0:T(1024)S(1)} %get-tuple-element.52, f32[32,12]{0,1:T(8,128)S(1)} %fusion.75, f32[768]{0:T(1024)S(1)} %copy-done.69, f32[768,4]{0,1:T(4,128)S(1)} %fusion.111), channel_id=2, replica_groups=mesh['fsdp'=32] {'fsdp'}, use_global_device_ids=true, to_apply=%region_22.23.clone | all-reduce | flops 4992 | bytes 39936
  960.3 324.7 %reduce-scatter.9.cloned.1.call-done = f32[96,8,768]{2,1,0:T(8,128)} async-done(((f32[3072,8,768]{2,1,0:T(8,128)}), f32[96,8,768]{2,1,0:T(8,128)}) %reduce-scatter.9.cloned.1.call-update) | async-done | bytes 2359312 | tf_op jit(solution)/shard_map/reduce_scatter | solution.py:152
  1289.2 100.6 %reduce-scatter.7.cloned.1.call-done = f32[24,768]{1,0:T(8,128)} async-done(((f32[768,768]{1,0:T(8,128)}), f32[24,768]{1,0:T(8,128)}) %reduce-scatter.7.cloned.1.call-update) | async-done | bytes 73744 | tf_op jit(solution)/shard_map/reduce_scatter | solution.py:244
  1389.8 124.5 %reduce-scatter.5.cloned.1.call-done = f32[24,2304]{1,0:T(8,128)} async-done(((f32[768,2304]{1,0:T(8,128)}), f32[24,2304]{1,0:T(8,128)}) %reduce-scatter.5.cloned.1.call-update) | async-done | bytes 221200 | tf_op jit(solution)/shard_map/reduce_scatter | solution.py:243
  (260 shorter events, 313.5 us)
Async XLA Ops:
  7.2 54.3 %copy-start = (bf16[32,12]{0,1:T(8,128)(2,1)S(1)}, bf16[32,12]{0,1:T(8,128)(2,1)}, u32[]{:S(2)}) copy-start(bf16[32,12]{0,1:T(8,128)(2,1)} %param.19) | copy-start | bytes 2308
  7.2 194.6 %all-gather.6.cloned.1.call-start = ((), (), s32[]{:S(2)}) async-start(), calls=%async_computation.3 | async-start | bytes 3649536 | tf_op jit(solution)/shard_map/all_gather | solution.py:46
  7.9 290.3 %all-gather.8.cloned.1.call-start = ((), (), s32[]{:S(2)}) async-start(), calls=%async_computation.4 | async-start | bytes 1216512 | tf_op jit(solution)/shard_map/all_gather | solution.py:47
  8.7 305.3 %all-gather.10.cloned.1.call-start = ((), (), s32[]{:S(2)}) async-start(), calls=%async_computation.5 | async-start | bytes 19464192 | tf_op jit(solution)/shard_map/all_gather | solution.py:113
  10.8 371.3 %all-gather.12.cloned.1.call-start = ((), (), s32[]{:S(2)}) async-start(), calls=%async_computation.6 | async-start | bytes 19464192 | tf_op jit(solution)/shard_map/all_gather | solution.py:114
  12.9 1272.2 %reduce-scatter.9.cloned.1.call-start = ((), (), s32[]{:S(2)}) async-start(), calls=%async_computation.9 | async-start | bytes 77856768 | tf_op jit(solution)/shard_map/reduce_scatter | solution.py:152
  15.3 186.4 %copy-start.14 = (bf16[1024,768]{0,1:T(8,128)(2,1)}, bf16[1024,768]{0,1:T(8,128)(2,1)S(1)}, u32[]{:S(2)}) copy-start(bf16[1024,768]{0,1:T(8,128)(2,1)S(1)} %copy.111) | copy-start | bytes 4718596
  58.0 143.8 %copy-start.65 = (f32[768]{0:T(1024)}, f32[768]{0:T(1024)S(1)}, u32[]{:S(2)}) copy-start(f32[768]{0:T(1024)S(1)} %convert_element_type.233) | copy-start | bytes 9220
  125.8 31.1 %copy-start.76 = (s32[1,4]{1,0:T(1,128)S(1)}, s32[1,4]{1,0:T(1,128)}, u32[]{:S(2)}) copy-start(s32[1,4]{1,0:T(1,128)} %param.14) | copy-start | bytes 52
  125.8 31.3 %copy-start.47 = (s32[1024,1]{0,1:T(1,128)S(1)}, s32[1024,1]{0,1:T(1,128)}, u32[]{:S(2)}) copy-start(s32[1024,1]{0,1:T(1,128)} %param.15) | copy-start | bytes 12292
  125.8 32.9 %copy-start.72 = (bf16[24,4]{0,1:T(4,128)(2,1)S(1)}, bf16[24,4]{0,1:T(4,128)(2,1)}, u32[]{:S(2)}) copy-start(bf16[24,4]{0,1:T(4,128)(2,1)} %param.21) | copy-start | bytes 580
  156.9 146.1 %copy-start.51 = (f32[768]{0:T(1024)}, f32[768]{0:T(1024)S(1)}, u32[]{:S(2)}) copy-start(f32[768]{0:T(1024)S(1)} %convert_element_type.254) | copy-start | bytes 9220
  198.9 114.1 %copy-start.58 = (bf16[768,4]{0,1:T(4,128)(2,1)}, bf16[768,4]{0,1:T(4,128)(2,1)S(1)}, u32[]{:S(2)}) copy-start(bf16[768,4]{0,1:T(4,128)(2,1)S(1)} %reshape.362) | copy-start | bytes 18436
  211.6 75.4 %copy-start.12 = (bf16[1024,768]{0,1:T(8,128)(2,1)}, bf16[1024,768]{0,1:T(8,128)(2,1)S(1)}, u32[]{:S(2)}) copy-start(bf16[1024,768]{0,1:T(8,128)(2,1)S(1)} %copy.112) | copy-start | bytes 4718596
  217.4 30.7 %copy-start.4 = (bf16[1024,768]{0,1:T(8,128)(2,1)}, bf16[1024,768]{0,1:T(8,128)(2,1)S(1)}, u32[]{:S(2)}) copy-start(bf16[1024,768]{0,1:T(8,128)(2,1)S(1)} %copy.114) | copy-start | bytes 4718596
  237.0 39.3 %copy-start.39 = (f32[12,512]{1,0:T(8,128)}, f32[12,512]{1,0:T(8,128)S(1)}, u32[]{:S(2)}) copy-start(f32[12,512]{1,0:T(8,128)S(1)} %get-tuple-element.78) | copy-start | bytes 73732
  248.1 28.2 %copy-start.43 = (f32[12,512]{1,0:T(8,128)}, f32[12,512]{1,0:T(8,128)S(1)}, u32[]{:S(2)}) copy-start(f32[12,512]{1,0:T(8,128)S(1)} %fusion.18) | copy-start | bytes 73732
  314.0 100.2 %copy-start.55 = (f32[1024]{0:T(1024)}, f32[1024]{0:T(1024)S(1)}, u32[]{:S(2)}) copy-start(f32[1024]{0:T(1024)S(1)} %get-tuple-element.60) | copy-start | bytes 12292
  335.9 67.3 %copy-start.63 = (s32[1024]{0:T(1024)S(1)}, s32[1024]{0:T(1024)}, u32[]{:S(2)}) copy-start(s32[1024]{0:T(1024)} %broadcast_clamp_fusion) | copy-start | bytes 12292
  455.6 29.3 %copy-start.31 = (bf16[2048,768]{1,0:T(8,128)(2,1)S(1)}, bf16[2048,768]{1,0:T(8,128)(2,1)}, u32[]{:S(2)}) copy-start(bf16[2048,768]{1,0:T(8,128)(2,1)} %scatter_custom_fusion) | copy-start | bytes 9437188
  629.8 760.0 %reduce-scatter.7.cloned.1.call-start = ((), (), s32[]{:S(2)}) async-start(), calls=%async_computation.8 | async-start | bytes 2433024 | tf_op jit(solution)/shard_map/reduce_scatter | solution.py:244
  705.1 24.7 %copy-start.25 = (bf16[512,768]{0,1:T(8,128)(2,1)S(1)}, bf16[512,768]{0,1:T(8,128)(2,1)}, u32[]{:S(2)}) copy-start(bf16[512,768]{0,1:T(8,128)(2,1)} %copy.113) | copy-start | bytes 2359300
  799.6 714.7 %reduce-scatter.5.cloned.1.call-start = ((), (), s32[]{:S(2)}) async-start(), calls=%async_computation.7 | async-start | bytes 7299072 | tf_op jit(solution)/shard_map/reduce_scatter | solution.py:243
  904.7 609.6 %copy-start.1 = (bf16[32,12]{0,1:T(8,128)(2,1)S(1)}, bf16[32,12]{0,1:T(8,128)(2,1)}, u32[]{:S(2)}) copy-start(bf16[32,12]{0,1:T(8,128)(2,1)} %param.19) | copy-start | bytes 2308
  (60 other events, 371.2 us)
Sparse Core Ops, SparseCore 0:
  10.9 62.8 all-gather.5
  76.7 52.8 all-gather.7
  132.5 123.8 all-gather.9
  259.2 122.8 all-gather.11
  629.9 655.1 reduce-scatter.8
  1291.6 98.1 reduce-scatter.6
  1396.0 118.2 reduce-scatter.4
where the time goes:
time: 1540 us; the launch traced here: 1520 us
  waiting for transfers between devices  597 us (39%)
  matrix products  384 us (25%)
  local copies, waits for them, and re-layouts  270 us (18%)
  other arithmetic  132 us (9%)
  blocking collectives  122 us (8%)
    reduce_scatter x1, waiting for transfers between devices, body(): lax.psum_scatter(jnp.concatenate([jnp.einsum('ecf,ecd->fed', grad_pre_sto...  325 us
    reduce_scatter x1, waiting for transfers between devices, body(): lax.psum_scatter(grad_w_qkv, 'fsdp', scatter_dimension=0, tiled=True)  124 us
    reduce_scatter x1, waiting for transfers between devices, body(): lax.psum_scatter(grad_w_out, 'fsdp', scatter_dimension=0, tiled=True)  101 us
    unnamed x2, blocking collectives  82.3 us
    concatenate x1, local copies, waits for them, and re-layouts, body(): jnp.concatenate([jnp.einsum('ecf,ecd->fed', grad_pre_store, dispatched, p...  74.9 us
    dot_general x2, local copies, waits for them, and re-layouts, block_scores(): jnp.einsum('qkb,bh->hqk', onehot, table, preferred_element_type=jnp.float32)  61.4 us
    concatenate x1, other arithmetic, body(): jnp.concatenate([jnp.einsum('ecf,ecd->fed', grad_pre_store, dispatched, p...  49.1 us
    convert_element_type x2, local copies, waits for them, and re-layouts, body(): grad_scores = (probs * (grad_probs - jnp.sum(probs * grad_probs, axis=-1,...  46.6 us
  transfers between devices with their start and end apart: 7, of which 4 were waited for; matrix products, arithmetic and copies ran while one was open for 34% of the time, Pallas kernels for 0%

commit v1 on v0

v1 whole, which is shorter than its diff:
```python
import functools

import jax
import jax.numpy as jnp
from jax import lax
from jax.experimental import pallas as pl
from jax.experimental.pallas import tpu as pltpu
from jax.sharding import PartitionSpec as P

D = 768
HEADS = 12
HEAD_DIM = 64
PAIRS = HEADS // 2
BUCKETS = 32
EXPERTS = 4
TOK_DEV = 1024
CAP = 512
ROWS = EXPERTS * CAP
AXIS = "fsdp"
F32 = jnp.float32
BF16 = jnp.bfloat16

norm_eps = 1e-06
masked_fill = -1e30
far_steps = (12, 16, 23, 32, 46, 64, 91)

TILE = 128
KEY_TILES = TOK_DEV // TILE
QUERY_BLOCK = 256
QUERY_BLOCKS = TOK_DEV // QUERY_BLOCK
HALVES = QUERY_BLOCK // TILE
NT = (((1,), (1,)), ((), ()))
NN = (((1,), (0,)), ((), ()))
TN = (((0,), (0,)), ((), ()))


def bucket_of(offset):
    distance = jnp.abs(offset)
    far_bucket = 8 + sum(((distance >= step).astype(jnp.int32) for step in far_steps))
    return jnp.where(distance < 8, distance, far_bucket) + 16 * (offset > 0).astype(jnp.int32)


def rms_norm(values, gain):
    return values * lax.rsqrt(jnp.mean(values * values, axis=-1, keepdims=True) + norm_eps) * gain


def along_z(value, size, shift):
    depth = size // 8
    return lax.ppermute(
        value, AXIS, [(i, (i // 8 + shift) % depth * 8 + i % 8) for i in range(size)]
    )


def along_quad(value, size, flip):
    return lax.ppermute(value, AXIS, [(i, i ^ (flip << 1)) for i in range(size)])


def along_core(value, size):
    return lax.ppermute(value, AXIS, [(i, i ^ 1) for i in range(size)])


def scatter_sums(partial, size):
    me = lax.axis_index(AXIS)
    depth = size // 8
    z, quad, core = me // 8, me // 2 % 4, me % 2
    rows = partial.shape[0] // size
    view = partial.reshape(depth, 4, 2, rows, partial.shape[1])
    mine = lax.dynamic_index_in_dim(view, core, 2, False)
    other = lax.dynamic_index_in_dim(view, 1 - core, 2, False).astype(BF16)
    total = mine + along_core(other, size).astype(F32)
    low = total.astype(BF16)
    arrived = [
        along_quad(lax.dynamic_index_in_dim(low, quad ^ flip, 1, False), size, flip)
        for flip in range(1, 4)
    ]
    total = lax.dynamic_index_in_dim(total, quad, 1, False)
    for piece in arrived:
        total = total + piece.astype(F32)
    low = total.astype(BF16)
    arrived = [
        along_z(lax.dynamic_index_in_dim(low, (z + shift) % depth, 0, False), size, shift)
        for shift in range(1, depth)
    ]
    total = lax.dynamic_index_in_dim(total, z, 0, False)
    for piece in arrived:
        total = total + piece.astype(F32)
    return total


def sum_everywhere(value, size):
    step = 1
    while step < size:
        value = value + lax.ppermute(value, AXIS, [(i, i ^ step) for i in range(size)])
        step *= 2
    return value


def score_tile(tile, block, keys, queries, near_ref, head):
    scores = lax.dot_general(
        keys[tile * TILE : (tile + 1) * TILE], queries, NT, preferred_element_type=F32
    )
    parts = []
    for half in range(HALVES):
        part = scores[:, half * TILE : (half + 1) * TILE]
        apart = tile - (block * HALVES + half)
        if abs(apart) <= 1:
            part = part + near_ref[head, apart + 1]
        parts.append(part)
    return parts


def fold(value, combine):
    return combine(value.reshape(value.shape[0] // 8, 8, value.shape[1]), axis=0)


def attend_kernel(
    q_ref, k_ref, v_ref, extra_q_ref, extra_k_ref, near_ref, out_ref, log_ref,
    score_ref, prob_ref, turned_ref,
):
    lane = lax.broadcasted_iota(jnp.int32, (TOK_DEV, 2 * HEAD_DIM), 1)
    queries = (q_ref[...].astype(F32) * 0.125).astype(BF16)
    keys = k_ref[...]
    values_t = v_ref[...].astype(F32).T.astype(BF16)
    for head in range(2):
        own = (lane < HEAD_DIM) if head == 0 else (lane >= HEAD_DIM)
        head_keys = jnp.where(own, keys, extra_k_ref[head])
        head_queries = jnp.where(own, queries, extra_q_ref[head])
        head_values = values_t[head * HEAD_DIM : (head + 1) * HEAD_DIM]
        for block in range(QUERY_BLOCKS):
            side = block % 2
            at = slice(block * QUERY_BLOCK, (block + 1) * QUERY_BLOCK)
            top = None
            for tile in range(KEY_TILES):
                parts = score_tile(tile, block, head_keys, head_queries[at], near_ref, head)
                highs = []
                for half, part in enumerate(parts):
                    score_ref[
                        side, tile * TILE : (tile + 1) * TILE, half * TILE : (half + 1) * TILE
                    ] = part
                    highs.append(fold(part, jnp.max))
                high = jnp.concatenate(highs, axis=1)
                top = high if top is None else jnp.maximum(top, high)
            top = jnp.max(top, axis=0, keepdims=True)
            total = jnp.zeros((8, QUERY_BLOCK), F32)
            for tile in range(KEY_TILES):
                rows = slice(tile * TILE, (tile + 1) * TILE)
                expo = jnp.exp(score_ref[side, rows, :] - top)
                total = total + fold(expo, jnp.sum)
                prob_ref[side, rows, :] = expo.astype(BF16)
            total = jnp.sum(total, axis=0, keepdims=True)
            mixed = lax.dot_general(head_values, prob_ref[side], NN, preferred_element_type=F32)
            turned_ref[head * HEAD_DIM : (head + 1) * HEAD_DIM, at] = mixed * (1.0 / total)
            log_ref[0, head : head + 1, at] = top + jnp.log(total)
    out_ref[...] = turned_ref[...].T.astype(BF16)


def attend_back_kernel(
    q_ref, k_ref, v_ref, grad_ref, log_ref, extra_q_ref, extra_k_ref, near_ref, bucket_ref,
    grad_q_ref, grad_k_ref, grad_v_ref, grad_table_ref,
    prob_ref, slope_ref, low_prob_ref, low_grad_ref, turned_ref, key_sum_ref, value_sum_ref,
    near_sum_ref,
):
    lane = lax.broadcasted_iota(jnp.int32, (TOK_DEV, 2 * HEAD_DIM), 1)
    queries = (q_ref[...].astype(F32) * 0.125).astype(BF16)
    keys = k_ref[...]
    keys_t = (keys.astype(F32) * 0.125).T.astype(BF16)
    values = v_ref[...]
    grads = grad_ref[...]
    zero = jnp.zeros_like(grads)
    for head in range(2):
        own = (lane < HEAD_DIM) if head == 0 else (lane >= HEAD_DIM)
        head_keys = jnp.where(own, keys, extra_k_ref[head])
        head_queries = jnp.where(own, queries, extra_q_ref[head])
        bare_queries = jnp.where(own, queries, zero)
        head_grads = jnp.where(own, grads, zero)
        head_keys_t = keys_t[head * HEAD_DIM : (head + 1) * HEAD_DIM]
        near_sum_ref[...] = jnp.zeros_like(near_sum_ref)
        far_sums = [jnp.zeros((8, TILE), F32), jnp.zeros((8, TILE), F32)]
        for block in range(QUERY_BLOCKS):
            side = block % 2
            at = slice(block * QUERY_BLOCK, (block + 1) * QUERY_BLOCK)
            logs = log_ref[0, head : head + 1, at]
            delta = jnp.zeros((8, QUERY_BLOCK), F32)
            for tile in range(KEY_TILES):
                rows = slice(tile * TILE, (tile + 1) * TILE)
                parts = score_tile(tile, block, head_keys, head_queries[at], near_ref, head)
                probs = jnp.exp(jnp.concatenate(parts, axis=1) - logs)
                slopes = lax.dot_general(
                    values[rows], head_grads[at], NT, preferred_element_type=F32
                )
                delta = delta + fold(probs * slopes, jnp.sum)
                prob_ref[side, rows, :] = probs
                low_prob_ref[side, rows, :] = probs.astype(BF16)
                slope_ref[side, rows, :] = slopes
            delta = jnp.sum(delta, axis=0, keepdims=True)
            for tile in range(KEY_TILES):
                rows = slice(tile * TILE, (tile + 1) * TILE)
                grad_scores = prob_ref[side, rows, :] * (slope_ref[side, rows, :] - delta)
                low_grad_ref[side, rows, :] = grad_scores.astype(BF16)
                for half in range(HALVES):
                    part = grad_scores[:, half * TILE : (half + 1) * TILE]
                    apart = tile - (block * HALVES + half)
                    if abs(apart) <= 1:
                        near_sum_ref[apart + 1] += part
                    else:
                        which = 0 if apart < 0 else 1
                        far_sums[which] = far_sums[which] + fold(part, jnp.sum)
            value_part = lax.dot_general(
                low_prob_ref[side], head_grads[at], NN, preferred_element_type=F32
            )
            key_part = lax.dot_general(
                low_grad_ref[side], bare_queries[at], NN, preferred_element_type=F32
            )
            if head == 0 and block == 0:
                value_sum_ref[...] = value_part
                key_sum_ref[...] = key_part
            else:
                value_sum_ref[...] += value_part
                key_sum_ref[...] += key_part
            turned_ref[head * HEAD_DIM : (head + 1) * HEAD_DIM, at] = lax.dot_general(
                head_keys_t, low_grad_ref[side], NN, preferred_element_type=F32
            )
        for bucket in range(BUCKETS):
            row = jnp.zeros((8, TILE), F32)
            for apart in (-1, 0, 1):
                if (apart < 0 and bucket >= 16) or (apart > 0 and bucket < 16):
                    continue
                picked = jnp.where(
                    bucket_ref[apart + 1] == bucket, near_sum_ref[apart + 1], 0.0
                )
                row = row + fold(picked, jnp.sum)
            if bucket == 15:
                row = row + far_sums[0]
            if bucket == 31:
                row = row + far_sums[1]
            grad_table_ref[0, head, bucket : bucket + 1, :] = jnp.sum(row, axis=0, keepdims=True)
    grad_q_ref[...] = turned_ref[...].T.astype(BF16)
    grad_k_ref[...] = key_sum_ref[...].astype(BF16)
    grad_v_ref[...] = value_sum_ref[...].astype(BF16)


def column(first):
    return pl.BlockSpec((TOK_DEV, 2 * HEAD_DIM), lambda pair: (0, first + pair))


def score_specs():
    return [
        pl.BlockSpec((2, TOK_DEV, 2 * HEAD_DIM), lambda pair: (0, 0, 0)),
        pl.BlockSpec((2, TOK_DEV, 2 * HEAD_DIM), lambda pair: (pair, 0, 0)),
        pl.BlockSpec((2, 3, TILE, TILE), lambda pair: (pair, 0, 0, 0)),
    ]


def attend(qkv, extra_q, extra_k, near):
    logs = pl.BlockSpec((1, 2, TOK_DEV), lambda pair: (pair, 0, 0))
    return pl.pallas_call(
        attend_kernel,
        grid=(PAIRS,),
        in_specs=[column(0), column(PAIRS), column(2 * PAIRS)] + score_specs(),
        out_specs=[column(0), logs],
        out_shape=[
            jax.ShapeDtypeStruct((TOK_DEV, D), BF16),
            jax.ShapeDtypeStruct((PAIRS, 2, TOK_DEV), F32),
        ],
        scratch_shapes=[
            pltpu.VMEM((2, TOK_DEV, QUERY_BLOCK), F32),
            pltpu.VMEM((2, TOK_DEV, QUERY_BLOCK), BF16),
            pltpu.VMEM((2 * HEAD_DIM, TOK_DEV), F32),
        ],
        compiler_params=pltpu.CompilerParams(vmem_limit_bytes=40 << 20),
        cost_estimate=pl.CostEstimate(
            flops=40_000_000_000, bytes_accessed=12 << 20, transcendentals=HEADS << 20
        ),
    )(qkv, qkv, qkv, extra_q, extra_k, near)


def attend_back(qkv, grad_mixed, logs, extra_q, extra_k, near, buckets):
    log_spec = pl.BlockSpec((1, 2, TOK_DEV), lambda pair: (pair, 0, 0))
    return pl.pallas_call(
        attend_back_kernel,
        grid=(PAIRS,),
        in_specs=[column(0), column(PAIRS), column(2 * PAIRS), column(0), log_spec]
        + score_specs()
        + [pl.BlockSpec((3, TILE, TILE), lambda pair: (0, 0, 0))],
        out_specs=[
            column(0),
            column(0),
            column(0),
            pl.BlockSpec((1, 2, BUCKETS, TILE), lambda pair: (pair, 0, 0, 0)),
        ],
        out_shape=[
            jax.ShapeDtypeStruct((TOK_DEV, D), BF16),
            jax.ShapeDtypeStruct((TOK_DEV, D), BF16),
            jax.ShapeDtypeStruct((TOK_DEV, D), BF16),
            jax.ShapeDtypeStruct((PAIRS, 2, BUCKETS, TILE), F32),
        ],
        scratch_shapes=[
            pltpu.VMEM((2, TOK_DEV, QUERY_BLOCK), F32),
            pltpu.VMEM((2, TOK_DEV, QUERY_BLOCK), F32),
            pltpu.VMEM((2, TOK_DEV, QUERY_BLOCK), BF16),
            pltpu.VMEM((2, TOK_DEV, QUERY_BLOCK), BF16),
            pltpu.VMEM((2 * HEAD_DIM, TOK_DEV), F32),
            pltpu.VMEM((TOK_DEV, 2 * HEAD_DIM), F32),
            pltpu.VMEM((TOK_DEV, 2 * HEAD_DIM), F32),
            pltpu.VMEM((3, TILE, TILE), F32),
        ],
        compiler_params=pltpu.CompilerParams(vmem_limit_bytes=48 << 20),
        cost_estimate=pl.CostEstimate(
            flops=80_000_000_000, bytes_accessed=20 << 20, transcendentals=HEADS << 20
        ),
    )(qkv, qkv, qkv, grad_mixed, logs, extra_q, extra_k, near, buckets)


def score_extras(table, doc_ids):
    lane = lax.iota(jnp.int32, HEAD_DIM)
    places = lax.iota(jnp.int32, TOK_DEV)
    tiles = places // TILE
    is_doc = lane < 4
    block_lane = (lane >= 4) & (lane < 4 + KEY_TILES)
    same = doc_ids[:, None] == lane[None, :]
    in_block = tiles[:, None] == (lane - 4)[None, :]
    extra_q = jnp.where((is_doc & same) | (block_lane & in_block), 1.0, 0.0).astype(BF16)
    apart = tiles[:, None] - (lane - 4)[None, :]
    mask_k = jnp.where(is_doc & ~same, masked_fill, 0.0)
    far = jnp.where(
        apart[None] < 0, table[15].astype(F32)[:, None, None], table[31].astype(F32)[:, None, None]
    )
    use_far = (block_lane & (jnp.abs(apart) > 1))[None]
    extra_k = jnp.where(use_far, far, mask_k[None]).astype(BF16)
    blank = jnp.zeros_like(extra_q)
    queries = jnp.stack(
        [jnp.concatenate([blank, extra_q], axis=1), jnp.concatenate([extra_q, blank], axis=1)]
    )
    pairs = extra_k.reshape(PAIRS, 2, TOK_DEV, HEAD_DIM)
    even = jnp.concatenate([jnp.zeros_like(pairs[:, 0]), pairs[:, 0]], axis=-1)
    odd = jnp.concatenate([pairs[:, 1], jnp.zeros_like(pairs[:, 1])], axis=-1)
    keys = jnp.stack([even, odd], axis=1).reshape(HEADS, TOK_DEV, 2 * HEAD_DIM)
    return queries, keys


def gelu_with_slope(x):
    scale, cubic = 0.7978845608028654, 0.044715
    square = x * x
    curve = jnp.tanh(scale * x * (1.0 + cubic * square))
    half = 0.5 * (1.0 + curve)
    slope = half + 0.5 * x * (1.0 - curve * curve) * (scale * (1.0 + 3.0 * cubic * square))
    return x * half, slope


def expert_kernel(rows_ref, up_ref, down_ref, out_ref, hidden_ref, slope_ref, sum_ref):
    step = pl.program_id(0)
    up = up_ref[...].reshape(-1, D)
    down = down_ref[...].reshape(-1, D)
    for chunk in range(EXPERTS):
        at = slice(chunk * CAP, (chunk + 1) * CAP)
        pre = lax.dot_general(rows_ref[at], up, NT, preferred_element_type=F32)
        hidden, slope = gelu_with_slope(pre)
        low = hidden.astype(BF16)
        hidden_ref[at] = low
        slope_ref[at] = slope.astype(BF16)
        part = lax.dot_general(low, down, NN, preferred_element_type=F32)

        @pl.when(step == 0)
        def _():
            sum_ref[at] = part

        @pl.when(step > 0)
        def _():
            sum_ref[at] += part

    @pl.when(step == pl.num_programs(0) - 1)
    def _():
        out_ref[...] = sum_ref[...].astype(BF16)


def expert_back_kernel(grad_ref, slope_ref, up_ref, down_ref, out_ref, grad_pre_ref, sum_ref):
    step = pl.program_id(0)
    up = up_ref[...].reshape(-1, D)
    down = down_ref[...].reshape(-1, D)
    for chunk in range(EXPERTS):
        at = slice(chunk * CAP, (chunk + 1) * CAP)
        grad_hidden = lax.dot_general(grad_ref[at], down, NT, preferred_element_type=F32)
        grad_pre = (grad_hidden * slope_ref[at].astype(F32)).astype(BF16)
        grad_pre_ref[at] = grad_pre
        part = lax.dot_general(grad_pre, up, NN, preferred_element_type=F32)

        @pl.when(step == 0)
        def _():
            sum_ref[at] = part

        @pl.when(step > 0)
        def _():
            sum_ref[at] += part

    @pl.when(step == pl.num_programs(0) - 1)
    def _():
        out_ref[...] = sum_ref[...].astype(BF16)


def expert_weight_kernel(rows_ref, grad_ref, hidden_ref, grad_pre_ref, out_ref):
    pieces, _, units, _ = out_ref.shape
    grad_up = lax.dot_general(grad_pre_ref[...], rows_ref[...], TN, preferred_element_type=F32)
    out_ref[:, 0] = grad_up.astype(BF16).reshape(pieces, units, D)
    grad_down = lax.dot_general(hidden_ref[...], grad_ref[...], TN, preferred_element_type=F32)
    out_ref[:, 1] = grad_down.astype(BF16).reshape(pieces, units, D)


def expert_layout(weights):
    pieces, _, units, _ = weights.shape
    per_step = max(1, D // units)
    steps = pieces // per_step
    width = per_step * units
    whole = pl.BlockSpec((ROWS, D), lambda step: (0, 0))
    part = pl.BlockSpec((ROWS, width), lambda step: (0, step))
    up = pl.BlockSpec((per_step, 1, units, D), lambda step: (step, 0, 0, 0))
    down = pl.BlockSpec((per_step, 1, units, D), lambda step: (step, 1, 0, 0))
    both = pl.BlockSpec((per_step, 2, units, D), lambda step: (step, 0, 0, 0))
    return steps, width, whole, part, up, down, both


def expert_cost(products, total):
    return pl.CostEstimate(
        flops=products * 2 * ROWS * D * total, bytes_accessed=40 << 20, transcendentals=0
    )


def expert_forward(rows, weights):
    steps, width, whole, part, up, down, _ = expert_layout(weights)
    total = steps * width
    return pl.pallas_call(
        expert_kernel,
        grid=(steps,),
        in_specs=[whole, up, down],
        out_specs=[whole, part, part],
        out_shape=[
            jax.ShapeDtypeStruct((ROWS, D), BF16),
            jax.ShapeDtypeStruct((ROWS, total), BF16),
            jax.ShapeDtypeStruct((ROWS, total), BF16),
        ],
        scratch_shapes=[pltpu.VMEM((ROWS, D), F32)],
        compiler_params=pltpu.CompilerParams(vmem_limit_bytes=56 << 20),
        cost_estimate=expert_cost(2, total),
    )(rows, weights, weights)


def expert_backward(grad_rows, slopes, weights):
    steps, width, whole, part, up, down, _ = expert_layout(weights)
    total = steps * width
    return pl.pallas_call(
        expert_back_kernel,
        grid=(steps,),
        in_specs=[whole, part, up, down],
        out_specs=[whole, part],
        out_shape=[
            jax.ShapeDtypeStruct((ROWS, D), BF16),
            jax.ShapeDtypeStruct((ROWS, total), BF16),
        ],
        scratch_shapes=[pltpu.VMEM((ROWS, D), F32)],
        compiler_params=pltpu.CompilerParams(vmem_limit_bytes=56 << 20),
        cost_estimate=expert_cost(2, total),
    )(grad_rows, slopes, weights, weights)


def expert_weight_grads(rows, grad_rows, hidden, grad_pre, weights):
    steps, width, whole, part, _, _, both = expert_layout(weights)
    total = steps * width
    return pl.pallas_call(
        expert_weight_kernel,
        grid=(steps,),
        in_specs=[whole, whole, part, part],
        out_specs=both,
        out_shape=jax.ShapeDtypeStruct(weights.shape, BF16),
        compiler_params=pltpu.CompilerParams(vmem_limit_bytes=56 << 20),
        cost_estimate=expert_cost(2, total),
    )(rows, grad_rows, hidden, grad_pre)


def swap_rows(pieces, size):
    return [pieces[0]] + [along_quad(pieces[flip], size, flip) for flip in range(1, EXPERTS)]


def body(
    size,
    tokens,
    cotangent,
    lengths,
    routes,
    gain_attn,
    w_qkv,
    w_out,
    table,
    gain_ffn,
    router,
    expert_up,
    expert_down,
):
    quad = lax.axis_index(AXIS) // 2 % 4
    owned = w_qkv.shape[0]
    units = expert_up.shape[0]
    depth = size // 8
    same_expert = [
        [8 * z + 2 * q + c for z in range(depth) for c in range(2)] for q in range(EXPERTS)
    ]

    narrow = jnp.concatenate(
        [router, gain_attn[:, None], gain_ffn[:, None], jnp.zeros((owned, 128 - EXPERTS - 2), BF16)],
        axis=1,
    )
    dense = lax.all_gather(
        jnp.concatenate([w_qkv, w_out, narrow], axis=1), AXIS, axis=0, tiled=True
    )
    qkv_w, out_w = dense[:, : 3 * D], dense[:, 3 * D : 4 * D]
    router_w = dense[:, 4 * D : 4 * D + EXPERTS]
    gain_first = dense[:, 4 * D + EXPERTS].astype(F32)
    gain_second = dense[:, 4 * D + EXPERTS + 1].astype(F32)

    def weights_for(flip):
        return jnp.stack(
            [
                lax.dynamic_index_in_dim(expert_up, quad ^ flip, 1, False),
                lax.dynamic_index_in_dim(expert_down, quad ^ flip, 1, False),
            ]
        )

    mine = jnp.stack(swap_rows([weights_for(flip) for flip in range(EXPERTS)], size), axis=1)
    weights = lax.all_gather(
        mine.reshape(1, 2, EXPERTS * units, D),
        AXIS,
        axis=0,
        tiled=True,
        axis_index_groups=same_expert,
    )

    ends = jnp.cumsum(lengths[0])
    places = lax.iota(jnp.int32, TOK_DEV)
    doc_ids = jnp.sum((places[:, None] >= ends[None, :]).astype(jnp.int32), axis=1)
    spread = lax.iota(jnp.int32, TILE)
    offsets = (
        TILE * jnp.arange(-1, 2)[:, None, None] + spread[None, :, None] - spread[None, None, :]
    )
    buckets = bucket_of(offsets)
    near = jnp.zeros((HEADS, 3, TILE, TILE), F32)
    for bucket in range(BUCKETS):
        near = jnp.where(
            (buckets == bucket)[None], table[bucket].astype(F32)[:, None, None, None], near
        )
    extra_q, extra_k = score_extras(table, doc_ids)

    route = routes[:, 0]
    chosen = (route[:, None] == lax.iota(jnp.int32, EXPERTS)[None, :]).astype(jnp.int32)
    rank = jnp.sum((jnp.cumsum(chosen, axis=0) - chosen) * chosen, axis=1)
    slot = (route ^ quad) * CAP + rank
    route_hot = chosen.astype(F32)

    def dispatch(values):
        return jnp.zeros((ROWS, D), BF16).at[slot].set(values).reshape(EXPERTS, CAP, D)

    tokens_f = tokens.astype(F32)
    normed = rms_norm(tokens_f, gain_first).astype(BF16)
    qkv = jnp.dot(normed, qkv_w, preferred_element_type=F32).astype(BF16)
    late_cotangent, qkv = lax.optimization_barrier((cotangent, qkv))
    upstream_rows = jnp.concatenate(swap_rows(dispatch(late_cotangent), size))
    mixed, logs = attend(qkv, extra_q, extra_k, near)
    attended = tokens_f + jnp.dot(mixed, out_w, preferred_element_type=F32)
    normed_ffn = rms_norm(attended, gain_second).astype(BF16)
    rows = jnp.concatenate(swap_rows(dispatch(normed_ffn), size))
    logits = jnp.dot(normed_ffn, router_w, preferred_element_type=F32)
    probs_route = jax.nn.softmax(logits, axis=-1)
    gate = jnp.sum(probs_route * route_hot, axis=1, keepdims=True)
    gate_slots = jnp.sum(
        jnp.where(slot[None, :] == lax.iota(jnp.int32, ROWS)[:, None], gate[:, 0][None, :], 0.0),
        axis=1,
    ).reshape(EXPERTS, CAP)
    gate_rows = jnp.concatenate(swap_rows(gate_slots, size))
    grad_rows = (gate_rows[:, None] * upstream_rows.astype(F32)).astype(BF16)

    expert_rows, hidden, slopes = expert_forward(rows, weights)
    expert_tok = jnp.concatenate(swap_rows(expert_rows.reshape(EXPERTS, CAP, D), size))[
        slot
    ].astype(F32)
    back_rows, grad_pre = expert_backward(grad_rows, slopes, weights)
    back_tok = jnp.concatenate(swap_rows(back_rows.reshape(EXPERTS, CAP, D), size))[slot].astype(
        F32
    )
    expert_grads = expert_weight_grads(rows, grad_rows, hidden, grad_pre, weights)
    expert_sums = lax.psum_scatter(
        expert_grads, AXIS, scatter_dimension=0, tiled=True, axis_index_groups=same_expert
    ).reshape(2, EXPERTS, units, D)

    output = (attended + gate * expert_tok).astype(BF16)
    upstream = cotangent.astype(F32)
    grad_gate = jnp.sum(upstream * expert_tok, axis=1, keepdims=True)
    grad_logits = (probs_route * (grad_gate * route_hot - grad_gate * gate)).astype(BF16)
    grad_normed_ffn = back_tok + jnp.einsum(
        "te,de->td", grad_logits, router_w, preferred_element_type=F32
    )
    unused_second, second_pull = jax.vjp(rms_norm, attended, gain_second)
    grad_res_norm, grad_gain_second = second_pull(grad_normed_ffn)
    grad_res = upstream + grad_res_norm
    grad_attn_out = grad_res.astype(BF16)
    grad_mixed = jnp.einsum(
        "tf,df->td", grad_attn_out, out_w, preferred_element_type=F32
    ).astype(BF16)
    grad_w_out = jnp.einsum("td,tf->df", mixed, grad_attn_out, preferred_element_type=F32)
    grad_router = jnp.einsum("td,te->de", normed_ffn, grad_logits, preferred_element_type=F32)
    first_sums = scatter_sums(
        jnp.concatenate(
            [
                grad_w_out,
                grad_router,
                grad_gain_second[:, None],
                jnp.zeros((D, 128 - EXPERTS - 1), F32),
            ],
            axis=1,
        ),
        size,
    )

    grad_q, grad_k, grad_v, grad_table = attend_back(
        qkv, grad_mixed, logs, extra_q, extra_k, near, buckets
    )
    table_sum = sum_everywhere(
        jnp.sum(grad_table, axis=-1).reshape(HEADS, BUCKETS).T, size
    )
    grad_qkv = jnp.concatenate([grad_q, grad_k, grad_v], axis=1)
    grad_w_qkv = jnp.einsum("td,tf->df", normed, grad_qkv, preferred_element_type=F32)
    grad_normed = jnp.einsum("tf,df->td", grad_qkv, qkv_w, preferred_element_type=F32)
    unused_first, first_pull = jax.vjp(rms_norm, tokens_f, gain_first)
    grad_tok_norm, grad_gain_first = first_pull(grad_normed)
    grad_tokens = (grad_res + grad_tok_norm).astype(BF16)
    last_sums = scatter_sums(
        jnp.concatenate([grad_w_qkv, grad_gain_first[:, None], jnp.zeros((D, 127), F32)], axis=1),
        size,
    )

    by_flip = jnp.stack(
        swap_rows([expert_sums[:, flip] for flip in range(EXPERTS)], size), axis=2
    ).astype(F32)
    by_expert = jnp.concatenate(
        [lax.dynamic_slice_in_dim(by_flip, quad ^ expert, 1, 2) for expert in range(EXPERTS)],
        axis=2,
    )
    return (
        output,
        grad_tokens,
        last_sums[:, 3 * D],
        last_sums[:, : 3 * D],
        first_sums[:, :D],
        table_sum,
        first_sums[:, D + EXPERTS],
        first_sums[:, D : D + EXPERTS],
        by_expert[0],
        by_expert[1],
    )


def solution(mesh):
    rows = P(AXIS, None)
    in_specs = (
        rows, rows, rows, rows, P(AXIS), rows, rows, P(), P(AXIS), rows,
        P(AXIS, None, None), P(AXIS, None, None),
    )
    out_specs = (
        rows, rows, P(AXIS), rows, rows, P(), P(AXIS), rows,
        P(AXIS, None, None), P(AXIS, None, None),
    )
    return jax.shard_map(
        functools.partial(body, mesh.shape[AXIS]),
        mesh=mesh,
        in_specs=in_specs,
        out_specs=out_specs,
        check_vma=False,
    )
```

time: 1540 us -> 552 us (0.36)
  waiting for transfers between devices: 597 us -> 133 us
  matrix products: 384 us -> 43.2 us
  local copies, waits for them, and re-layouts: 270 us -> 69.5 us
  Pallas kernels: 0 us -> 178 us
  blocking collectives: 122 us -> 0 us
  other arithmetic: 132 us -> 59.8 us
  starting transfers between devices: 0.28 us -> 48.9 us
    reduce_scatter x3 -> x1, waiting for transfers between devices: 550 us -> 0.01 us  [body(): lax.psum_scatter(expert_grads, AXIS, scatter_dimension=0, tiled=True, axi...]
    dot_general x31 -> x9, matrix products: 384 us -> 43.2 us  [the longest x1 9.43 us: body(): jnp.einsum('tf,df->td', grad_qkv, qkv_w, preferred_element_type=F32)]
    pallas_call x0 -> x5, Pallas kernels: none -> 178 us  [the longest x1 48.9 us: attend_back(): pl.pallas_call(attend_back_kernel, grid=(PAIRS,), in_specs=[column(0), co...]
    ppermute x0 -> x40, waiting for transfers between devices: none -> 112 us  [the longest x27 105 us: along_quad(): return lax.ppermute(value, AXIS, [(i, i ^ flip << 1) for i in range(size)])]
    unnamed x2 -> x0, blocking collectives: 82.3 us -> none
    concatenate x1 -> x9, local copies, waits for them, and re-layouts: 74.9 us -> 13.3 us  [the longest x2 8.61 us: body(): jnp.concatenate([grad_w_qkv, grad_gain_first[:, None], jnp.zeros((D, 127)...]
    dot_general x2 -> x0, local copies, waits for them, and re-layouts: 61.4 us -> none  [block_scores(): jnp.einsum('qkb,bh->hqk', onehot, table, preferred_element_type=jnp.float32)]
    ppermute x0 -> x40, starting transfers between devices: none -> 48.7 us  [the longest x27 33.8 us: along_quad(): return lax.ppermute(value, AXIS, [(i, i ^ flip << 1) for i in range(size)])]
  transfers between devices with their start and end apart: 7 -> 43, of which waited for: 4 -> 26; matrix products, arithmetic and copies ran while one was open for 34% -> 28% of each run, Pallas kernels for 0% -> 25%
where the time goes in v1:
time: 552 us; the launch traced here: 547 us
  Pallas kernels  178 us (32%)
  waiting for transfers between devices  133 us (24%)
  local copies, waits for them, and re-layouts  69.5 us (13%)
  other arithmetic  59.8 us (11%)
  starting transfers between devices  48.9 us (9%)
  matrix products  43.2 us (8%)
  between operations  14.9 us (3%)
    ppermute x27, waiting for transfers between devices, along_quad(): return lax.ppermute(value, AXIS, [(i, i ^ flip << 1) for i in range(size)])  105 us
    pallas_call x1, Pallas kernels, attend_back(): pl.pallas_call(attend_back_kernel, grid=(PAIRS,), in_specs=[column(0), co...  48.9 us
    pallas_call x1, Pallas kernels, expert_forward(): pl.pallas_call(expert_kernel, grid=(steps,), in_specs=[whole, up, down],...  41.7 us
    ppermute x27, starting transfers between devices, along_quad(): return lax.ppermute(value, AXIS, [(i, i ^ flip << 1) for i in range(size)])  33.8 us
    pallas_call x1, Pallas kernels, expert_backward(): pl.pallas_call(expert_back_kernel, grid=(steps,), in_specs=[whole, part,...  33.6 us
    pallas_call x1, Pallas kernels, attend(): pl.pallas_call(attend_kernel, grid=(PAIRS,), in_specs=[column(0), column(...  27.6 us
    pallas_call x1, Pallas kernels, expert_weight_grads(): pl.pallas_call(expert_weight_kernel, grid=(steps,), in_specs=[whole, whol...  26.4 us
    all_gather x1, waiting for transfers between devices, body(): lax.all_gather(jnp.concatenate([w_qkv, w_out, narrow], axis=1), AXIS, axi...  20.9 us
  transfers between devices with their start and end apart: 43, of which 26 were waited for; matrix products, arithmetic and copies ran while one was open for 28% of the time, Pallas kernels for 25%

profile of v1, /device:TPU:0, one launch (start us, length us, event | category | flops | bytes accessed | tf_op | source)
XLA Modules:
  0.0 547.2 jit_solution(13133938692764240880)
XLA Ops:
  11.3 5.3 constant_dynamic-slice_fusion.10
  21.6 6.2 %collective-permute-done.4 = bf16[2,96,768]{2,1,0:T(8,128)(2,1)S(1)} collective-permute-done((bf16[2,96,768]{2,1,0:T(8,128)(2,1)S(1)}, bf16[2,96,768]{2,1,0:T(8,128)(2,1)S(1)}, u32[]{:S(2)}, u32[]{:S(2)}) %collective-permute-start.4) | collective-permute-done | bytes 294944 | tf_op jit(solution)/shard_map/ppermute | solution.py:55
  47.5 10.9 %select_select_fusion.near_ref = f32[12,3,128,128]{3,2,1,0:T(8,128)} fusion(f32[12]{0:T(128)S(1)} %get-tuple-element.142, f32[12]{0:T(128)S(1)} %get-tuple-element.143, f32[12]{0:T(128)S(1)} %get-tuple-element.113, f32[12]{0:T(128)S(1)} %get-tuple-element.114, f32[12]{0:T(128)S(1)} %get-tuple-element.115, f32[12]{0:T(128)S(1)} %get-tuple-element.116, ...), kind=kLoop, calls=%fused_computation.46 | loop fusion | flops 18874368 | bytes 3933696 | tf_op jit(solution)/shard_map/jit(_where)/select_n | solution.py:544
  58.4 20.9 %all-gather.3.cloned.1.call-done = bf16[768,3200]{1,0:T(8,128)(2,1)} async-done(((bf16[24,3200]{1,0:T(8,128)(2,1)}), bf16[768,3200]{1,0:T(8,128)(2,1)}) %all-gather.3.cloned.1.call-update) | async-done | bytes 4915216 | tf_op jit(solution)/shard_map/all_gather | solution.py:509
  80.8 6.6 %convolution_convert_fusion.q_ref.k_ref.v_ref = bf16[1024,2304]{1,0:T(8,128)(2,1)S(1)} fusion(bf16[768,3200]{1,0:T(8,128)(2,1)} %all-gather.3.cloned.1.call-done, bf16[1024,768]{1,0:T(8,128)(2,1)} %param.12, f32[768]{0:T(1024)S(1)} %get-tuple-element.109, f32[1024]{0:T(1024)S(1)} %fusion.71), kind=kOutput, calls=%fused_computation.13 | convolution fusion | flops 3629383680 | bytes 9837568 | tf_op jit(solution)/shard_map/dot_general | solution.py:560
  87.4 27.6 %shard_map.195 = (bf16[1024,768]{1,0:T(8,128)(2,1)S(1)}, f32[6,2,1024]{2,1,0:T(2,128)S(1)}) custom-call(bf16[1024,2304]{1,0:T(8,128)(2,1)S(1)} %convolution_convert_fusion.q_ref.k_ref.v_ref, bf16[1024,2304]{1,0:T(8,128)(2,1)S(1)} %convolution_convert_fusion.q_ref.k_ref.v_ref, bf16[1024,2304]{1,0:T(8,128)(2,1)S(1)} %convolution_convert_fusion.q_ref.k_ref.v_ref, ...), custom_call_target="tpu_custom_call" | custom-call | flops 40000000000 | bytes 12582912 | tf_op jit(solution)/shard_map/pallas_call | solution.py:256
  118.4 8.0 %scatter_custom_fusion = bf16[2048,768]{1,0:T(8,128)(2,1)} fusion(s32[1024]{0:T(1024)S(1)} %bitcast.191, bf16[]{:T(256)} %constant.241.clone.1, f32[1024,768]{1,0:T(8,128)S(1)} %get-tuple-element.245, f32[768]{0:T(1024)S(1)} %get-tuple-element.108, f32[1024]{0:T(1024)S(1)} %fusion.72), kind=kCustom, calls=%fused_computation.53 | custom fusion | flops 2359296 | bytes 6299650 | tf_op jit(solution)/shard_map/scatter | solution.py:556
  137.7 6.8 %scatter_custom_fusion.1 = bf16[2048,768]{1,0:T(8,128)(2,1)S(1)} fusion(s32[1024]{0:T(1024)S(1)} %bitcast.192, bf16[1024,768]{1,0:T(8,128)(2,1)} %param.13, bf16[]{:T(256)} %constant.241.clone.1), kind=kCustom, calls=%fused_computation.51 | custom fusion | bytes 3146240 | tf_op jit(solution)/shard_map/scatter | solution.py:556
  156.7 11.3 %collective-permute-done.1 = bf16[512,768]{1,0:T(8,128)(2,1)S(1)} collective-permute-done((bf16[512,768]{1,0:T(8,128)(2,1)}, bf16[512,768]{1,0:T(8,128)(2,1)S(1)}, u32[]{:S(2)}, u32[]{:S(2)}) %collective-permute-start.1) | collective-permute-done | bytes 786464 | tf_op jit(solution)/shard_map/ppermute | solution.py:55
  175.1 14.5 %collective-permute-done.14 = bf16[512,768]{1,0:T(8,128)(2,1)S(1)} collective-permute-done((bf16[512,768]{1,0:T(8,128)(2,1)S(1)}, bf16[512,768]{1,0:T(8,128)(2,1)S(1)}, u32[]{:S(2)}, u32[]{:S(2)}) %collective-permute-start.14) | collective-permute-done | bytes 786464 | tf_op jit(solution)/shard_map/ppermute | solution.py:55
  189.7 11.9 %collective-permute-done.13 = bf16[512,768]{1,0:T(8,128)(2,1)S(1)} collective-permute-done((bf16[512,768]{1,0:T(8,128)(2,1)S(1)}, bf16[512,768]{1,0:T(8,128)(2,1)S(1)}, u32[]{:S(2)}, u32[]{:S(2)}) %collective-permute-start.13) | collective-permute-done | bytes 786464 | tf_op jit(solution)/shard_map/ppermute | solution.py:55
  208.1 41.7 %shard_map.196 = (bf16[2048,768]{1,0:T(8,128)(2,1)}, bf16[2048,3072]{1,0:T(8,128)(2,1)}, bf16[2048,3072]{1,0:T(8,128)(2,1)}) custom-call(bf16[2048,768]{1,0:T(8,128)(2,1)} %pad_maximum_fusion.1.rows_ref, bf16[8,2,384,768]{3,2,1,0:T(8,128)(2,1)} %all-gather.5.cloned.1.call-done.up_ref.down_ref, ...), custom_call_target="tpu_custom_call" | custom-call | flops 19327352832 | bytes 41943040 | tf_op jit(solution)/shard_map/pallas_call | solution.py:430
  256.8 33.6 %shard_map.197 = (bf16[2048,768]{1,0:T(8,128)(2,1)}, bf16[2048,3072]{1,0:T(8,128)(2,1)}) custom-call(bf16[2048,768]{1,0:T(8,128)(2,1)} %multiply_convert_fusion.grad_ref, bf16[2048,3072]{1,0:T(8,128)(2,1)} %get-tuple-element.27.slope_ref, bf16[8,2,384,768]{3,2,1,0:T(8,128)(2,1)} %all-gather.5.cloned.1.call-done.up_ref.down_ref, ...), custom_call_target="tpu_custom_call" | custom-call | flops 19327352832 | bytes 41943040 | tf_op jit(solution)/shard_map/pallas_call | solution.py:449
  290.4 26.4 %shard_map.199 = bf16[8,2,384,768]{3,2,1,0:T(8,128)(2,1)} custom-call(bf16[2048,768]{1,0:T(8,128)(2,1)} %pad_maximum_fusion.1.rows_ref, bf16[2048,768]{1,0:T(8,128)(2,1)} %multiply_convert_fusion.grad_ref, bf16[2048,3072]{1,0:T(8,128)(2,1)} %get-tuple-element.34.hidden_ref, bf16[2048,3072]{1,0:T(8,128)(2,1)} %get-tuple-element.35.grad_pre_ref), custom_call_target="tpu_custom_call" | custom-call | flops 19327352832 | bytes 41943040 | tf_op jit(solution)/shard_map/pallas_call | solution.py:467
  325.8 5.2 gather_fusion
  335.1 7.1 %collective-permute-done.17 = bf16[512,768]{1,0:T(8,128)(2,1)} collective-permute-done((bf16[512,768]{1,0:T(8,128)(2,1)}, bf16[512,768]{1,0:T(8,128)(2,1)}, u32[]{:S(2)}, u32[]{:S(2)}) %collective-permute-start.17) | collective-permute-done | bytes 786464 | tf_op jit(solution)/shard_map/ppermute | solution.py:55
  342.2 13.5 %collective-permute-done.16 = bf16[512,768]{1,0:T(8,128)(2,1)} collective-permute-done((bf16[512,768]{1,0:T(8,128)(2,1)}, bf16[512,768]{1,0:T(8,128)(2,1)}, u32[]{:S(2)}, u32[]{:S(2)}) %collective-permute-start.16) | collective-permute-done | bytes 786464 | tf_op jit(solution)/shard_map/ppermute | solution.py:55
  357.7 5.4 gather_fusion.1
  363.1 5.5 %multiply_reduce_fusion = (f32[768]{0:T(1024)S(1)}, f32[1024]{0:T(1024)S(1)}, f32[1024,768]{1,0:T(8,128)}) fusion(f32[1024,768]{1,0:T(8,128)} %copy-done.7, f32[1024]{0:T(1024)S(1)} %fusion.72, bf16[1024,768]{1,0:T(8,128)(2,1)} %gather_fusion.1, f32[768]{0:T(1024)S(1)} %get-tuple-element.108, bf16[1024,4]{0,1:T(4,128)(2,1)S(1)} %fusion.64, ...), kind=kOutput, calls=%fused_computation.36 | convolution fusion | flops 12581120 | bytes 8083456 | tf_op jit(solution)/shard_map/te,de->td/dot_general | solution.py:594
  379.6 48.9 %shard_map.198 = (bf16[1024,768]{1,0:T(8,128)(2,1)S(1)}, bf16[1024,768]{1,0:T(8,128)(2,1)S(1)}, bf16[1024,768]{1,0:T(8,128)(2,1)S(1)}, f32[6,2,32,128]{3,2,1,0:T(8,128)S(1)}) custom-call(bf16[1024,2304]{1,0:T(8,128)(2,1)} %copy-done.6, bf16[1024,2304]{1,0:T(8,128)(2,1)} %copy-done.6, bf16[1024,2304]{1,0:T(8,128)(2,1)} %copy-done.6, ...), custom_call_target="tpu_custom_call" | custom-call | flops 80000000000 | bytes 20971520 | tf_op jit(solution)/shard_map/pallas_call | solution.py:279
  430.0 9.4 %fusion.3 = (f32[768]{0:T(1024)S(1)}, f32[1024]{0:T(1024)S(1)}, f32[1024,768]{1,0:T(8,128)}) fusion(bf16[1024,768]{1,0:T(8,128)(2,1)S(1)} %copy-done.15, f32[1024]{0:T(1024)S(1)} %copy-done.31, f32[768]{0:T(1024)S(1)} %copy-done.29, bf16[1024,2304]{1,0:T(8,128)(2,1)S(1)} %constant_dynamic-update-slice_fusion, bf16[768,3200]{1,0:T(8,128)(2,1)} %all-gather.3.cloned.1.call-done), kind=kOutput, calls=%fused_computation.24 | convolution fusion | flops 3629381888 | bytes 12990464 | tf_op jit(solution)/shard_map/tf,df->td/dot_general | solution.py:627
  439.7 8.4 %fusion.34 = f32[768,2304]{1,0:T(8,128)} fusion(bf16[1024,2304]{1,0:T(8,128)(2,1)} %copy-done.24, bf16[1024,768]{1,0:T(8,128)(2,1)S(1)} %copy-done.15, f32[768]{0:T(1024)S(1)} %copy-done.29, f32[1024]{0:T(1024)S(1)} %copy-done.31), kind=kOutput, calls=%fused_computation.88 | convolution fusion | flops 3627024384 | bytes 13376512 | tf_op jit(solution)/shard_map/td,tf->df/dot_general | solution.py:626
  448.1 8.3 %concatenate.67 = f32[4,4,2,24,2432]{4,3,2,1,0:T(8,128)} concatenate(f32[4,4,2,24,2304]{4,3,2,1,0:T(8,128)} %bitcast.166, f32[4,4,2,24,1]{4,3,2,1,0:T(8,128)S(1)} %concatenate.73, f32[4,4,2,24,127]{4,3,2,1,0:T(8,128)S(1)} %broadcast_in_dim.601), dimensions={4} | concatenate | bytes 14942208 | tf_op jit(solution)/shard_map/concatenate | solution.py:632
  510.3 5.4 collective-permute-done.21
  (276 shorter events, 183.4 us)
Async XLA Ops:
  7.2 72.2 %all-gather.3.cloned.1.call-start = ((), (), s32[]{:S(2)}) async-start(), calls=%async_computation.1 | async-start | bytes 5068800 | tf_op jit(solution)/shard_map/all_gather | solution.py:509
  11.2 196.9 %all-gather.5.cloned.1.call-start = ((), (), s32[]{:S(2)}) async-start(), calls=%async_computation.2 | async-start | bytes 10616832 | tf_op jit(solution)/shard_map/all_gather | solution.py:526
  21.4 14.0 %collective-permute-start.5 = (bf16[2,96,768]{2,1,0:T(8,128)(2,1)S(1)}, bf16[2,96,768]{2,1,0:T(8,128)(2,1)S(1)}, u32[]{:S(2)}, u32[]{:S(2)}) collective-permute-start(bf16[2,96,768]{2,1,0:T(8,128)(2,1)S(1)} %pad_maximum_fusion.9), channel_id=1, source_target_pairs={{0,6},{1,7},{2,4},{3,5},{4,2},{5,3},{6,0},{7,1},{8,14},{9,15},{10,... | collective-permute-start | bytes 884744 | tf_op jit(solution)/shard_map/ppermute | solution.py:55
  36.7 486.8 %reduce-scatter.2.cloned.1.call-start = ((), (), s32[]{:S(2)}) async-start(), calls=%async_computation.3 | async-start | bytes 10616832 | tf_op jit(solution)/shard_map/reduce_scatter | solution.py:586
  130.1 24.8 %collective-permute-start.2 = (bf16[512,768]{1,0:T(8,128)(2,1)}, bf16[512,768]{1,0:T(8,128)(2,1)}, u32[]{:S(2)}, u32[]{:S(2)}) collective-permute-start(bf16[512,768]{1,0:T(8,128)(2,1)} %get-tuple-element.169), channel_id=1, source_target_pairs={{0,6},{1,7},{2,4},{3,5},{4,2},{5,3},{6,0},{7,1},{8,14},{9,15},{10,... | collective-permute-start | bytes 2359304 | tf_op jit(solution)/shard_map/ppermute | solution.py:55
  135.5 15.6 %collective-permute-start.11 = (f32[512]{0:T(512)S(1)}, f32[512]{0:T(512)S(1)}, u32[]{:S(2)}, u32[]{:S(2)}) collective-permute-start(f32[512]{0:T(512)S(1)} %get-tuple-element.207), channel_id=1, source_target_pairs={{0,6},{1,7},{2,4},{3,5},{4,2},{5,3},{6,0},{7,1},{8,14},{9,15},{10,... | collective-permute-start | bytes 6152 | tf_op jit(solution)/shard_map/ppermute | solution.py:55
  146.7 21.2 %collective-permute-start.1 = (bf16[512,768]{1,0:T(8,128)(2,1)}, bf16[512,768]{1,0:T(8,128)(2,1)S(1)}, u32[]{:S(2)}, u32[]{:S(2)}) collective-permute-start(bf16[512,768]{1,0:T(8,128)(2,1)} %get-tuple-element.170), channel_id=1, source_target_pairs={{0,4},{1,5},{2,6},{3,7},{4,0},{5,1},{6,2},{7,3},{8,12},{9,13},{10,... | collective-permute-start | bytes 2359304 | tf_op jit(solution)/shard_map/ppermute | solution.py:55
  151.2 20.7 %collective-permute-start = (bf16[512,768]{1,0:T(8,128)(2,1)}, bf16[512,768]{1,0:T(8,128)(2,1)S(1)}, u32[]{:S(2)}, u32[]{:S(2)}) collective-permute-start(bf16[512,768]{1,0:T(8,128)(2,1)} %get-tuple-element.171), channel_id=1, source_target_pairs={{0,2},{1,3},{2,0},{3,1},{4,6},{5,7},{6,4},{7,5},{8,10},{9,11},{10,... | collective-permute-start | bytes 2359304 | tf_op jit(solution)/shard_map/ppermute | solution.py:55
  152.8 36.9 %collective-permute-start.14 = (bf16[512,768]{1,0:T(8,128)(2,1)S(1)}, bf16[512,768]{1,0:T(8,128)(2,1)S(1)}, u32[]{:S(2)}, u32[]{:S(2)}) collective-permute-start(bf16[512,768]{1,0:T(8,128)(2,1)S(1)} %get-tuple-element.161), channel_id=1, source_target_pairs={{0,6},{1,7},{2,4},{3,5},{4,2},{5,3},{6,0},{7,1},{8,14},{9,15},{10,... | collective-permute-start | bytes 2359304 | tf_op jit(solution)/shard_map/ppermute | solution.py:55
  154.4 47.2 %collective-permute-start.13 = (bf16[512,768]{1,0:T(8,128)(2,1)S(1)}, bf16[512,768]{1,0:T(8,128)(2,1)S(1)}, u32[]{:S(2)}, u32[]{:S(2)}) collective-permute-start(bf16[512,768]{1,0:T(8,128)(2,1)S(1)} %get-tuple-element.162), channel_id=1, source_target_pairs={{0,4},{1,5},{2,6},{3,7},{4,0},{5,1},{6,2},{7,3},{8,12},{9,13},{10,... | collective-permute-start | bytes 2359304 | tf_op jit(solution)/shard_map/ppermute | solution.py:55
  154.9 49.0 %collective-permute-start.12 = (bf16[512,768]{1,0:T(8,128)(2,1)S(1)}, bf16[512,768]{1,0:T(8,128)(2,1)S(1)}, u32[]{:S(2)}, u32[]{:S(2)}) collective-permute-start(bf16[512,768]{1,0:T(8,128)(2,1)S(1)} %get-tuple-element.163), channel_id=1, source_target_pairs={{0,2},{1,3},{2,0},{3,1},{4,6},{5,7},{6,4},{7,5},{8,10},{9,11},{10,... | collective-permute-start | bytes 2359304 | tf_op jit(solution)/shard_map/ppermute | solution.py:55
  253.3 70.1 %collective-permute-start.8 = (bf16[512,768]{1,0:T(8,128)(2,1)}, bf16[512,768]{1,0:T(8,128)(2,1)}, u32[]{:S(2)}, u32[]{:S(2)}) collective-permute-start(bf16[512,768]{1,0:T(8,128)(2,1)} %get-tuple-element.165), channel_id=1, source_target_pairs={{0,6},{1,7},{2,4},{3,5},{4,2},{5,3},{6,0},{7,1},{8,14},{9,15},{10,... | collective-permute-start | bytes 2359304 | tf_op jit(solution)/shard_map/ppermute | solution.py:55
  254.7 69.3 %collective-permute-start.7 = (bf16[512,768]{1,0:T(8,128)(2,1)}, bf16[512,768]{1,0:T(8,128)(2,1)}, u32[]{:S(2)}, u32[]{:S(2)}) collective-permute-start(bf16[512,768]{1,0:T(8,128)(2,1)} %get-tuple-element.166), channel_id=1, source_target_pairs={{0,4},{1,5},{2,6},{3,7},{4,0},{5,1},{6,2},{7,3},{8,12},{9,13},{10,... | collective-permute-start | bytes 2359304 | tf_op jit(solution)/shard_map/ppermute | solution.py:55
  256.2 67.8 %collective-permute-start.6 = (bf16[512,768]{1,0:T(8,128)(2,1)}, bf16[512,768]{1,0:T(8,128)(2,1)}, u32[]{:S(2)}, u32[]{:S(2)}) collective-permute-start(bf16[512,768]{1,0:T(8,128)(2,1)} %get-tuple-element.167), channel_id=1, source_target_pairs={{0,2},{1,3},{2,0},{3,1},{4,6},{5,7},{6,4},{7,5},{8,10},{9,11},{10,... | collective-permute-start | bytes 2359304 | tf_op jit(solution)/shard_map/ppermute | solution.py:55
  320.5 21.7 %collective-permute-start.17 = (bf16[512,768]{1,0:T(8,128)(2,1)}, bf16[512,768]{1,0:T(8,128)(2,1)}, u32[]{:S(2)}, u32[]{:S(2)}) collective-permute-start(bf16[512,768]{1,0:T(8,128)(2,1)} %get-tuple-element.157), channel_id=1, source_target_pairs={{0,6},{1,7},{2,4},{3,5},{4,2},{5,3},{6,0},{7,1},{8,14},{9,15},{10,... | collective-permute-start | bytes 2359304 | tf_op jit(solution)/shard_map/ppermute | solution.py:55
  321.8 33.8 %collective-permute-start.16 = (bf16[512,768]{1,0:T(8,128)(2,1)}, bf16[512,768]{1,0:T(8,128)(2,1)}, u32[]{:S(2)}, u32[]{:S(2)}) collective-permute-start(bf16[512,768]{1,0:T(8,128)(2,1)} %get-tuple-element.158), channel_id=1, source_target_pairs={{0,4},{1,5},{2,6},{3,7},{4,0},{5,1},{6,2},{7,3},{8,12},{9,13},{10,... | collective-permute-start | bytes 2359304 | tf_op jit(solution)/shard_map/ppermute | solution.py:55
  323.4 32.3 %collective-permute-start.15 = (bf16[512,768]{1,0:T(8,128)(2,1)}, bf16[512,768]{1,0:T(8,128)(2,1)}, u32[]{:S(2)}, u32[]{:S(2)}) collective-permute-start(bf16[512,768]{1,0:T(8,128)(2,1)} %get-tuple-element.159), channel_id=1, source_target_pairs={{0,2},{1,3},{2,0},{3,1},{4,6},{5,7},{6,4},{7,5},{8,10},{9,11},{10,... | collective-permute-start | bytes 2359304 | tf_op jit(solution)/shard_map/ppermute | solution.py:55
  460.1 31.8 %collective-permute-start.18 = (bf16[4,4,24,2432]{3,2,1,0:T(8,128)(2,1)}, bf16[4,4,24,2432]{3,2,1,0:T(8,128)(2,1)}, u32[]{:S(2)}, u32[]{:S(2)}) collective-permute-start(bf16[4,4,24,2432]{3,2,1,0:T(8,128)(2,1)} %fusion.14), channel_id=1, source_target_pairs={{0,1},{1,0},{2,3},{3,2},{4,5},{5,4},{6,7},{7,6},{8,9},{9,8},{10,11... | collective-permute-start | bytes 5603336 | tf_op jit(solution)/shard_map/ppermute | solution.py:59
  464.9 11.5 %collective-permute-start.25 = (bf16[4,4,24,896]{3,2,0,1:T(8,128)(2,1)}, bf16[4,4,24,896]{3,2,0,1:T(8,128)(2,1)}, u32[]{:S(2)}, u32[]{:S(2)}) collective-permute-start(bf16[4,4,24,896]{3,2,0,1:T(8,128)(2,1)} %fusion.26), channel_id=1, source_target_pairs={{0,1},{1,0},{2,3},{3,2},{4,5},{5,4},{6,7},{7,6},{8,9},{9,8},{10,11... | collective-permute-start | bytes 2064392 | tf_op jit(solution)/shard_map/ppermute | solution.py:59
  481.3 16.5 %collective-permute-start.36 = (f32[32,12]{0,1:T(8,128)S(1)}, f32[32,12]{0,1:T(8,128)S(1)}, u32[]{:S(2)}, u32[]{:S(2)}) collective-permute-start(f32[32,12]{0,1:T(8,128)S(1)} %add.1784), channel_id=1, source_target_pairs={{0,16},{1,17},{2,18},{3,19},{4,20},{5,21},{6,22},{7,23},{8,24},{9,... | collective-permute-start | bytes 4616 | tf_op jit(solution)/shard_map/ppermute | solution.py:93
  488.3 15.0 %collective-permute-start.31 = (bf16[24,896]{1,0:T(8,128)(2,1)S(1)}, bf16[24,896]{1,0:T(8,128)(2,1)S(1)}, u32[]{:S(2)}, u32[]{:S(2)}) collective-permute-start(bf16[24,896]{1,0:T(8,128)(2,1)S(1)} %get-tuple-element.204), channel_id=1, source_target_pairs={{0,24},{1,25},{2,26},{3,27},{4,28},{5,29},{6,30},{7,31},{8,0},{9,1... | collective-permute-start | bytes 129032 | tf_op jit(solution)/shard_map/ppermute | solution.py:49
  497.1 13.2 %collective-permute-start.19 = (bf16[4,24,2432]{2,1,0:T(8,128)(2,1)S(1)}, bf16[4,24,2432]{2,1,0:T(8,128)(2,1)S(1)}, u32[]{:S(2)}, u32[]{:S(2)}) collective-permute-start(bf16[4,24,2432]{2,1,0:T(8,128)(2,1)S(1)} %get-tuple-element.180), channel_id=1, source_target_pairs={{0,2},{1,3},{2,0},{3,1},{4,6},{5,7},{6,4},{7,5},{8,10},{9,11},{10,... | collective-permute-start | bytes 1400840 | tf_op jit(solution)/shard_map/ppermute | solution.py:55
  497.7 18.0 %collective-permute-start.21 = (bf16[4,24,2432]{2,1,0:T(8,128)(2,1)S(1)}, bf16[4,24,2432]{2,1,0:T(8,128)(2,1)S(1)}, u32[]{:S(2)}, u32[]{:S(2)}) collective-permute-start(bf16[4,24,2432]{2,1,0:T(8,128)(2,1)S(1)} %get-tuple-element.181), channel_id=1, source_target_pairs={{0,6},{1,7},{2,4},{3,5},{4,2},{5,3},{6,0},{7,1},{8,14},{9,15},{10,... | collective-permute-start | bytes 1400840 | tf_op jit(solution)/shard_map/ppermute | solution.py:55
  499.3 17.9 %collective-permute-start.20 = (bf16[4,24,2432]{2,1,0:T(8,128)(2,1)S(1)}, bf16[4,24,2432]{2,1,0:T(8,128)(2,1)S(1)}, u32[]{:S(2)}, u32[]{:S(2)}) collective-permute-start(bf16[4,24,2432]{2,1,0:T(8,128)(2,1)S(1)} %get-tuple-element.182), channel_id=1, source_target_pairs={{0,4},{1,5},{2,6},{3,7},{4,0},{5,1},{6,2},{7,3},{8,12},{9,13},{10,... | collective-permute-start | bytes 1400840 | tf_op jit(solution)/shard_map/ppermute | solution.py:55
  (53 other events, 523.1 us)
Sparse Core Ops, SparseCore 0:
  11.5 67.8 all-gather.2
  81.6 89.5 all-gather.4
  317.0 98.3 reduce-scatter.1

commit v2 on v1

--- a/solution.py
+++ b/solution.py
@@ -11,10 +11,14 @@
 HEADS = 12
 HEAD_DIM = 64
 PAIRS = HEADS // 2
+PARTS = 3
+PART_PAIRS = PAIRS // PARTS
+PART = D // PARTS
 BUCKETS = 32
 EXPERTS = 4
 TOK_DEV = 1024
 CAP = 512
+ROW_CHUNK = 256
 ROWS = EXPERTS * CAP
 AXIS = "fsdp"
 F32 = jnp.float32
@@ -59,40 +63,40 @@
     return lax.ppermute(value, AXIS, [(i, i ^ 1) for i in range(size)])
 
 
-def scatter_sums(partial, size):
+def destinations(size, owned):
     me = lax.axis_index(AXIS)
     depth = size // 8
     z, quad, core = me // 8, me // 2 % 4, me % 2
-    rows = partial.shape[0] // size
-    view = partial.reshape(depth, 4, 2, rows, partial.shape[1])
-    mine = lax.dynamic_index_in_dim(view, core, 2, False)
-    other = lax.dynamic_index_in_dim(view, 1 - core, 2, False).astype(BF16)
-    total = mine + along_core(other, size).astype(F32)
-    low = total.astype(BF16)
-    arrived = [
-        along_quad(lax.dynamic_index_in_dim(low, quad ^ flip, 1, False), size, flip)
-        for flip in range(1, 4)
-    ]
-    total = lax.dynamic_index_in_dim(total, quad, 1, False)
-    for piece in arrived:
-        total = total + piece.astype(F32)
-    low = total.astype(BF16)
-    arrived = [
-        along_z(lax.dynamic_index_in_dim(low, (z + shift) % depth, 0, False), size, shift)
-        for shift in range(1, depth)
-    ]
-    total = lax.dynamic_index_in_dim(total, z, 0, False)
-    for piece in arrived:
-        total = total + piece.astype(F32)
-    return total
-
-
-def sum_everywhere(value, size):
-    step = 1
-    while step < size:
-        value = value + lax.ppermute(value, AXIS, [(i, i ^ step) for i in range(size)])
-        step *= 2
-    return value
+    place = lax.iota(jnp.int32, size * owned)
+    block, inner = place // owned, place % owned
+    shift, flip, cross = block % depth, block // depth % 4, block // (depth * 4)
+    owner = ((z + shift) % depth * 4 + (quad ^ flip)) * 2 + (core ^ cross)
+    source = owner * owned + inner
+    return (place[:, None] == source[None, :]).astype(BF16)
+
+
+def for_quad(total):
+    view = total.reshape(4, -1, total.shape[1])
+    return [view[flip].astype(BF16) for flip in range(1, 4)], view
+
+
+def add_z(total, size):
+    depth = size // 8
+    view = total.reshape(depth, -1, total.shape[1])
+    out = view[0]
+    for shift in range(1, depth):
+        out = out + along_z(view[shift].astype(BF16), size, shift).astype(F32)
+    return out
+
+
+def sum_all(values):
+    while len(values) > 1:
+        values = [left + right for left, right in zip(values[::2], values[1::2])]
+    return values[0]
+
+
+def along_z_flip(value, size, flip):
+    return lax.ppermute(value, AXIS, [(i, i ^ (flip << 3)) for i in range(size)])
 
 
 def score_tile(tile, block, keys, queries, near_ref, head):
@@ -156,7 +160,7 @@
 
 def attend_back_kernel(
     q_ref, k_ref, v_ref, grad_ref, log_ref, extra_q_ref, extra_k_ref, near_ref, bucket_ref,
-    grad_q_ref, grad_k_ref, grad_v_ref, grad_table_ref,
+    grad_qkv_ref, grad_table_ref,
     prob_ref, slope_ref, low_prob_ref, low_grad_ref, turned_ref, key_sum_ref, value_sum_ref,
     near_sum_ref,
 ):
@@ -234,20 +238,20 @@
             if bucket == 31:
                 row = row + far_sums[1]
             grad_table_ref[0, head, bucket : bucket + 1, :] = jnp.sum(row, axis=0, keepdims=True)
-    grad_q_ref[...] = turned_ref[...].T.astype(BF16)
-    grad_k_ref[...] = key_sum_ref[...].astype(BF16)
-    grad_v_ref[...] = value_sum_ref[...].astype(BF16)
+    grad_qkv_ref[0] = turned_ref[...].T.astype(BF16)
+    grad_qkv_ref[1] = key_sum_ref[...].astype(BF16)
+    grad_qkv_ref[2] = value_sum_ref[...].astype(BF16)
 
 
 def column(first):
     return pl.BlockSpec((TOK_DEV, 2 * HEAD_DIM), lambda pair: (0, first + pair))
 
 
-def score_specs():
+def score_specs(first):
     return [
         pl.BlockSpec((2, TOK_DEV, 2 * HEAD_DIM), lambda pair: (0, 0, 0)),
-        pl.BlockSpec((2, TOK_DEV, 2 * HEAD_DIM), lambda pair: (pair, 0, 0)),
-        pl.BlockSpec((2, 3, TILE, TILE), lambda pair: (pair, 0, 0, 0)),
+        pl.BlockSpec((2, TOK_DEV, 2 * HEAD_DIM), lambda pair: (first + pair, 0, 0)),
+        pl.BlockSpec((2, 3, TILE, TILE), lambda pair: (first + pair, 0, 0, 0)),
     ]
 
 
@@ -256,7 +260,7 @@
     return pl.pallas_call(
         attend_kernel,
         grid=(PAIRS,),
-        in_specs=[column(0), column(PAIRS), column(2 * PAIRS)] + score_specs(),
+        in_specs=[column(0), column(PAIRS), column(2 * PAIRS)] + score_specs(0),
         out_specs=[column(0), logs],
         out_shape=[
             jax.ShapeDtypeStruct((TOK_DEV, D), BF16),
@@ -274,25 +278,27 @@
     )(qkv, qkv, qkv, extra_q, extra_k, near)
 
 
-def attend_back(qkv, grad_mixed, logs, extra_q, extra_k, near, buckets):
-    log_spec = pl.BlockSpec((1, 2, TOK_DEV), lambda pair: (pair, 0, 0))
+def attend_back(part, qkv, grad_mixed, logs, extra_q, extra_k, near, buckets):
+    first = part * PART_PAIRS
     return pl.pallas_call(
         attend_back_kernel,
-        grid=(PAIRS,),
-        in_specs=[column(0), column(PAIRS), column(2 * PAIRS), column(0), log_spec]
-        + score_specs()
+        grid=(PART_PAIRS,),
+        in_specs=[
+            column(first),
+            column(PAIRS + first),
+            column(2 * PAIRS + first),
+            column(first),
+            pl.BlockSpec((1, 2, TOK_DEV), lambda pair: (first + pair, 0, 0)),
+        ]
+        + score_specs(first)
         + [pl.BlockSpec((3, TILE, TILE), lambda pair: (0, 0, 0))],
         out_specs=[
-            column(0),
-            column(0),
-            column(0),
+            pl.BlockSpec((3, TOK_DEV, 2 * HEAD_DIM), lambda pair: (0, 0, pair)),
             pl.BlockSpec((1, 2, BUCKETS, TILE), lambda pair: (pair, 0, 0, 0)),
         ],
         out_shape=[
-            jax.ShapeDtypeStruct((TOK_DEV, D), BF16),
-            jax.ShapeDtypeStruct((TOK_DEV, D), BF16),
-            jax.ShapeDtypeStruct((TOK_DEV, D), BF16),
-            jax.ShapeDtypeStruct((PAIRS, 2, BUCKETS, TILE), F32),
+            jax.ShapeDtypeStruct((3, TOK_DEV, PART), BF16),
+            jax.ShapeDtypeStruct((PART_PAIRS, 2, BUCKETS, TILE), F32),
         ],
         scratch_shapes=[
             pltpu.VMEM((2, TOK_DEV, QUERY_BLOCK), F32),
@@ -306,7 +312,9 @@
         ],
         compiler_params=pltpu.CompilerParams(vmem_limit_bytes=48 << 20),
         cost_estimate=pl.CostEstimate(
-            flops=80_000_000_000, bytes_accessed=20 << 20, transcendentals=HEADS << 20
+            flops=80_000_000_000 // PARTS,
+            bytes_accessed=8 << 20,
+            transcendentals=(HEADS << 20) // PARTS,
         ),
     )(qkv, qkv, qkv, grad_mixed, logs, extra_q, extra_k, near, buckets)
 
@@ -341,68 +349,227 @@
 def gelu_with_slope(x):
     scale, cubic = 0.7978845608028654, 0.044715
     square = x * x
-    curve = jnp.tanh(scale * x * (1.0 + cubic * square))
-    half = 0.5 * (1.0 + curve)
-    slope = half + 0.5 * x * (1.0 - curve * curve) * (scale * (1.0 + 3.0 * cubic * square))
-    return x * half, slope
-
-
-def expert_kernel(rows_ref, up_ref, down_ref, out_ref, hidden_ref, slope_ref, sum_ref):
+    half = 0.5 + 0.5 * jnp.tanh(x * (scale + (scale * cubic) * square))
+    value = x * half
+    slope = half + value * (1.0 - half) * (2.0 * scale + (6.0 * scale * cubic) * square)
+    return value, slope
+
+
+def expert_kernel(
+    rows_ref, upstream_ref, gate_ref, up_ref, down_ref,
+    out_ref, back_ref, grad_ref, hidden_ref, grad_pre_ref, out_sum_ref, back_sum_ref,
+):
     step = pl.program_id(0)
     up = up_ref[...].reshape(-1, D)
     down = down_ref[...].reshape(-1, D)
-    for chunk in range(EXPERTS):
-        at = slice(chunk * CAP, (chunk + 1) * CAP)
+
+    @pl.when(step == 0)
+    def _():
+        out_sum_ref[...] = jnp.zeros_like(out_sum_ref)
+        back_sum_ref[...] = jnp.zeros_like(back_sum_ref)
+        gate = jnp.broadcast_to(gate_ref[...], (TILE, CAP)).T
+        for first in range(0, D, TILE):
+            lanes = slice(first, first + TILE)
+            grad_ref[:, lanes] = (gate * upstream_ref[:, lanes].astype(F32)).astype(BF16)
+
+    for first in range(0, CAP, ROW_CHUNK):
+        at = slice(first, first + ROW_CHUNK)
         pre = lax.dot_general(rows_ref[at], up, NT, preferred_element_type=F32)
+        grad_hidden = lax.dot_general(grad_ref[at], down, NT, preferred_element_type=F32)
         hidden, slope = gelu_with_slope(pre)
-        low = hidden.astype(BF16)
-        hidden_ref[at] = low
-        slope_ref[at] = slope.astype(BF16)
-        part = lax.dot_general(low, down, NN, preferred_element_type=F32)
-
-        @pl.when(step == 0)
-        def _():
-            sum_ref[at] = part
-
-        @pl.when(step > 0)
-        def _():
-            sum_ref[at] += part
+        hidden = hidden.astype(BF16)
+        grad_pre = (grad_hidden * slope).astype(BF16)
+        hidden_ref[at] = hidden
+        grad_pre_ref[at] = grad_pre
+        out_sum_ref[at] += lax.dot_general(hidden, down, NN, preferred_element_type=F32)
+        back_sum_ref[at] += lax.dot_general(grad_pre, up, NN, preferred_element_type=F32)
 
     @pl.when(step == pl.num_programs(0) - 1)
     def _():
-        out_ref[...] = sum_ref[...].astype(BF16)
-
-
-def expert_back_kernel(grad_ref, slope_ref, up_ref, down_ref, out_ref, grad_pre_ref, sum_ref):
-    step = pl.program_id(0)
-    up = up_ref[...].reshape(-1, D)
-    down = down_ref[...].reshape(-1, D)
+        out_ref[...] = out_sum_ref[...].astype(BF16)
+        back_ref[...] = back_sum_ref[...].astype(BF16)
+
+
+def expert_weight_kernel(*refs):
+    out_ref = refs[-1]
+    rows, grads, hiddens, grad_pres = (refs[EXPERTS * i : EXPERTS * (i + 1)] for i in range(4))
+    pieces, _, units, _ = out_ref.shape
+    for which, lefts, rights in ((0, grad_pres, rows), (1, hiddens, grads)):
+        total = None
+        for left_ref, right_ref in zip(lefts, rights):
+            part = lax.dot_general(
+                left_ref[...], right_ref[...], TN, preferred_element_type=F32
+            )
+            total = part if total is None else total + part
+        out_ref[:, which] = total.astype(BF16).reshape(pieces, units, D)
+
+
+def weight_kernel(left_ref, right_ref, mine_ref, other_ref):
+    half = D // 2
+    for which in range(right_ref.shape[0]):
+        width = right_ref.shape[2]
+        lanes = slice(which * width, (which + 1) * width)
+        for first, out_ref in ((0, mine_ref), (half, other_ref)):
+            part = lax.dot_general(
+                left_ref[:, first : first + half],
+                right_ref[which],
+                TN,
+                preferred_element_type=F32,
+            )
+            out_ref[:, lanes] = part.astype(out_ref.dtype)
+
+
+def weight_halves(left, right):
+    width = right.shape[0] * right.shape[2]
+    whole = pl.BlockSpec((TOK_DEV, D), lambda step: (0, 0))
+    out = pl.BlockSpec((D // 2, width), lambda step: (0, 0))
+    return pl.pallas_call(
+        weight_kernel,
+        grid=(1,),
+        in_specs=[whole, pl.BlockSpec(right.shape, lambda step: (0, 0, 0))],
+        out_specs=[out, out],
+        out_shape=[
+            jax.ShapeDtypeStruct((D // 2, width), F32),
+            jax.ShapeDtypeStruct((D // 2, width), BF16),
+        ],
+        compiler_params=pltpu.CompilerParams(vmem_limit_bytes=40 << 20),
+        cost_estimate=pl.CostEstimate(
+            flops=2 * TOK_DEV * D * width, bytes_accessed=6 << 20, transcendentals=0
+        ),
+    )(left, right)
+
+
+def token_grad_kernel(
+    grads_0, grads_1, grads_2, weights_0, weights_1, weights_2, tokens_ref, gain_ref, rest_ref,
+    out_ref,
+):
+    grad = None
+    for grads_ref, weights_ref in zip(
+        (grads_0, grads_1, grads_2), (weights_0, weights_1, weights_2)
+    ):
+        for which in range(3):
+            part = lax.dot_general(
+                grads_ref[which],
+                weights_ref[:, which * PART : (which + 1) * PART],
+                NT,
+                preferred_element_type=F32,
+            )
+            grad = part if grad is None else grad + part
+    values = tokens_ref[...].astype(F32)
+    grad = grad * gain_ref[...]
+    inverse = lax.rsqrt(jnp.mean(values * values, axis=-1, keepdims=True) + norm_eps)
+    along = jnp.mean(values * grad, axis=-1, keepdims=True)
+    out_ref[...] = (
+        rest_ref[...] + inverse * (grad - values * (inverse * inverse * along))
+    ).astype(BF16)
+
+
+def token_grad(grads, weights, tokens, gain, rest):
+    rows = TOK_DEV // 4
+    part = pl.BlockSpec((rows, D), lambda step: (step, 0))
+    return pl.pallas_call(
+        token_grad_kernel,
+        grid=(TOK_DEV // rows,),
+        in_specs=[pl.BlockSpec((3, rows, PART), lambda step: (0, step, 0))] * PARTS
+        + [pl.BlockSpec((D, 3 * PART), lambda step: (0, 0))] * PARTS
+        + [part, pl.BlockSpec((1, D), lambda step: (0, 0)), part],
+        out_specs=part,
+        out_shape=jax.ShapeDtypeStruct((TOK_DEV, D), BF16),
+        compiler_params=pltpu.CompilerParams(vmem_limit_bytes=48 << 20),
+        cost_estimate=pl.CostEstimate(
+            flops=6 * TOK_DEV * D * D, bytes_accessed=14 << 20, transcendentals=0
+        ),
+    )(*grads, *weights, tokens, gain, rest)
+
+
+def early_kernel(
+    slot_ref, values_ref, bucket_ref, table_ref, out_0, out_1, out_2, out_3, near_ref
+):
+    dispatch_kernel(slot_ref, values_ref, None, out_0, out_1, out_2, out_3)
+
+    def fill(head, carry):
+        for apart, first, last in ((0, 1, 16), (1, 0, BUCKETS), (2, 17, BUCKETS)):
+            buckets = bucket_ref[apart]
+            tile = jnp.zeros((TILE, TILE), F32)
+            for bucket in range(first, last):
+                tile = jnp.where(buckets == bucket, table_ref[bucket, head], tile)
+            near_ref[head, apart] = tile
+        return carry
+
+    lax.fori_loop(0, HEADS, fill, 0)
+
+
+def early(slot_row, values, buckets, table):
+    vmem = pl.BlockSpec(memory_space=pltpu.VMEM)
+    result = pl.pallas_call(
+        early_kernel,
+        in_specs=[vmem, vmem, vmem, pl.BlockSpec(memory_space=pltpu.SMEM)],
+        out_shape=[jax.ShapeDtypeStruct((CAP, D), BF16)] * EXPERTS
+        + [jax.ShapeDtypeStruct((HEADS, 3, TILE, TILE), F32)],
+        compiler_params=pltpu.CompilerParams(vmem_limit_bytes=40 << 20),
+        cost_estimate=pl.CostEstimate(
+            flops=8 * ROWS * TOK_DEV * D, bytes_accessed=6 << 20, transcendentals=0
+        ),
+    )(slot_row, values, buckets, table)
+    return list(result[:EXPERTS]), result[EXPERTS]
+
+
+def dispatch_kernel(slot_ref, values_ref, gate_ref, out_0, out_1, out_2, out_3, *gate_outs):
+    values = values_ref[...]
+    for chunk, out_ref in enumerate((out_0, out_1, out_2, out_3)):
+        wanted = chunk * CAP + lax.broadcasted_iota(jnp.int32, (CAP, TOK_DEV), 0)
+        hit = wanted == slot_ref[...]
+        out_ref[...] = lax.dot_general(
+            jnp.where(hit, 1.0, 0.0).astype(BF16), values, NN, preferred_element_type=F32
+        ).astype(BF16)
+        if gate_outs:
+            gates = jnp.sum(jnp.where(hit, gate_ref[...], 0.0), axis=1, keepdims=True)
+            gate_outs[chunk][...] = jnp.broadcast_to(gates, (CAP, TILE)).T[0:1]
+
+
+def dispatch(slot_row, values, gate_row):
+    result = pl.pallas_call(
+        dispatch_kernel,
+        out_shape=[jax.ShapeDtypeStruct((CAP, D), BF16)] * EXPERTS
+        + [jax.ShapeDtypeStruct((1, CAP), F32)] * EXPERTS,
+        compiler_params=pltpu.CompilerParams(vmem_limit_bytes=40 << 20),
+        cost_estimate=pl.CostEstimate(
+            flops=2 * ROWS * TOK_DEV * D, bytes_accessed=6 << 20, transcendentals=0
+        ),
+    )(slot_row, values, gate_row)
+    return list(result[:EXPERTS]), list(result[EXPERTS:])
+
+
+def combine_kernel(slot_ref, *refs):
+    rows = slot_ref.shape[0]
+    totals = [None, None]
     for chunk in range(EXPERTS):
-        at = slice(chunk * CAP, (chunk + 1) * CAP)
-        grad_hidden = lax.dot_general(grad_ref[at], down, NT, preferred_element_type=F32)
-        grad_pre = (grad_hidden * slope_ref[at].astype(F32)).astype(BF16)
-        grad_pre_ref[at] = grad_pre
-        part = lax.dot_general(grad_pre, up, NN, preferred_element_type=F32)
-
-        @pl.when(step == 0)
-        def _():
-            sum_ref[at] = part
-
-        @pl.when(step > 0)
-        def _():
-            sum_ref[at] += part
-
-    @pl.when(step == pl.num_programs(0) - 1)
-    def _():
-        out_ref[...] = sum_ref[...].astype(BF16)
-
-
-def expert_weight_kernel(rows_ref, grad_ref, hidden_ref, grad_pre_ref, out_ref):
-    pieces, _, units, _ = out_ref.shape
-    grad_up = lax.dot_general(grad_pre_ref[...], rows_ref[...], TN, preferred_element_type=F32)
-    out_ref[:, 0] = grad_up.astype(BF16).reshape(pieces, units, D)
-    grad_down = lax.dot_general(hidden_ref[...], grad_ref[...], TN, preferred_element_type=F32)
-    out_ref[:, 1] = grad_down.astype(BF16).reshape(pieces, units, D)
+        place = chunk * CAP + lax.broadcasted_iota(jnp.int32, (rows, CAP), 1)
+        hit = jnp.where(place == slot_ref[...], 1.0, 0.0).astype(BF16)
+        for which in range(2):
+            part = lax.dot_general(
+                hit, refs[which * EXPERTS + chunk][...], NN, preferred_element_type=F32
+            )
+            totals[which] = part if totals[which] is None else totals[which] + part
+    for which in range(2):
+        refs[2 * EXPERTS + which][...] = totals[which]
+
+
+def combine(slot_column, first, second):
+    rows = TOK_DEV // 4
+    part = pl.BlockSpec((rows, D), lambda step: (step, 0))
+    return pl.pallas_call(
+        combine_kernel,
+        grid=(TOK_DEV // rows,),
+        in_specs=[pl.BlockSpec((rows, 1), lambda step: (step, 0))]
+        + [pl.BlockSpec((CAP, D), lambda step: (0, 0))] * (2 * EXPERTS),
+        out_specs=[part, part],
+        out_shape=[jax.ShapeDtypeStruct((TOK_DEV, D), F32)] * 2,
+        compiler_params=pltpu.CompilerParams(vmem_limit_bytes=60 << 20),
+        cost_estimate=pl.CostEstimate(
+            flops=4 * ROWS * TOK_DEV * D, bytes_accessed=12 << 20, transcendentals=0
+        ),
+    )(slot_column, *first, *second)
 
 
 def expert_layout(weights):
@@ -410,69 +577,44 @@
     per_step = max(1, D // units)
     steps = pieces // per_step
     width = per_step * units
-    whole = pl.BlockSpec((ROWS, D), lambda step: (0, 0))
-    part = pl.BlockSpec((ROWS, width), lambda step: (0, step))
+    whole = pl.BlockSpec((CAP, D), lambda step: (0, 0))
+    part = pl.BlockSpec((CAP, width), lambda step: (0, step))
     up = pl.BlockSpec((per_step, 1, units, D), lambda step: (step, 0, 0, 0))
     down = pl.BlockSpec((per_step, 1, units, D), lambda step: (step, 1, 0, 0))
     both = pl.BlockSpec((per_step, 2, units, D), lambda step: (step, 0, 0, 0))
-    return steps, width, whole, part, up, down, both
-
-
-def expert_cost(products, total):
-    return pl.CostEstimate(
-        flops=products * 2 * ROWS * D * total, bytes_accessed=40 << 20, transcendentals=0
-    )
-
-
-def expert_forward(rows, weights):
-    steps, width, whole, part, up, down, _ = expert_layout(weights)
-    total = steps * width
+    return steps, steps * width, whole, part, up, down, both
+
+
+def expert_pass(rows, upstream, gate, weights):
+    steps, total, whole, part, up, down, _ = expert_layout(weights)
     return pl.pallas_call(
         expert_kernel,
         grid=(steps,),
-        in_specs=[whole, up, down],
-        out_specs=[whole, part, part],
-        out_shape=[
-            jax.ShapeDtypeStruct((ROWS, D), BF16),
-            jax.ShapeDtypeStruct((ROWS, total), BF16),
-            jax.ShapeDtypeStruct((ROWS, total), BF16),
-        ],
-        scratch_shapes=[pltpu.VMEM((ROWS, D), F32)],
-        compiler_params=pltpu.CompilerParams(vmem_limit_bytes=56 << 20),
-        cost_estimate=expert_cost(2, total),
-    )(rows, weights, weights)
-
-
-def expert_backward(grad_rows, slopes, weights):
-    steps, width, whole, part, up, down, _ = expert_layout(weights)
-    total = steps * width
-    return pl.pallas_call(
-        expert_back_kernel,
-        grid=(steps,),
-        in_specs=[whole, part, up, down],
-        out_specs=[whole, part],
-        out_shape=[
-            jax.ShapeDtypeStruct((ROWS, D), BF16),
-            jax.ShapeDtypeStruct((ROWS, total), BF16),
-        ],
-        scratch_shapes=[pltpu.VMEM((ROWS, D), F32)],
-        compiler_params=pltpu.CompilerParams(vmem_limit_bytes=56 << 20),
-        cost_estimate=expert_cost(2, total),
-    )(grad_rows, slopes, weights, weights)
-
-
-def expert_weight_grads(rows, grad_rows, hidden, grad_pre, weights):
-    steps, width, whole, part, _, _, both = expert_layout(weights)
-    total = steps * width
+        in_specs=[whole, whole, pl.BlockSpec((1, CAP), lambda step: (0, 0)), up, down],
+        out_specs=[whole, whole, whole, part, part],
+        out_shape=[jax.ShapeDtypeStruct((CAP, D), BF16)] * 3
+        + [jax.ShapeDtypeStruct((CAP, total), BF16)] * 2,
+        scratch_shapes=[pltpu.VMEM((CAP, D), F32)] * 2,
+        compiler_params=pltpu.CompilerParams(vmem_limit_bytes=48 << 20),
+        cost_estimate=pl.CostEstimate(
+            flops=8 * CAP * D * total, bytes_accessed=20 << 20, transcendentals=CAP * total
+        ),
+    )(rows, upstream, gate, weights, weights)
+
+
+def expert_weight_grads(rows, grads, hiddens, grad_pres, weights):
+    steps, total, whole, part, _, _, both = expert_layout(weights)
     return pl.pallas_call(
         expert_weight_kernel,
         grid=(steps,),
-        in_specs=[whole, whole, part, part],
+        in_specs=[whole] * (2 * EXPERTS) + [part] * (2 * EXPERTS),
         out_specs=both,
         out_shape=jax.ShapeDtypeStruct(weights.shape, BF16),
         compiler_params=pltpu.CompilerParams(vmem_limit_bytes=56 << 20),
-        cost_estimate=expert_cost(2, total),
-    )(rows, grad_rows, hidden, grad_pre)
+        cost_estimate=pl.CostEstimate(
+            flops=4 * ROWS * D * total, bytes_accessed=40 << 20, transcendentals=0
+        ),
+    )(*rows, *grads, *hiddens, *grad_pres)
 
 
 def swap_rows(pieces, size):
@@ -506,13 +648,10 @@
         [router, gain_attn[:, None], gain_ffn[:, None], jnp.zeros((owned, 128 - EXPERTS - 2), BF16)],
         axis=1,
     )
-    dense = lax.all_gather(
-        jnp.concatenate([w_qkv, w_out, narrow], axis=1), AXIS, axis=0, tiled=True
-    )
-    qkv_w, out_w = dense[:, : 3 * D], dense[:, 3 * D : 4 * D]
-    router_w = dense[:, 4 * D : 4 * D + EXPERTS]
-    gain_first = dense[:, 4 * D + EXPERTS].astype(F32)
-    gain_second = dense[:, 4 * D + EXPERTS + 1].astype(F32)
+    owned_dense = jnp.concatenate([w_qkv, w_out, narrow], axis=1)
+    z_dense = [along_z(owned_dense, size, -shift) for shift in range(1, depth)]
+    hand_on = destinations(size, owned)
+    turned_tokens = jnp.dot(tokens, hand_on, preferred_element_type=F32)
 
     def weights_for(flip):
         return jnp.stack(
@@ -522,7 +661,34 @@
             ]
         )
 
-    mine = jnp.stack(swap_rows([weights_for(flip) for flip in range(EXPERTS)], size), axis=1)
+    arrived_weights = swap_rows([weights_for(flip) for flip in range(EXPERTS)], size)
+    ends = jnp.cumsum(lengths[0])
+    places = lax.iota(jnp.int32, TOK_DEV)
+    doc_ids = jnp.sum((places[:, None] >= ends[None, :]).astype(jnp.int32), axis=1)
+    spread = lax.iota(jnp.int32, TILE)
+    offsets = (
+        TILE * jnp.arange(-1, 2)[:, None, None] + spread[None, :, None] - spread[None, None, :]
+    )
+    buckets = bucket_of(offsets)
+    extra_q, extra_k = score_extras(table, doc_ids)
+
+    route = routes[:, 0]
+    chosen = (route[:, None] == lax.iota(jnp.int32, EXPERTS)[None, :]).astype(jnp.int32)
+    rank = jnp.sum((jnp.cumsum(chosen, axis=0) - chosen) * chosen, axis=1)
+    slot = (route ^ quad) * CAP + rank
+    slot_row, slot_column = slot[None, :], slot[:, None]
+    route_hot = chosen.astype(F32)
+
+    tokens_f = tokens.astype(F32)
+    (
+        z_dense, arrived_weights, slot_row, buckets, extra_q, extra_k, turned_tokens, hand_on
+    ) = lax.optimization_barrier(
+        (
+            z_dense, arrived_weights, slot_row, buckets, extra_q, extra_k, turned_tokens,
+            hand_on,
+        )
+    )
+    mine = jnp.stack(arrived_weights, axis=1)
     weights = lax.all_gather(
         mine.reshape(1, 2, EXPERTS * units, D),
         AXIS,
@@ -530,59 +696,86 @@
         tiled=True,
         axis_index_groups=same_expert,
     )
-
-    ends = jnp.cumsum(lengths[0])
-    places = lax.iota(jnp.int32, TOK_DEV)
-    doc_ids = jnp.sum((places[:, None] >= ends[None, :]).astype(jnp.int32), axis=1)
-    spread = lax.iota(jnp.int32, TILE)
-    offsets = (
-        TILE * jnp.arange(-1, 2)[:, None, None] + spread[None, :, None] - spread[None, None, :]
-    )
-    buckets = bucket_of(offsets)
-    near = jnp.zeros((HEADS, 3, TILE, TILE), F32)
-    for bucket in range(BUCKETS):
-        near = jnp.where(
-            (buckets == bucket)[None], table[bucket].astype(F32)[:, None, None, None], near
-        )
-    extra_q, extra_k = score_extras(table, doc_ids)
-
-    route = routes[:, 0]
-    chosen = (route[:, None] == lax.iota(jnp.int32, EXPERTS)[None, :]).astype(jnp.int32)
-    rank = jnp.sum((jnp.cumsum(chosen, axis=0) - chosen) * chosen, axis=1)
-    slot = (route ^ quad) * CAP + rank
-    route_hot = chosen.astype(F32)
-
-    def dispatch(values):
-        return jnp.zeros((ROWS, D), BF16).at[slot].set(values).reshape(EXPERTS, CAP, D)
-
-    tokens_f = tokens.astype(F32)
-    normed = rms_norm(tokens_f, gain_first).astype(BF16)
-    qkv = jnp.dot(normed, qkv_w, preferred_element_type=F32).astype(BF16)
-    late_cotangent, qkv = lax.optimization_barrier((cotangent, qkv))
-    upstream_rows = jnp.concatenate(swap_rows(dispatch(late_cotangent), size))
+    quad_dense = jnp.concatenate([owned_dense] + z_dense)
+    arrived_dense = [along_quad(quad_dense, size, flip) for flip in range(1, 4)]
+    (upstream_rows, near), arrived_dense = lax.optimization_barrier(
+        (early(slot_row, cotangent, buckets, table.astype(F32)), arrived_dense)
+    )
+    core_dense = jnp.concatenate([quad_dense] + arrived_dense)
+    dense = jnp.concatenate([core_dense, along_core(core_dense, size)])
+    turned_gain = dense[:, 4 * D + EXPERTS].astype(F32)
+    turned_normed = rms_norm(turned_tokens, turned_gain).astype(BF16)
+    qkv = jnp.dot(turned_normed, dense[:, : 3 * D], preferred_element_type=F32).astype(BF16)
+    upstream_rows, qkv = lax.optimization_barrier((upstream_rows, qkv))
+    upstream_rows = swap_rows(upstream_rows, size)
+    side = jnp.dot(hand_on, dense[:, 3 * D :], preferred_element_type=F32).astype(BF16)
+    side, qkv = lax.optimization_barrier((side, qkv))
+    out_w = side[:, :D]
+    router_w = side[:, D : D + EXPERTS]
+    gain_first = side[:, D + EXPERTS].astype(F32)
+    gain_second = side[:, D + EXPERTS + 1].astype(F32)
     mixed, logs = attend(qkv, extra_q, extra_k, near)
+    mixed, upstream_rows = lax.optimization_barrier((mixed, upstream_rows))
     attended = tokens_f + jnp.dot(mixed, out_w, preferred_element_type=F32)
     normed_ffn = rms_norm(attended, gain_second).astype(BF16)
-    rows = jnp.concatenate(swap_rows(dispatch(normed_ffn), size))
     logits = jnp.dot(normed_ffn, router_w, preferred_element_type=F32)
     probs_route = jax.nn.softmax(logits, axis=-1)
     gate = jnp.sum(probs_route * route_hot, axis=1, keepdims=True)
-    gate_slots = jnp.sum(
-        jnp.where(slot[None, :] == lax.iota(jnp.int32, ROWS)[:, None], gate[:, 0][None, :], 0.0),
-        axis=1,
-    ).reshape(EXPERTS, CAP)
-    gate_rows = jnp.concatenate(swap_rows(gate_slots, size))
-    grad_rows = (gate_rows[:, None] * upstream_rows.astype(F32)).astype(BF16)
-
-    expert_rows, hidden, slopes = expert_forward(rows, weights)
-    expert_tok = jnp.concatenate(swap_rows(expert_rows.reshape(EXPERTS, CAP, D), size))[
-        slot
-    ].astype(F32)
-    back_rows, grad_pre = expert_backward(grad_rows, slopes, weights)
-    back_tok = jnp.concatenate(swap_rows(back_rows.reshape(EXPERTS, CAP, D), size))[slot].astype(
-        F32
-    )
-    expert_grads = expert_weight_grads(rows, grad_rows, hidden, grad_pre, weights)
+    rows, gates = dispatch(slot_row, normed_ffn, gate.reshape(1, TOK_DEV))
+    rows[0], late_mixed, late_dense = lax.optimization_barrier((rows[0], mixed, dense))
+    gates = swap_rows(gates, size)
+    rows[1], rows[2] = along_quad(rows[1], size, 1), along_quad(rows[2], size, 2)
+    turned_mixed = jnp.dot(late_mixed, hand_on, preferred_element_type=F32).astype(BF16)
+    qkv_parts = [
+        jnp.dot(
+            hand_on,
+            jnp.concatenate(
+                [
+                    late_dense[:, which * D + part * PART : which * D + (part + 1) * PART]
+                    for which in range(3)
+                ],
+                axis=1,
+            ),
+            preferred_element_type=F32,
+        ).astype(BF16)
+        for part in range(PARTS)
+    ]
+    rows[1], rows[3], gates, turned_mixed, qkv_parts = lax.optimization_barrier(
+        (rows[1], rows[3], gates, turned_mixed, qkv_parts)
+    )
+    rows[3] = along_quad(rows[3], size, 3)
+
+    def run(flip, rows_in):
+        return list(expert_pass(rows_in, upstream_rows[flip], gates[flip], weights))
+
+    def out_of(flip, which):
+        return along_quad(passes[flip][which], size, flip)
+
+    passes = {}
+    passes[1] = run(1, rows[1])
+    rows_2, passes[1][2] = lax.optimization_barrier((rows[2], passes[1][2]))
+    out_1 = out_of(1, 0)
+    passes[2] = run(2, rows_2)
+    passes[2][2], out_1 = lax.optimization_barrier((passes[2][2], out_1))
+    rows_3, passes[2][2] = lax.optimization_barrier((rows[3], passes[2][2]))
+    back_1, out_2 = out_of(1, 1), out_of(2, 0)
+    passes[3] = run(3, rows_3)
+    passes[3][2], back_1, out_2 = lax.optimization_barrier((passes[3][2], back_1, out_2))
+    rows_0, passes[3][2] = lax.optimization_barrier((rows[0], passes[3][2]))
+    back_2 = out_of(2, 1)
+    passes[0] = run(0, rows_0)
+    passes[0][2], back_2 = lax.optimization_barrier((passes[0][2], back_2))
+    out_3, back_3 = out_of(3, 0), out_of(3, 1)
+    order = [passes[flip] for flip in range(EXPERTS)]
+    expert_grads = expert_weight_grads(
+        rows, *([member[which] for member in order] for which in (2, 3, 4)), weights
+    )
+    expert_grads, out_3, back_3 = lax.optimization_barrier((expert_grads, out_3, back_3))
+    expert_tok, back_tok = combine(
+        slot_column,
+        (passes[0][0], out_1, out_2, out_3),
+        (passes[0][1], back_1, back_2, back_3),
+    )
     expert_sums = lax.psum_scatter(
         expert_grads, AXIS, scatter_dimension=0, tiled=True, axis_index_groups=same_expert
     ).reshape(2, EXPERTS, units, D)
@@ -601,41 +794,86 @@
     grad_mixed = jnp.einsum(
         "tf,df->td", grad_attn_out, out_w, preferred_element_type=F32
     ).astype(BF16)
-    grad_w_out = jnp.einsum("td,tf->df", mixed, grad_attn_out, preferred_element_type=F32)
     grad_router = jnp.einsum("td,te->de", normed_ffn, grad_logits, preferred_element_type=F32)
-    first_sums = scatter_sums(
-        jnp.concatenate(
-            [
-                grad_w_out,
-                grad_router,
-                grad_gain_second[:, None],
-                jnp.zeros((D, 128 - EXPERTS - 1), F32),
-            ],
-            axis=1,
-        ),
-        size,
-    )
-
-    grad_q, grad_k, grad_v, grad_table = attend_back(
-        qkv, grad_mixed, logs, extra_q, extra_k, near, buckets
-    )
-    table_sum = sum_everywhere(
-        jnp.sum(grad_table, axis=-1).reshape(HEADS, BUCKETS).T, size
-    )
-    grad_qkv = jnp.concatenate([grad_q, grad_k, grad_v], axis=1)
-    grad_w_qkv = jnp.einsum("td,tf->df", normed, grad_qkv, preferred_element_type=F32)
-    grad_normed = jnp.einsum("tf,df->td", grad_qkv, qkv_w, preferred_element_type=F32)
-    unused_first, first_pull = jax.vjp(rms_norm, tokens_f, gain_first)
-    grad_tok_norm, grad_gain_first = first_pull(grad_normed)
-    grad_tokens = (grad_res + grad_tok_norm).astype(BF16)
-    last_sums = scatter_sums(
-        jnp.concatenate([grad_w_qkv, grad_gain_first[:, None], jnp.zeros((D, 127), F32)], axis=1),
-        size,
-    )
-
-    by_flip = jnp.stack(
-        swap_rows([expert_sums[:, flip] for flip in range(EXPERTS)], size), axis=2
-    ).astype(F32)
+
+    narrow = jnp.concatenate(
+        [grad_router, grad_gain_second[:, None], jnp.zeros((D, 128 - EXPERTS - 1), F32)], axis=1
+    ).astype(BF16)
+    narrow = lax.dot_general(hand_on, narrow, TN, preferred_element_type=F32)
+    narrow_mine, narrow_other = narrow[: D // 2], narrow[D // 2 :].astype(BF16)
+    out_mine, out_other = weight_halves(turned_mixed, grad_attn_out[None])
+
+    def attend_part(part, logs):
+        return attend_back(part, qkv, grad_mixed, logs, extra_q, extra_k, near, buckets)
+
+    grads_0, table_0 = attend_part(0, logs)
+    mine, other = weight_halves(turned_normed, grads_0)
+    other = jnp.concatenate([out_other, narrow_other, other], axis=1)
+    mine = jnp.concatenate([out_mine, narrow_mine, mine], axis=1)
+    logs, other, mine = lax.optimization_barrier((logs, other, mine))
+    arrived = along_core(other, size)
+    (grads_1, table_1), arrived = lax.optimization_barrier((attend_part(1, logs), arrived))
+    low, view = for_quad(mine + arrived.astype(F32))
+    mine_1, other_1 = weight_halves(turned_normed, grads_1)
+    logs, low, view, other_1, mine_1 = lax.optimization_barrier(
+        (logs, low, view, other_1, mine_1)
+    )
+    arrived_1 = along_core(other_1, size)
+    arrived = [along_quad(low[flip - 1], size, flip) for flip in range(1, 4)]
+    (grads_2, table_2), arrived, arrived_1, expert_sums = lax.optimization_barrier(
+        (attend_part(2, logs), arrived, arrived_1, expert_sums)
+    )
+    mine_2, other_2 = weight_halves(turned_normed, grads_2)
+    table_grad = jnp.concatenate(
+        [
+            jnp.sum(part, axis=-1).reshape(HEADS // PARTS, BUCKETS)
+            for part in (table_0, table_1, table_2)
+        ]
+    ).reshape(-1, 128)
+    other_2, mine_2, table_grad, expert_sums = lax.optimization_barrier(
+        (other_2, mine_2, table_grad, expert_sums)
+    )
+    by_flip = swap_rows([expert_sums[:, flip] for flip in range(EXPERTS)], size)
+
+    arrived_2 = along_core(other_2, size)
+    table_grad = table_grad + along_core(table_grad, size)
+    total = view[0] + sum(piece.astype(F32) for piece in arrived)
+    late_1 = mine_1 + arrived_1.astype(F32)
+    arrived_2, table_grad, total, late_1 = lax.optimization_barrier(
+        (arrived_2, table_grad, total, late_1)
+    )
+    low, view = for_quad(
+        jnp.concatenate([late_1, mine_2 + arrived_2.astype(F32)], axis=1)
+    )
+    low, view, late_grads = lax.optimization_barrier((low, view, [grads_0, grads_1, grads_2]))
+    arrived = [along_quad(low[flip - 1], size, flip) for flip in range(1, 4)]
+    tables = [table_grad] + [along_quad(table_grad, size, flip) for flip in range(1, 4)]
+    grad_tokens = token_grad(late_grads, qkv_parts, tokens, gain_first[None], grad_res)
+    arrived, tables, grad_tokens, by_flip = lax.optimization_barrier(
+        (arrived, tables, grad_tokens, by_flip)
+    )
+    table_grad = sum_all(tables)
+    total = jnp.concatenate(
+        [total, view[0] + sum(piece.astype(F32) for piece in arrived)], axis=1
+    )
+    sums = add_z(total, size)
+    table_sum = sum_all(
+        [table_grad] + [along_z_flip(table_grad, size, flip) for flip in range(1, depth)]
+    )
+    table_sum = table_sum.reshape(HEADS, BUCKETS).T
+    out_sum = sums[:, :D]
+    router_sum = sums[:, D : D + EXPERTS]
+    gain_second_sum = sums[:, D + EXPERTS]
+    qkv_sum = (
+        sums[:, D + 128 :]
+        .reshape(owned, PARTS, 3, PART)
+        .transpose(0, 2, 1, 3)
+        .reshape(owned, 3 * D)
+    )
+
+    gain_first_sum = jnp.sum(w_qkv.astype(F32) * qkv_sum, axis=1) / gain_attn.astype(F32)
+
+    by_flip = jnp.stack(by_flip, axis=2).astype(F32)
     by_expert = jnp.concatenate(
         [lax.dynamic_slice_in_dim(by_flip, quad ^ expert, 1, 2) for expert in range(EXPERTS)],
         axis=2,
@@ -643,12 +881,12 @@
     return (
         output,
         grad_tokens,
-        last_sums[:, 3 * D],
-        last_sums[:, : 3 * D],
-        first_sums[:, :D],
+        gain_first_sum,
+        qkv_sum,
+        out_sum,
         table_sum,
-        first_sums[:, D + EXPERTS],
-        first_sums[:, D : D + EXPERTS],
+        gain_second_sum,
+        router_sum,
         by_expert[0],
         by_expert[1],
     )

time: 552 us -> 452 us (0.82)
  waiting for transfers between devices: 133 us -> 52.6 us
  Pallas kernels: 178 us -> 210 us
  other arithmetic: 59.8 us -> 32.3 us
  local copies, waits for them, and re-layouts: 69.5 us -> 46.1 us
  matrix products: 43.2 us -> 30.4 us
  starting transfers between devices: 48.9 us -> 55.9 us
    ppermute x27 -> x33, waiting for transfers between devices: 105 us -> 37.5 us  [along_quad(): return lax.ppermute(value, AXIS, [(i, i ^ flip << 1) for i in range(size)])]
    pallas_call x4 -> x16, Pallas kernels: 151 us -> 182 us  [the longest x4 64.4 us: expert_pass(): pl.pallas_call(expert_kernel, grid=(steps,), in_specs=[whole, whole, pl.B...]
    all_gather x1 -> x0, waiting for transfers between devices: 20.9 us -> none  [body(): lax.all_gather(jnp.concatenate([w_qkv, w_out, narrow], axis=1), AXIS, axi...]
    unnamed x82 -> x157, local copies, waits for them, and re-layouts: 10.7 us -> 30 us
    convert_element_type x10 -> x6, other arithmetic: 16.2 us -> 1.65 us  [the longest x1 0.42 us: destinations(): return (place[:, None] == source[None, :]).astype(BF16)]
    concatenate x9 -> x4, local copies, waits for them, and re-layouts: 13.3 us -> 1.55 us  [the longest x1 0.99 us: body(): owned_dense = jnp.concatenate([w_qkv, w_out, narrow], axis=1)]
    select_n x2 -> x0, other arithmetic: 10.9 us -> none  [the longest x1 10.9 us: body(): jnp.where((buckets == bucket)[None], table[bucket].astype(F32)[:, None, N...]
    gather x2 -> x0, local copies, waits for them, and re-layouts: 10.6 us -> none  [the longest x1 5.4 us: body(): jnp.concatenate(swap_rows(back_rows.reshape(EXPERTS, CAP, D), size))[slot]]
  transfers between devices with their start and end apart: 43 -> 49, of which waited for: 26 -> 14; matrix products, arithmetic and copies ran while one was open for 28% -> 18% of each run, Pallas kernels for 25% -> 47%
where the time goes in v2:
time: 452 us; the launch traced here: 443 us
  Pallas kernels  210 us (46%)
  starting transfers between devices  55.9 us (12%)
  waiting for transfers between devices  52.6 us (12%)
  local copies, waits for them, and re-layouts  46.1 us (10%)
  other arithmetic  32.3 us (7%)
  matrix products  30.4 us (7%)
  between operations  15.5 us (3%)
    pallas_call x4, Pallas kernels, expert_pass(): pl.pallas_call(expert_kernel, grid=(steps,), in_specs=[whole, whole, pl.B...  64.4 us
    pallas_call x3, Pallas kernels, attend_back(): pl.pallas_call(attend_back_kernel, grid=(PART_PAIRS,), in_specs=[column(f...  52.4 us
    ppermute x33, starting transfers between devices, along_quad(): return lax.ppermute(value, AXIS, [(i, i ^ flip << 1) for i in range(size)])  39.6 us
    ppermute x33, waiting for transfers between devices, along_quad(): return lax.ppermute(value, AXIS, [(i, i ^ flip << 1) for i in range(size)])  37.5 us
    unnamed x157, local copies, waits for them, and re-layouts  30 us
    pallas_call x1, Pallas kernels, attend(): pl.pallas_call(attend_kernel, grid=(PAIRS,), in_specs=[column(0), column(...  27.9 us
    pallas_call x1, Pallas kernels, expert_weight_grads(): pl.pallas_call(expert_weight_kernel, grid=(steps,), in_specs=[whole] * (2...  27.4 us
    pallas_call x1, Pallas kernels, combine(): pl.pallas_call(combine_kernel, grid=(TOK_DEV // rows,), in_specs=[pl.Bloc...  11.3 us
  transfers between devices with their start and end apart: 49, of which 14 were waited for; matrix products, arithmetic and copies ran while one was open for 18% of the time, Pallas kernels for 47%

profile of v2, /device:TPU:0, one launch (start us, length us, event | category | flops | bytes accessed | tf_op | source)
XLA Modules:
  0.0 443.1 jit_solution(6684258414040999377)
XLA Ops:
  16.2 5.2 %constant_dynamic-slice_fusion.4 = (bf16[96,1,768]{2,1,0:T(2,128)(2,1)S(1)}, bf16[96,1,768]{2,1,0:T(2,128)(2,1)S(1)}, bf16[96,1,768]{2,1,0:T(2,128)(2,1)S(1)}, b...) fusion(bf16[96,4,768]{2,1,0:T(4,128)(2,1)} %param.23, ...), kind=kLoop, calls=%fused_computation.229 | loop fusion | bytes 2359312 | tf_op jit(solution)/shard_map/jit(dynamic_index_in_dim)/dynamic_slice | solution.py:660
  46.5 3.6 collective-permute-done
  59.9 7.5 %shard_map.195 = (bf16[512,768]{1,0:T(8,128)(2,1)S(1)}, bf16[512,768]{1,0:T(8,128)(2,1)S(1)}, bf16[512,768]{1,0:T(8,128)(2,1)S(1)}, bf16[512,768]{1,0:T(8,128)(2,1)S(1)}, f32[12,3,128,128]{3,2,1,0:T(8,128)S(1)}) custom-call(s32[1,1024]{1,0:T(1,128)S(1)} %add.286.slot_ref, bf16[1024,768]{1,0:T(8,128)(2,1)S(1)} %copy-done, ...), custom_call_target="tpu_custom_call" | custom-call | flops 12884901888 | bytes 6291456 | tf_op jit(solution)/shard_map/pallas_call | solution.py:504
  72.4 9.4 %collective-permute-done.7 = bf16[96,3200]{1,0:T(8,128)(2,1)S(1)} collective-permute-done((bf16[96,3200]{1,0:T(8,128)(2,1)S(1)}, bf16[96,3200]{1,0:T(8,128)(2,1)S(1)}, u32[]{:S(2)}, u32[]{:S(2)}) %collective-permute-start.7) | collective-permute-done | bytes 614432 | tf_op jit(solution)/shard_map/ppermute | solution.py:59
  88.1 4.0 convolution_convert_fusion.q_ref.k_ref.v_ref
  98.1 27.9 %shard_map.196 = (bf16[1024,768]{1,0:T(8,128)(2,1)S(1)}, f32[6,2,1024]{2,1,0:T(2,128)S(1)}) custom-call(bf16[1024,2304]{1,0:T(8,128)(2,1)S(1)} %convolution_convert_fusion.q_ref.k_ref.v_ref, bf16[1024,2304]{1,0:T(8,128)(2,1)S(1)} %convolution_convert_fusion.q_ref.k_ref.v_ref, bf16[1024,2304]{1,0:T(8,128)(2,1)S(1)} %convolution_convert_fusion.q_ref.k_ref.v_ref, ...), custom_call_target="tpu_custom_call" | custom-call | flops 40000000000 | bytes 12582912 | tf_op jit(solution)/shard_map/pallas_call | solution.py:260
  126.3 5.9 %collective-permute-done.11.upstream_ref = bf16[512,768]{1,0:T(8,128)(2,1)S(1)} collective-permute-done((bf16[512,768]{1,0:T(8,128)(2,1)S(1)}, bf16[512,768]{1,0:T(8,128)(2,1)S(1)}, u32[]{:S(2)}, u32[]{:S(2)}) %collective-permute-start.11) | collective-permute-done | bytes 786464 | tf_op jit(solution)/shard_map/ppermute | solution.py:59
  139.0 4.7 %shard_map.197 = (bf16[512,768]{1,0:T(8,128)(2,1)S(1)}, bf16[512,768]{1,0:T(8,128)(2,1)S(1)}, bf16[512,768]{1,0:T(8,128)(2,1)}, bf16[512,768]{1,0:T(8,128)(2,1)}...) custom-call(s32[1,1024]{1,0:T(1,128)S(1)} %add.286.slot_ref, ...), custom_call_target="tpu_custom_call" | custom-call | flops 3221225472 | bytes 6291456 | tf_op jit(solution)/shard_map/pallas_call | solution.py:531
  158.5 6.1 %collective-permute-done.13.rows_ref.refs_1_ = bf16[512,768]{1,0:T(8,128)(2,1)S(1)} collective-permute-done((bf16[512,768]{1,0:T(8,128)(2,1)S(1)}, bf16[512,768]{1,0:T(8,128)(2,1)S(1)}, u32[]{:S(2)}, u32[]{:S(2)}) %collective-permute-start.13) | collective-permute-done | bytes 786464 | tf_op jit(solution)/shard_map/ppermute | solution.py:59
  169.4 16.1 %shard_map.198 = (bf16[512,768]{1,0:T(8,128)(2,1)S(1)}, bf16[512,768]{1,0:T(8,128)(2,1)S(1)}, bf16[512,768]{1,0:T(8,128)(2,1)S(1)}, bf16[512,3072]{1,0:T(8,128)(2,1)}, bf16[512,3072]{1,0:T(8,128)(2,1)}) custom-call(bf16[512,768]{1,0:T(8,128)(2,1)S(1)} %copy-done.22, bf16[512,768]{1,0:T(8,128)(2,1)S(1)} %copy-done.24, ...), custom_call_target="tpu_custom_call" | custom-call | flops 9663676416 | bytes 20971520 | tf_op jit(solution)/shard_map/pallas_call | solution.py:590
  187.5 15.9 %shard_map.199 = (bf16[512,768]{1,0:T(8,128)(2,1)S(1)}, bf16[512,768]{1,0:T(8,128)(2,1)S(1)}, bf16[512,768]{1,0:T(8,128)(2,1)S(1)}, bf16[512,3072]{1,0:T(8,128)(2,1)}, bf16[512,3072]{1,0:T(8,128)(2,1)}) custom-call(bf16[512,768]{1,0:T(8,128)(2,1)} %collective-permute-done.18.rows_ref.refs_2_, bf16[512,768]{1,0:T(8,128)(2,1)S(1)} %copy-done.20, ...), custom_call_target="tpu_custom_call" | custom-call | flops 9663676416 | bytes 20971520 | tf_op jit(solution)/shard_map/pallas_call | solution.py:590
  207.2 16.5 %shard_map.200 = (bf16[512,768]{1,0:T(8,128)(2,1)}, bf16[512,768]{1,0:T(8,128)(2,1)}, bf16[512,768]{1,0:T(8,128)(2,1)S(1)}, bf16[512,3072]{1,0:T(8,128)(2,1)}, bf16[512,3072]{1,0:T(8,128)(2,1)}) custom-call(bf16[512,768]{1,0:T(8,128)(2,1)} %collective-permute-done.17.rows_ref.refs_3_, bf16[512,768]{1,0:T(8,128)(2,1)S(1)} %copy-done.18, ...), custom_call_target="tpu_custom_call" | custom-call | flops 9663676416 | bytes 20971520 | tf_op jit(solution)/shard_map/pallas_call | solution.py:590
  224.8 16.0 %shard_map.201 = (bf16[512,768]{1,0:T(8,128)(2,1)S(1)}, bf16[512,768]{1,0:T(8,128)(2,1)S(1)}, bf16[512,768]{1,0:T(8,128)(2,1)S(1)}, bf16[512,3072]{1,0:T(8,128)(2,1)}, bf16[512,3072]{1,0:T(8,128)(2,1)}) custom-call(bf16[512,768]{1,0:T(8,128)(2,1)S(1)} %copy-done.30, bf16[512,768]{1,0:T(8,128)(2,1)S(1)} %copy-done.32, ...), custom_call_target="tpu_custom_call" | custom-call | flops 9663676416 | bytes 20971520 | tf_op jit(solution)/shard_map/pallas_call | solution.py:590
  247.3 27.4 %shard_map.202 = bf16[8,2,384,768]{3,2,1,0:T(8,128)(2,1)} custom-call(bf16[512,768]{1,0:T(8,128)(2,1)} %copy-done.29, bf16[512,768]{1,0:T(8,128)(2,1)} %copy-done.21, bf16[512,768]{1,0:T(8,128)(2,1)} %collective-permute-done.18.rows_ref.refs_2_, bf16[512,768]{1,0:T(8,128)(2,1)} %collective-permute-done.17.rows_ref.refs_3_, bf16[512,768]{1,0:T(8,128)(2,1)} %copy-done.38, ...), custom_call_target="tpu_custom_call" | custom-call | flops 19327352832 | bytes 41943040 | tf_op jit(solution)/shard_map/pallas_call | solution.py:607
  278.0 11.3 %shard_map.203 = (f32[1024,768]{1,0:T(8,128)}, f32[1024,768]{1,0:T(8,128)}) custom-call(s32[1024,1]{1,0:T(8,128)} %get-tuple-element.447.slot_ref, bf16[512,768]{1,0:T(8,128)(2,1)} %copy-done.34, bf16[512,768]{1,0:T(8,128)(2,1)} %copy-done.64, bf16[512,768]{1,0:T(8,128)(2,1)} %copy-done.66, bf16[512,768]{1,0:T(8,128)(2,1)} %collective-permute-done.23.refs_3_, ...), custom_call_target="tpu_custom_call" | custom-call | flops 6442450944 | bytes 12582912 | tf_op jit(solution)/shard_map/pallas_call | solution.py:561
  292.2 4.3 multiply_reduce_fusion
  302.3 17.6 %shard_map.205 = (bf16[3,1024,256]{2,1,0:T(8,128)(2,1)S(1)}, f32[2,2,32,128]{3,2,1,0:T(8,128)S(1)}) custom-call(bf16[1024,2304]{1,0:T(8,128)(2,1)} %copy-done.28, bf16[1024,2304]{1,0:T(8,128)(2,1)} %copy-done.28, bf16[1024,2304]{1,0:T(8,128)(2,1)} %copy-done.28, bf16[1024,768]{1,0:T(8,128)(2,1)S(1)} %convolution_convert_fusion.1.grad_ref, ...), custom_call_target="tpu_custom_call" | custom-call | flops 26666665984 | bytes 8388608 | tf_op jit(solution)/shard_map/pallas_call | solution.py:283
  328.2 17.5 %shard_map.207 = (bf16[3,1024,256]{2,1,0:T(8,128)(2,1)S(1)}, f32[2,2,32,128]{3,2,1,0:T(8,128)S(1)}) custom-call(bf16[1024,2304]{1,0:T(8,128)(2,1)} %copy-done.28, bf16[1024,2304]{1,0:T(8,128)(2,1)} %copy-done.28, bf16[1024,2304]{1,0:T(8,128)(2,1)} %copy-done.28, bf16[1024,768]{1,0:T(8,128)(2,1)S(1)} %copy-done.27, ...), custom_call_target="tpu_custom_call" | custom-call | flops 26666665984 | bytes 8388608 | tf_op jit(solution)/shard_map/pallas_call | solution.py:283
  356.0 17.2 %shard_map.209 = (bf16[3,1024,256]{2,1,0:T(8,128)(2,1)S(1)}, f32[2,2,32,128]{3,2,1,0:T(8,128)S(1)}) custom-call(bf16[1024,2304]{1,0:T(8,128)(2,1)} %copy-done.28, bf16[1024,2304]{1,0:T(8,128)(2,1)} %copy-done.28, bf16[1024,2304]{1,0:T(8,128)(2,1)} %copy-done.28, bf16[1024,768]{1,0:T(8,128)(2,1)S(1)} %copy-done.27, ...), custom_call_target="tpu_custom_call" | custom-call | flops 26666665984 | bytes 8388608 | tf_op jit(solution)/shard_map/pallas_call | solution.py:283
  393.1 4.0 collective-permute-done.39
  400.6 8.2 %shard_map.211 = bf16[1024,768]{1,0:T(8,128)(2,1)} custom-call(bf16[3,1024,256]{2,1,0:T(8,128)(2,1)S(1)} %get-tuple-element.309.right_ref.grads_0, bf16[3,1024,256]{2,1,0:T(8,128)(2,1)} %copy-done.4, bf16[3,1024,256]{2,1,0:T(8,128)(2,1)} %copy-done.5, bf16[768,768]{1,0:T(8,128)(2,1)S(1)} %copy-done.9, bf16[768,768]{1,0:T(8,128)(2,1)S(1)} %copy-done.8, ...), custom_call_target="tpu_custom_call" | custom-call | flops 3623878656 | bytes 14680064 | tf_op jit(solution)/shard_map/pallas_call | solution.py:470
  408.9 4.7 %collective-permute-done.33 = bf16[96,1536]{1,0:T(8,128)(2,1)S(1)} collective-permute-done((bf16[96,1536]{1,0:T(8,128)(2,1)S(1)}, bf16[96,1536]{1,0:T(8,128)(2,1)S(1)}, u32[]{:S(2)}, u32[]{:S(2)}) %collective-permute-start.33) | collective-permute-done | bytes 294944 | tf_op jit(solution)/shard_map/ppermute | solution.py:59
  418.3 3.8 collective-permute-start.43
  427.1 5.8 %collective-permute-done.42 = bf16[24,3200]{1,0:T(8,128)(2,1)S(1)} collective-permute-done((bf16[24,3200]{1,0:T(8,128)(2,1)S(1)}, bf16[24,3200]{1,0:T(8,128)(2,1)S(1)}, u32[]{:S(2)}, u32[]{:S(2)}) %collective-permute-start.42) | collective-permute-done | bytes 153632 | tf_op jit(solution)/shard_map/ppermute | solution.py:53
  (372 shorter events, 166.8 us)
Async XLA Ops:
  7.2 159.9 %all-gather.2.cloned.1.call-start = ((), (), s32[]{:S(2)}) async-start(), calls=%async_computation.1 | async-start | bytes 10616832 | tf_op jit(solution)/shard_map/all_gather | solution.py:692
  10.5 34.4 %collective-permute-start.2 = (bf16[24,3200]{1,0:T(8,128)(2,1)S(1)}, bf16[24,3200]{1,0:T(8,128)(2,1)}, u32[]{:S(2)}, u32[]{:S(2)}) collective-permute-start(bf16[24,3200]{1,0:T(8,128)(2,1)S(1)} %concatenate.57), channel_id=1, source_target_pairs={{0,8},{1,9},{2,10},{3,11},{4,12},{5,13},{6,14},{7,15},{8,16},{9,17... | collective-permute-start | bytes 460808 | tf_op jit(solution)/shard_map/ppermute | solution.py:53
  13.6 33.0 %collective-permute-start.1 = (bf16[24,3200]{1,0:T(8,128)(2,1)S(1)}, bf16[24,3200]{1,0:T(8,128)(2,1)}, u32[]{:S(2)}, u32[]{:S(2)}) collective-permute-start(bf16[24,3200]{1,0:T(8,128)(2,1)S(1)} %concatenate.57), channel_id=1, source_target_pairs={{0,16},{1,17},{2,18},{3,19},{4,20},{5,21},{6,22},{7,23},{8,24},{9,... | collective-permute-start | bytes 460808 | tf_op jit(solution)/shard_map/ppermute | solution.py:53
  22.2 28.0 %collective-permute-start.5 = (bf16[2,96,768]{2,1,0:T(8,128)(2,1)}, bf16[2,96,768]{2,1,0:T(8,128)(2,1)}, u32[]{:S(2)}, u32[]{:S(2)}) collective-permute-start(bf16[2,96,768]{2,1,0:T(8,128)(2,1)} %pad_maximum_fusion.12), channel_id=1, source_target_pairs={{0,6},{1,7},{2,4},{3,5},{4,2},{5,3},{6,0},{7,1},{8,14},{9,15},{10,... | collective-permute-start | bytes 884744 | tf_op jit(solution)/shard_map/ppermute | solution.py:59
  25.5 24.7 %collective-permute-start.4 = (bf16[2,96,768]{2,1,0:T(8,128)(2,1)}, bf16[2,96,768]{2,1,0:T(8,128)(2,1)}, u32[]{:S(2)}, u32[]{:S(2)}) collective-permute-start(bf16[2,96,768]{2,1,0:T(8,128)(2,1)} %pad_maximum_fusion.11), channel_id=1, source_target_pairs={{0,4},{1,5},{2,6},{3,7},{4,0},{5,1},{6,2},{7,3},{8,12},{9,13},{10,... | collective-permute-start | bytes 884744 | tf_op jit(solution)/shard_map/ppermute | solution.py:59
  26.8 23.4 %collective-permute-start.3 = (bf16[2,96,768]{2,1,0:T(8,128)(2,1)}, bf16[2,96,768]{2,1,0:T(8,128)(2,1)}, u32[]{:S(2)}, u32[]{:S(2)}) collective-permute-start(bf16[2,96,768]{2,1,0:T(8,128)(2,1)} %pad_maximum_fusion.10), channel_id=1, source_target_pairs={{0,2},{1,3},{2,0},{3,1},{4,6},{5,7},{6,4},{7,5},{8,10},{9,11},{10,... | collective-permute-start | bytes 884744 | tf_op jit(solution)/shard_map/ppermute | solution.py:59
  53.3 323.9 %reduce-scatter.2.cloned.1.call-start = ((), (), s32[]{:S(2)}) async-start(), calls=%async_computation.2 | async-start | bytes 10616832 | tf_op jit(solution)/shard_map/reduce_scatter | solution.py:779
  57.2 24.7 %collective-permute-start.7 = (bf16[96,3200]{1,0:T(8,128)(2,1)S(1)}, bf16[96,3200]{1,0:T(8,128)(2,1)S(1)}, u32[]{:S(2)}, u32[]{:S(2)}) collective-permute-start(bf16[96,3200]{1,0:T(8,128)(2,1)S(1)} %pad_maximum_fusion.7), channel_id=1, source_target_pairs={{0,4},{1,5},{2,6},{3,7},{4,0},{5,1},{6,2},{7,3},{8,12},{9,13},{10,... | collective-permute-start | bytes 1843208 | tf_op jit(solution)/shard_map/ppermute | solution.py:59
  57.7 24.3 %collective-permute-start.6 = (bf16[96,3200]{1,0:T(8,128)(2,1)S(1)}, bf16[96,3200]{1,0:T(8,128)(2,1)S(1)}, u32[]{:S(2)}, u32[]{:S(2)}) collective-permute-start(bf16[96,3200]{1,0:T(8,128)(2,1)S(1)} %pad_maximum_fusion.7), channel_id=1, source_target_pairs={{0,2},{1,3},{2,0},{3,1},{4,6},{5,7},{6,4},{7,5},{8,10},{9,11},{10,... | collective-permute-start | bytes 1843208 | tf_op jit(solution)/shard_map/ppermute | solution.py:59
  94.6 31.7 %collective-permute-start.10 = (bf16[512,768]{1,0:T(8,128)(2,1)S(1)}, bf16[512,768]{1,0:T(8,128)(2,1)S(1)}, u32[]{:S(2)}, u32[]{:S(2)}) collective-permute-start(bf16[512,768]{1,0:T(8,128)(2,1)S(1)} %get-tuple-element.196), channel_id=1, source_target_pairs={{0,2},{1,3},{2,0},{3,1},{4,6},{5,7},{6,4},{7,5},{8,10},{9,11},{10,... | collective-permute-start | bytes 2359304 | tf_op jit(solution)/shard_map/ppermute | solution.py:59
  96.1 36.2 %collective-permute-start.11 = (bf16[512,768]{1,0:T(8,128)(2,1)S(1)}, bf16[512,768]{1,0:T(8,128)(2,1)S(1)}, u32[]{:S(2)}, u32[]{:S(2)}) collective-permute-start(bf16[512,768]{1,0:T(8,128)(2,1)S(1)} %get-tuple-element.197), channel_id=1, source_target_pairs={{0,4},{1,5},{2,6},{3,7},{4,0},{5,1},{6,2},{7,3},{8,12},{9,13},{10,... | collective-permute-start | bytes 2359304 | tf_op jit(solution)/shard_map/ppermute | solution.py:59
  96.8 35.4 %collective-permute-start.12 = (bf16[512,768]{1,0:T(8,128)(2,1)S(1)}, bf16[512,768]{1,0:T(8,128)(2,1)S(1)}, u32[]{:S(2)}, u32[]{:S(2)}) collective-permute-start(bf16[512,768]{1,0:T(8,128)(2,1)S(1)} %get-tuple-element.198), channel_id=1, source_target_pairs={{0,6},{1,7},{2,4},{3,5},{4,2},{5,3},{6,0},{7,1},{8,14},{9,15},{10,... | collective-permute-start | bytes 2359304 | tf_op jit(solution)/shard_map/ppermute | solution.py:59
  147.4 38.0 %collective-permute-start.18 = (bf16[512,768]{1,0:T(8,128)(2,1)}, bf16[512,768]{1,0:T(8,128)(2,1)}, u32[]{:S(2)}, u32[]{:S(2)}) collective-permute-start(bf16[512,768]{1,0:T(8,128)(2,1)} %get-tuple-element.212), channel_id=1, source_target_pairs={{0,4},{1,5},{2,6},{3,7},{4,0},{5,1},{6,2},{7,3},{8,12},{9,13},{10,... | collective-permute-start | bytes 2359304 | tf_op jit(solution)/shard_map/ppermute | solution.py:59
  165.5 41.7 %collective-permute-start.17 = (bf16[512,768]{1,0:T(8,128)(2,1)}, bf16[512,768]{1,0:T(8,128)(2,1)}, u32[]{:S(2)}, u32[]{:S(2)}) collective-permute-start(bf16[512,768]{1,0:T(8,128)(2,1)} %get-tuple-element.211), channel_id=1, source_target_pairs={{0,6},{1,7},{2,4},{3,5},{4,2},{5,3},{6,0},{7,1},{8,14},{9,15},{10,... | collective-permute-start | bytes 2359304 | tf_op jit(solution)/shard_map/ppermute | solution.py:59
  185.4 20.9 %collective-permute-start.19 = (bf16[512,768]{1,0:T(8,128)(2,1)S(1)}, bf16[512,768]{1,0:T(8,128)(2,1)S(1)}, u32[]{:S(2)}, u32[]{:S(2)}) collective-permute-start(bf16[512,768]{1,0:T(8,128)(2,1)S(1)} %get-tuple-element.225), channel_id=1, source_target_pairs={{0,2},{1,3},{2,0},{3,1},{4,6},{5,7},{6,4},{7,5},{8,10},{9,11},{10,... | collective-permute-start | bytes 2359304 | tf_op jit(solution)/shard_map/ppermute | solution.py:59
  186.0 38.5 %collective-permute-start.20 = (bf16[512,768]{1,0:T(8,128)(2,1)S(1)}, bf16[512,768]{1,0:T(8,128)(2,1)S(1)}, u32[]{:S(2)}, u32[]{:S(2)}) collective-permute-start(bf16[512,768]{1,0:T(8,128)(2,1)S(1)} %get-tuple-element.231), channel_id=1, source_target_pairs={{0,2},{1,3},{2,0},{3,1},{4,6},{5,7},{6,4},{7,5},{8,10},{9,11},{10,... | collective-permute-start | bytes 2359304 | tf_op jit(solution)/shard_map/ppermute | solution.py:59
  204.3 20.5 %collective-permute-start.21 = (bf16[512,768]{1,0:T(8,128)(2,1)S(1)}, bf16[512,768]{1,0:T(8,128)(2,1)S(1)}, u32[]{:S(2)}, u32[]{:S(2)}) collective-permute-start(bf16[512,768]{1,0:T(8,128)(2,1)S(1)} %get-tuple-element.232), channel_id=1, source_target_pairs={{0,4},{1,5},{2,6},{3,7},{4,0},{5,1},{6,2},{7,3},{8,12},{9,13},{10,... | collective-permute-start | bytes 2359304 | tf_op jit(solution)/shard_map/ppermute | solution.py:59
  205.0 38.5 %collective-permute-start.22 = (bf16[512,768]{1,0:T(8,128)(2,1)S(1)}, bf16[512,768]{1,0:T(8,128)(2,1)S(1)}, u32[]{:S(2)}, u32[]{:S(2)}) collective-permute-start(bf16[512,768]{1,0:T(8,128)(2,1)S(1)} %get-tuple-element.241), channel_id=1, source_target_pairs={{0,4},{1,5},{2,6},{3,7},{4,0},{5,1},{6,2},{7,3},{8,12},{9,13},{10,... | collective-permute-start | bytes 2359304 | tf_op jit(solution)/shard_map/ppermute | solution.py:59
  244.4 30.3 %collective-permute-start.23 = (bf16[512,768]{1,0:T(8,128)(2,1)}, bf16[512,768]{1,0:T(8,128)(2,1)}, u32[]{:S(2)}, u32[]{:S(2)}) collective-permute-start(bf16[512,768]{1,0:T(8,128)(2,1)} %get-tuple-element.254), channel_id=1, source_target_pairs={{0,6},{1,7},{2,4},{3,5},{4,2},{5,3},{6,0},{7,1},{8,14},{9,15},{10,... | collective-permute-start | bytes 2359304 | tf_op jit(solution)/shard_map/ppermute | solution.py:59
  245.7 32.1 %collective-permute-start.24 = (bf16[512,768]{1,0:T(8,128)(2,1)}, bf16[512,768]{1,0:T(8,128)(2,1)}, u32[]{:S(2)}, u32[]{:S(2)}) collective-permute-start(bf16[512,768]{1,0:T(8,128)(2,1)} %get-tuple-element.255), channel_id=1, source_target_pairs={{0,6},{1,7},{2,4},{3,5},{4,2},{5,3},{6,0},{7,1},{8,14},{9,15},{10,... | collective-permute-start | bytes 2359304 | tf_op jit(solution)/shard_map/ppermute | solution.py:59
  325.7 20.1 %collective-permute-start.25 = (bf16[384,1664]{1,0:T(8,128)(2,1)}, bf16[384,1664]{1,0:T(8,128)(2,1)}, u32[]{:S(2)}, u32[]{:S(2)}) collective-permute-start(bf16[384,1664]{1,0:T(8,128)(2,1)} %pad_maximum_fusion.5), channel_id=1, source_target_pairs={{0,1},{1,0},{2,3},{3,2},{4,5},{5,4},{6,7},{7,6},{8,9},{9,8},{10,11... | collective-permute-start | bytes 3833864 | tf_op jit(solution)/shard_map/ppermute | solution.py:63
  352.5 22.0 %collective-permute-start.26 = (bf16[96,1664]{1,0:T(8,128)(2,1)}, bf16[96,1664]{1,0:T(8,128)(2,1)}, u32[]{:S(2)}, u32[]{:S(2)}) collective-permute-start(bf16[96,1664]{1,0:T(8,128)(2,1)} %get-tuple-element.282), channel_id=1, source_target_pairs={{0,2},{1,3},{2,0},{3,1},{4,6},{5,7},{6,4},{7,5},{8,10},{9,11},{10,... | collective-permute-start | bytes 958472 | tf_op jit(solution)/shard_map/ppermute | solution.py:59
  353.0 21.4 %collective-permute-start.27 = (bf16[96,1664]{1,0:T(8,128)(2,1)}, bf16[96,1664]{1,0:T(8,128)(2,1)}, u32[]{:S(2)}, u32[]{:S(2)}) collective-permute-start(bf16[96,1664]{1,0:T(8,128)(2,1)} %get-tuple-element.283), channel_id=1, source_target_pairs={{0,4},{1,5},{2,6},{3,7},{4,0},{5,1},{6,2},{7,3},{8,12},{9,13},{10,... | collective-permute-start | bytes 958472 | tf_op jit(solution)/shard_map/ppermute | solution.py:59
  354.3 20.2 %collective-permute-start.28 = (bf16[96,1664]{1,0:T(8,128)(2,1)}, bf16[96,1664]{1,0:T(8,128)(2,1)}, u32[]{:S(2)}, u32[]{:S(2)}) collective-permute-start(bf16[96,1664]{1,0:T(8,128)(2,1)} %get-tuple-element.284), channel_id=1, source_target_pairs={{0,6},{1,7},{2,4},{3,5},{4,2},{5,3},{6,0},{7,1},{8,14},{9,15},{10,... | collective-permute-start | bytes 958472 | tf_op jit(solution)/shard_map/ppermute | solution.py:59
  (95 other events, 928.6 us)
Sparse Core Ops, SparseCore 0:
  53.4 91.5 all-gather.1
  278.0 99.0 reduce-scatter.1

commit v3 on v2

--- a/solution.py
+++ b/solution.py
@@ -30,7 +30,7 @@
 
 TILE = 128
 KEY_TILES = TOK_DEV // TILE
-QUERY_BLOCK = 256
+QUERY_BLOCK = 512
 QUERY_BLOCKS = TOK_DEV // QUERY_BLOCK
 HALVES = QUERY_BLOCK // TILE
 NT = (((1,), (1,)), ((), ()))
@@ -80,23 +80,16 @@
     return [view[flip].astype(BF16) for flip in range(1, 4)], view
 
 
-def add_z(total, size):
-    depth = size // 8
-    view = total.reshape(depth, -1, total.shape[1])
-    out = view[0]
-    for shift in range(1, depth):
-        out = out + along_z(view[shift].astype(BF16), size, shift).astype(F32)
-    return out
-
-
 def sum_all(values):
     while len(values) > 1:
-        values = [left + right for left, right in zip(values[::2], values[1::2])]
+        half = len(values) // 2
+        values = [left + right for left, right in zip(values[:half], values[half:])]
     return values[0]
 
 
-def along_z_flip(value, size, flip):
-    return lax.ppermute(value, AXIS, [(i, i ^ (flip << 3)) for i in range(size)])
+def with_table(low, table):
+    rows = low.shape[0]
+    return jnp.concatenate([low, jnp.pad(table, ((0, rows - 3), (0, 0)))], axis=1)
 
 
 def score_tile(tile, block, keys, queries, near_ref, head):
@@ -540,7 +533,12 @@
     return list(result[:EXPERTS]), list(result[EXPERTS:])
 
 
-def combine_kernel(slot_ref, *refs):
+def finish_kernel(
+    slot_ref, attended_ref, upstream_ref, probs_ref, hot_ref, gate_ref, gain_ref, router_ref,
+    weight_ref, *refs,
+):
+    pieces = refs[: 2 * EXPERTS]
+    out_ref, rest_ref, low_ref, mixed_ref, logits_ref, gain_sum_ref = refs[2 * EXPERTS :]
     rows = slot_ref.shape[0]
     totals = [None, None]
     for chunk in range(EXPERTS):
@@ -548,33 +546,79 @@
         hit = jnp.where(place == slot_ref[...], 1.0, 0.0).astype(BF16)
         for which in range(2):
             part = lax.dot_general(
-                hit, refs[which * EXPERTS + chunk][...], NN, preferred_element_type=F32
+                hit, pieces[which * EXPERTS + chunk][...], NN, preferred_element_type=F32
             )
             totals[which] = part if totals[which] is None else totals[which] + part
-    for which in range(2):
-        refs[2 * EXPERTS + which][...] = totals[which]
-
-
-def combine(slot_column, first, second):
+    expert_rows, back_rows = totals
+    attended, upstream = attended_ref[...], upstream_ref[...].astype(F32)
+    gate = gate_ref[...]
+    out_ref[...] = (attended + gate * expert_rows).astype(BF16)
+    grad_gate = jnp.sum(upstream * expert_rows, axis=1, keepdims=True)
+    grad_logits = probs_ref[...] * (grad_gate * hot_ref[...] - grad_gate * gate)
+    logits_ref[...] = grad_logits
+    grad_logits = grad_logits.astype(BF16).astype(F32)
+    grad = back_rows
+    for expert in range(EXPERTS):
+        grad = grad + grad_logits[:, expert : expert + 1] * router_ref[expert : expert + 1]
+    inverse = lax.rsqrt(jnp.mean(attended * attended, axis=-1, keepdims=True) + norm_eps)
+    gain_part = jnp.sum(grad * (attended * inverse), axis=0, keepdims=True)
+
+    @pl.when(pl.program_id(0) == 0)
+    def _():
+        gain_sum_ref[...] = gain_part
+
+    @pl.when(pl.program_id(0) > 0)
+    def _():
+        gain_sum_ref[...] += gain_part
+
+    grad = grad * gain_ref[...]
+    along = jnp.mean(attended * grad, axis=-1, keepdims=True)
+    rest = upstream + inverse * (grad - attended * (inverse * inverse * along))
+    rest_ref[...] = rest
+    low = rest.astype(BF16)
+    low_ref[...] = low
+    mixed_ref[...] = lax.dot_general(
+        low, weight_ref[...], NT, preferred_element_type=F32
+    ).astype(BF16)
+
+
+def finish(slot_column, attended, upstream, probs, hot, gate, gain, router_t, weight, first, second):
     rows = TOK_DEV // 4
-    part = pl.BlockSpec((rows, D), lambda step: (step, 0))
+
+    def part(width):
+        return pl.BlockSpec((rows, width), lambda step: (step, 0))
+
+    def whole(shape):
+        return pl.BlockSpec(shape, lambda step: (0, 0))
+
     return pl.pallas_call(
-        combine_kernel,
+        finish_kernel,
         grid=(TOK_DEV // rows,),
-        in_specs=[pl.BlockSpec((rows, 1), lambda step: (step, 0))]
-        + [pl.BlockSpec((CAP, D), lambda step: (0, 0))] * (2 * EXPERTS),
-        out_specs=[part, part],
-        out_shape=[jax.ShapeDtypeStruct((TOK_DEV, D), F32)] * 2,
+        in_specs=[part(1), part(D), part(D), part(EXPERTS), part(EXPERTS), part(1)]
+        + [whole((1, D)), whole((EXPERTS, D)), whole((D, D))]
+        + [whole((CAP, D))] * (2 * EXPERTS),
+        out_specs=[part(D), part(D), part(D), part(D), part(EXPERTS), whole((1, D))],
+        out_shape=[
+            jax.ShapeDtypeStruct((TOK_DEV, D), BF16),
+            jax.ShapeDtypeStruct((TOK_DEV, D), F32),
+            jax.ShapeDtypeStruct((TOK_DEV, D), BF16),
+            jax.ShapeDtypeStruct((TOK_DEV, D), BF16),
+            jax.ShapeDtypeStruct((TOK_DEV, EXPERTS), F32),
+            jax.ShapeDtypeStruct((1, D), F32),
+        ],
         compiler_params=pltpu.CompilerParams(vmem_limit_bytes=60 << 20),
         cost_estimate=pl.CostEstimate(
-            flops=4 * ROWS * TOK_DEV * D, bytes_accessed=12 << 20, transcendentals=0
+            flops=4 * ROWS * TOK_DEV * D, bytes_accessed=20 << 20, transcendentals=0
         ),
-    )(slot_column, *first, *second)
-
-
-def expert_layout(weights):
+    )(
+        slot_column, attended, upstream, probs, hot, gate, gain, router_t, weight,
+        *first, *second,
+    )
+
+
+def expert_layout(weights, width):
     pieces, _, units, _ = weights.shape
-    per_step = max(1, D // units)
+    per_step = max(1, width // units)
     steps = pieces // per_step
     width = per_step * units
     whole = pl.BlockSpec((CAP, D), lambda step: (0, 0))
@@ -586,7 +630,7 @@
 
 
 def expert_pass(rows, upstream, gate, weights):
-    steps, total, whole, part, up, down, _ = expert_layout(weights)
+    steps, total, whole, part, up, down, _ = expert_layout(weights, D)
     return pl.pallas_call(
         expert_kernel,
         grid=(steps,),
@@ -603,7 +647,7 @@
 
 
 def expert_weight_grads(rows, grads, hiddens, grad_pres, weights):
-    steps, total, whole, part, _, _, both = expert_layout(weights)
+    steps, total, whole, part, _, _, both = expert_layout(weights, D // 2)
     return pl.pallas_call(
         expert_weight_kernel,
         grid=(steps,),
@@ -715,12 +759,12 @@
     gain_first = side[:, D + EXPERTS].astype(F32)
     gain_second = side[:, D + EXPERTS + 1].astype(F32)
     mixed, logs = attend(qkv, extra_q, extra_k, near)
-    mixed, upstream_rows = lax.optimization_barrier((mixed, upstream_rows))
     attended = tokens_f + jnp.dot(mixed, out_w, preferred_element_type=F32)
     normed_ffn = rms_norm(attended, gain_second).astype(BF16)
     logits = jnp.dot(normed_ffn, router_w, preferred_element_type=F32)
     probs_route = jax.nn.softmax(logits, axis=-1)
     gate = jnp.sum(probs_route * route_hot, axis=1, keepdims=True)
+    normed_ffn, upstream_rows = lax.optimization_barrier((normed_ffn, upstream_rows))
     rows, gates = dispatch(slot_row, normed_ffn, gate.reshape(1, TOK_DEV))
     rows[0], late_mixed, late_dense = lax.optimization_barrier((rows[0], mixed, dense))
     gates = swap_rows(gates, size)
@@ -740,8 +784,9 @@
         ).astype(BF16)
         for part in range(PARTS)
     ]
-    rows[1], rows[3], gates, turned_mixed, qkv_parts = lax.optimization_barrier(
-        (rows[1], rows[3], gates, turned_mixed, qkv_parts)
+    router_t = router_w.astype(F32).T
+    rows[1], rows[3], gates, turned_mixed, qkv_parts, router_t = lax.optimization_barrier(
+        (rows[1], rows[3], gates, turned_mixed, qkv_parts, router_t)
     )
     rows[3] = along_quad(rows[3], size, 3)
 
@@ -771,8 +816,9 @@
         rows, *([member[which] for member in order] for which in (2, 3, 4)), weights
     )
     expert_grads, out_3, back_3 = lax.optimization_barrier((expert_grads, out_3, back_3))
-    expert_tok, back_tok = combine(
-        slot_column,
+    output, grad_res, grad_attn_out, grad_mixed, grad_logits, grad_gain_second = finish(
+        slot_column, attended, cotangent, probs_route, route_hot, gate, gain_second[None],
+        router_t, out_w,
         (passes[0][0], out_1, out_2, out_3),
         (passes[0][1], back_1, back_2, back_3),
     )
@@ -780,24 +826,11 @@
         expert_grads, AXIS, scatter_dimension=0, tiled=True, axis_index_groups=same_expert
     ).reshape(2, EXPERTS, units, D)
 
-    output = (attended + gate * expert_tok).astype(BF16)
-    upstream = cotangent.astype(F32)
-    grad_gate = jnp.sum(upstream * expert_tok, axis=1, keepdims=True)
-    grad_logits = (probs_route * (grad_gate * route_hot - grad_gate * gate)).astype(BF16)
-    grad_normed_ffn = back_tok + jnp.einsum(
-        "te,de->td", grad_logits, router_w, preferred_element_type=F32
-    )
-    unused_second, second_pull = jax.vjp(rms_norm, attended, gain_second)
-    grad_res_norm, grad_gain_second = second_pull(grad_normed_ffn)
-    grad_res = upstream + grad_res_norm
-    grad_attn_out = grad_res.astype(BF16)
-    grad_mixed = jnp.einsum(
-        "tf,df->td", grad_attn_out, out_w, preferred_element_type=F32
-    ).astype(BF16)
+    grad_logits = grad_logits.astype(BF16)
     grad_router = jnp.einsum("td,te->de", normed_ffn, grad_logits, preferred_element_type=F32)
 
     narrow = jnp.concatenate(
-        [grad_router, grad_gain_second[:, None], jnp.zeros((D, 128 - EXPERTS - 1), F32)], axis=1
+        [grad_router, grad_gain_second.T, jnp.zeros((D, 128 - EXPERTS - 1), F32)], axis=1
     ).astype(BF16)
     narrow = lax.dot_general(hand_on, narrow, TN, preferred_element_type=F32)
     narrow_mine, narrow_other = narrow[: D // 2], narrow[D // 2 :].astype(BF16)
@@ -830,35 +863,44 @@
             for part in (table_0, table_1, table_2)
         ]
     ).reshape(-1, 128)
-    other_2, mine_2, table_grad, expert_sums = lax.optimization_barrier(
-        (other_2, mine_2, table_grad, expert_sums)
-    )
-    by_flip = swap_rows([expert_sums[:, flip] for flip in range(EXPERTS)], size)
+    by_flip = [expert_sums[:, flip] for flip in range(EXPERTS)]
+    table_low = table_grad.astype(BF16)
+    other_2, mine_2, table_low, by_flip = lax.optimization_barrier(
+        (with_table(other_2, table_low), mine_2, table_low, by_flip)
+    )
 
     arrived_2 = along_core(other_2, size)
-    table_grad = table_grad + along_core(table_grad, size)
+    by_flip = swap_rows(by_flip, size)
     total = view[0] + sum(piece.astype(F32) for piece in arrived)
     late_1 = mine_1 + arrived_1.astype(F32)
-    arrived_2, table_grad, total, late_1 = lax.optimization_barrier(
-        (arrived_2, table_grad, total, late_1)
-    )
+    arrived_2, total, late_1, by_flip[1] = lax.optimization_barrier(
+        (arrived_2, total, late_1, by_flip[1])
+    )
+    table_low = (table_low.astype(F32) + arrived_2[:3, 3 * PART :].astype(F32)).astype(BF16)
     low, view = for_quad(
-        jnp.concatenate([late_1, mine_2 + arrived_2.astype(F32)], axis=1)
-    )
-    low, view, late_grads = lax.optimization_barrier((low, view, [grads_0, grads_1, grads_2]))
+        jnp.concatenate([late_1, mine_2 + arrived_2[:, : 3 * PART].astype(F32)], axis=1)
+    )
+    low = [with_table(piece, table_low) for piece in low]
+    low, view, table_low, late_grads = lax.optimization_barrier(
+        (low, view, table_low, [grads_0, grads_1, grads_2])
+    )
     arrived = [along_quad(low[flip - 1], size, flip) for flip in range(1, 4)]
-    tables = [table_grad] + [along_quad(table_grad, size, flip) for flip in range(1, 4)]
     grad_tokens = token_grad(late_grads, qkv_parts, tokens, gain_first[None], grad_res)
-    arrived, tables, grad_tokens, by_flip = lax.optimization_barrier(
-        (arrived, tables, grad_tokens, by_flip)
-    )
-    table_grad = sum_all(tables)
+    arrived, grad_tokens, by_flip = lax.optimization_barrier((arrived, grad_tokens, by_flip))
+    table_low = sum_all(
+        [table_low.astype(F32)] + [piece[:3, 6 * PART :].astype(F32) for piece in arrived]
+    ).astype(BF16)
     total = jnp.concatenate(
-        [total, view[0] + sum(piece.astype(F32) for piece in arrived)], axis=1
-    )
-    sums = add_z(total, size)
+        [total, view[0] + sum(piece[:, : 6 * PART].astype(F32) for piece in arrived)], axis=1
+    ).reshape(depth, owned, -1)
+    width = total.shape[2]
+    arrived = [
+        along_z(with_table(total[shift].astype(BF16), table_low), size, shift)
+        for shift in range(1, depth)
+    ]
+    sums = total[0] + sum(piece[:, :width].astype(F32) for piece in arrived)
     table_sum = sum_all(
-        [table_grad] + [along_z_flip(table_grad, size, flip) for flip in range(1, depth)]
+        [table_low.astype(F32)] + [piece[:3, width:].astype(F32) for piece in arrived]
     )
     table_sum = table_sum.reshape(HEADS, BUCKETS).T
     out_sum = sums[:, :D]

time: 452 us -> 437 us (0.967)
  starting transfers between devices: 55.9 us -> 46.5 us
  matrix products: 30.4 us -> 21.6 us
  local copies, waits for them, and re-layouts: 46.1 us -> 54.6 us
    pallas_call x3, Pallas kernels: 52.4 us -> 46 us  [attend_back(): pl.pallas_call(attend_back_kernel, grid=(PART_PAIRS,), in_specs=[column(f...]
    dot_general x2 -> x0, matrix products: 5.78 us -> none  [the longest x1 4.33 us: body(): jnp.einsum('te,de->td', grad_logits, router_w, preferred_element_type=F32)]
    pallas_call x1, Pallas kernels: 11.3 us -> 16.6 us  [finish(): pl.pallas_call(finish_kernel, grid=(TOK_DEV // rows,), in_specs=[part(1),...]
    ppermute x33 -> x30, starting transfers between devices: 39.6 us -> 35.5 us  [along_quad(): return lax.ppermute(value, AXIS, [(i, i ^ flip << 1) for i in range(size)])]
    ppermute x33 -> x30, waiting for transfers between devices: 37.5 us -> 34.2 us  [along_quad(): return lax.ppermute(value, AXIS, [(i, i ^ flip << 1) for i in range(size)])]
    unnamed x157 -> x155, local copies, waits for them, and re-layouts: 30 us -> 30.6 us
  transfers between devices with their start and end apart: 49 -> 42, of which waited for: 14 -> 17; matrix products, arithmetic and copies ran while one was open for 18% -> 18% of each run, Pallas kernels for 47% -> 48%
where the time goes in v3:
time: 437 us; the launch traced here: 429 us
  Pallas kernels  207 us (47%)
  local copies, waits for them, and re-layouts  54.6 us (12%)
  waiting for transfers between devices  50.6 us (12%)
  starting transfers between devices  46.5 us (11%)
  other arithmetic  32.4 us (7%)
  matrix products  21.6 us (5%)
  between operations  15.5 us (4%)
    pallas_call x4, Pallas kernels, expert_pass(): pl.pallas_call(expert_kernel, grid=(steps,), in_specs=[whole, whole, pl.B...  65.9 us
    pallas_call x3, Pallas kernels, attend_back(): pl.pallas_call(attend_back_kernel, grid=(PART_PAIRS,), in_specs=[column(f...  46 us
    ppermute x30, starting transfers between devices, along_quad(): return lax.ppermute(value, AXIS, [(i, i ^ flip << 1) for i in range(size)])  35.5 us
    ppermute x30, waiting for transfers between devices, along_quad(): return lax.ppermute(value, AXIS, [(i, i ^ flip << 1) for i in range(size)])  34.2 us
    unnamed x155, local copies, waits for them, and re-layouts  30.6 us
    pallas_call x1, Pallas kernels, expert_weight_grads(): pl.pallas_call(expert_weight_kernel, grid=(steps,), in_specs=[whole] * (2...  26.8 us
    pallas_call x1, Pallas kernels, attend(): pl.pallas_call(attend_kernel, grid=(PAIRS,), in_specs=[column(0), column(...  24.2 us
    pallas_call x1, Pallas kernels, finish(): pl.pallas_call(finish_kernel, grid=(TOK_DEV // rows,), in_specs=[part(1),...  16.6 us
  transfers between devices with their start and end apart: 42, of which 17 were waited for; matrix products, arithmetic and copies ran while one was open for 18% of the time, Pallas kernels for 48%

profile of v3, /device:TPU:0, one launch (start us, length us, event | category | flops | bytes accessed | tf_op | source)
XLA Modules:
  0.0 428.7 jit_solution(10200421815479960577)
XLA Ops:
  10.5 5.1 %collective-permute-start = (bf16[24,3200]{1,0:T(8,128)(2,1)S(1)}, bf16[24,3200]{1,0:T(8,128)(2,1)}, u32[]{:S(2)}, u32[]{:S(2)}) collective-permute-start(bf16[24,3200]{1,0:T(8,128)(2,1)S(1)} %concatenate.79), channel_id=1, source_target_pairs={{0,24},{1,25},{2,26},{3,27},{4,28},{5,29},{6,30},{7,31},{8,0},{9,1... | collective-permute-start | bytes 460808 | tf_op jit(solution)/shard_map/ppermute | solution.py:53
  15.6 6.0 %constant_dynamic-slice_fusion.4 = (bf16[96,1,768]{2,1,0:T(2,128)(2,1)S(1)}, bf16[96,1,768]{2,1,0:T(2,128)(2,1)S(1)}, bf16[96,1,768]{2,1,0:T(2,128)(2,1)S(1)}, b...) fusion(bf16[96,4,768]{2,1,0:T(4,128)(2,1)} %param.23, ...), kind=kLoop, calls=%fused_computation.221 | loop fusion | bytes 2359312 | tf_op jit(solution)/shard_map/jit(dynamic_index_in_dim)/dynamic_slice | solution.py:704
  47.1 3.4 collective-permute-done.2
  59.8 8.8 %shard_map.195 = (bf16[512,768]{1,0:T(8,128)(2,1)S(1)}, bf16[512,768]{1,0:T(8,128)(2,1)}, bf16[512,768]{1,0:T(8,128)(2,1)}, bf16[512,768]{1,0:T(8,128)(2,1)}, f32[12,3,128,128]{3,2,1,0:T(8,128)S(1)}) custom-call(s32[1,1024]{1,0:T(1,128)S(1)} %add.281.slot_ref, bf16[1024,768]{1,0:T(8,128)(2,1)S(1)} %copy-done.18, s32[3,128,128]{2,1,0:T(8,128)S(1)} %fusion.45.bucket_ref, ...), custom_call_target="tpu_custom_call" | custom-call | flops 12884901888 | bytes 6291456 | tf_op jit(solution)/shard_map/pallas_call | solution.py:497
  71.4 10.9 %collective-permute-done.7 = bf16[96,3200]{1,0:T(8,128)(2,1)S(1)} collective-permute-done((bf16[96,3200]{1,0:T(8,128)(2,1)S(1)}, bf16[96,3200]{1,0:T(8,128)(2,1)S(1)}, u32[]{:S(2)}, u32[]{:S(2)}) %collective-permute-start.7) | collective-permute-done | bytes 614432 | tf_op jit(solution)/shard_map/ppermute | solution.py:59
  88.4 4.1 convolution_convert_fusion.q_ref.k_ref.v_ref
  97.9 24.2 %shard_map.196 = (bf16[1024,768]{1,0:T(8,128)(2,1)S(1)}, f32[6,2,1024]{2,1,0:T(2,128)S(1)}) custom-call(bf16[1024,2304]{1,0:T(8,128)(2,1)S(1)} %convolution_convert_fusion.q_ref.k_ref.v_ref, bf16[1024,2304]{1,0:T(8,128)(2,1)S(1)} %convolution_convert_fusion.q_ref.k_ref.v_ref, bf16[1024,2304]{1,0:T(8,128)(2,1)S(1)} %convolution_convert_fusion.q_ref.k_ref.v_ref, ...), custom_call_target="tpu_custom_call" | custom-call | flops 40000000000 | bytes 12582912 | tf_op jit(solution)/shard_map/pallas_call | solution.py:253
  131.8 4.6 %shard_map.197 = (bf16[512,768]{1,0:T(8,128)(2,1)S(1)}, bf16[512,768]{1,0:T(8,128)(2,1)S(1)}, bf16[512,768]{1,0:T(8,128)(2,1)}, bf16[512,768]{1,0:T(8,128)(2,1)}...) custom-call(s32[1,1024]{1,0:T(1,128)S(1)} %add.281.slot_ref, ...), custom_call_target="tpu_custom_call" | custom-call | flops 3221225472 | bytes 6291456 | tf_op jit(solution)/shard_map/pallas_call | solution.py:524
  152.3 3.9 collective-permute-done.14.gate_ref
  157.7 16.5 %shard_map.198 = (bf16[512,768]{1,0:T(8,128)(2,1)S(1)}, bf16[512,768]{1,0:T(8,128)(2,1)S(1)}, bf16[512,768]{1,0:T(8,128)(2,1)S(1)}, bf16[512,3072]{1,0:T(8,128)(2,1)}, bf16[512,3072]{1,0:T(8,128)(2,1)}) custom-call(bf16[512,768]{1,0:T(8,128)(2,1)S(1)} %collective-permute-done.13.rows_ref.refs_1_, bf16[512,768]{1,0:T(8,128)(2,1)} %collective-permute-done.10.upstream_ref, ...), custom_call_target="tpu_custom_call" | custom-call | flops 9663676416 | bytes 20971520 | tf_op jit(solution)/shard_map/pallas_call | solution.py:634
  177.7 16.3 %shard_map.199 = (bf16[512,768]{1,0:T(8,128)(2,1)S(1)}, bf16[512,768]{1,0:T(8,128)(2,1)S(1)}, bf16[512,768]{1,0:T(8,128)(2,1)S(1)}, bf16[512,3072]{1,0:T(8,128)(2,1)}, bf16[512,3072]{1,0:T(8,128)(2,1)}) custom-call(bf16[512,768]{1,0:T(8,128)(2,1)} %collective-permute-done.18.rows_ref.refs_2_, bf16[512,768]{1,0:T(8,128)(2,1)} %collective-permute-done.11.upstream_ref, ...), custom_call_target="tpu_custom_call" | custom-call | flops 9663676416 | bytes 20971520 | tf_op jit(solution)/shard_map/pallas_call | solution.py:634
  198.4 16.6 %shard_map.200 = (bf16[512,768]{1,0:T(8,128)(2,1)}, bf16[512,768]{1,0:T(8,128)(2,1)S(1)}, bf16[512,768]{1,0:T(8,128)(2,1)S(1)}, bf16[512,3072]{1,0:T(8,128)(2,1)}, bf16[512,3072]{1,0:T(8,128)(2,1)}) custom-call(bf16[512,768]{1,0:T(8,128)(2,1)} %collective-permute-done.17.rows_ref.refs_3_, bf16[512,768]{1,0:T(8,128)(2,1)} %collective-permute-done.12.upstream_ref, ...), custom_call_target="tpu_custom_call" | custom-call | flops 9663676416 | bytes 20971520 | tf_op jit(solution)/shard_map/pallas_call | solution.py:634
  215.3 16.5 %shard_map.201 = (bf16[512,768]{1,0:T(8,128)(2,1)S(1)}, bf16[512,768]{1,0:T(8,128)(2,1)S(1)}, bf16[512,768]{1,0:T(8,128)(2,1)S(1)}, bf16[512,3072]{1,0:T(8,128)(2,1)}, bf16[512,3072]{1,0:T(8,128)(2,1)}) custom-call(bf16[512,768]{1,0:T(8,128)(2,1)S(1)} %copy-done.30, bf16[512,768]{1,0:T(8,128)(2,1)S(1)} %copy-done.32, ...), custom_call_target="tpu_custom_call" | custom-call | flops 9663676416 | bytes 20971520 | tf_op jit(solution)/shard_map/pallas_call | solution.py:634
  237.5 26.8 %shard_map.202 = bf16[8,2,384,768]{3,2,1,0:T(8,128)(2,1)} custom-call(bf16[512,768]{1,0:T(8,128)(2,1)} %copy-done.29, bf16[512,768]{1,0:T(8,128)(2,1)} %copy-done.19, bf16[512,768]{1,0:T(8,128)(2,1)} %collective-permute-done.18.rows_ref.refs_2_, bf16[512,768]{1,0:T(8,128)(2,1)} %collective-permute-done.17.rows_ref.refs_3_, bf16[512,768]{1,0:T(8,128)(2,1)} %copy-done.36, ...), custom_call_target="tpu_custom_call" | custom-call | flops 19327352832 | bytes 41943040 | tf_op jit(solution)/shard_map/pallas_call | solution.py:651
  273.4 16.6 %shard_map.203 = (bf16[1024,768]{1,0:T(8,128)(2,1)}, f32[1024,768]{1,0:T(8,128)}, bf16[1024,768]{1,0:T(8,128)(2,1)}, bf16[1024,768]{1,0:T(8,128)(2,1)}, f32[1024,4]{1,0:T(8,128)}, /*index=5*/f32[1,768]{1,0:T(1,128)}) custom-call(s32[1024,1]{1,0:T(8,128)} %get-tuple-element.453.slot_ref, f32[1024,768]{1,0:T(8,128)} %copy-done.43, ...), custom_call_target="tpu_custom_call" | custom-call | flops 6442450944 | bytes 20971520 | tf_op jit(solution)/shard_map/pallas_call | solution.py:594
  295.1 15.4 %shard_map.205 = (bf16[3,1024,256]{2,1,0:T(8,128)(2,1)S(1)}, f32[2,2,32,128]{3,2,1,0:T(8,128)S(1)}) custom-call(bf16[1024,2304]{1,0:T(8,128)(2,1)} %copy-done.24, bf16[1024,2304]{1,0:T(8,128)(2,1)} %copy-done.24, bf16[1024,2304]{1,0:T(8,128)(2,1)} %copy-done.24, bf16[1024,768]{1,0:T(8,128)(2,1)S(1)} %copy-done.25, ...), custom_call_target="tpu_custom_call" | custom-call | flops 26666665984 | bytes 8388608 | tf_op jit(solution)/shard_map/pallas_call | solution.py:276
  319.3 15.4 %shard_map.207 = (bf16[3,1024,256]{2,1,0:T(8,128)(2,1)S(1)}, f32[2,2,32,128]{3,2,1,0:T(8,128)S(1)}) custom-call(bf16[1024,2304]{1,0:T(8,128)(2,1)} %copy-done.24, bf16[1024,2304]{1,0:T(8,128)(2,1)} %copy-done.24, bf16[1024,2304]{1,0:T(8,128)(2,1)} %copy-done.24, bf16[1024,768]{1,0:T(8,128)(2,1)S(1)} %copy-done.26, ...), custom_call_target="tpu_custom_call" | custom-call | flops 26666665984 | bytes 8388608 | tf_op jit(solution)/shard_map/pallas_call | solution.py:276
  337.1 3.5 fusion.97
  345.5 15.2 %shard_map.209 = (bf16[3,1024,256]{2,1,0:T(8,128)(2,1)S(1)}, f32[2,2,32,128]{3,2,1,0:T(8,128)S(1)}) custom-call(bf16[1024,2304]{1,0:T(8,128)(2,1)} %copy-done.24, bf16[1024,2304]{1,0:T(8,128)(2,1)} %copy-done.24, bf16[1024,2304]{1,0:T(8,128)(2,1)} %copy-done.24, bf16[1024,768]{1,0:T(8,128)(2,1)S(1)} %copy-done.26, ...), custom_call_target="tpu_custom_call" | custom-call | flops 26666665984 | bytes 8388608 | tf_op jit(solution)/shard_map/pallas_call | solution.py:276
  362.0 3.1 reduce-scatter.2.cloned.1.call-done
  377.9 3.5 collective-permute-done.31
  385.8 8.0 %shard_map.211 = bf16[1024,768]{1,0:T(8,128)(2,1)} custom-call(bf16[3,1024,256]{2,1,0:T(8,128)(2,1)S(1)} %get-tuple-element.318.right_ref.grads_0, bf16[3,1024,256]{2,1,0:T(8,128)(2,1)} %copy-done.3, bf16[3,1024,256]{2,1,0:T(8,128)(2,1)} %copy-done.4, bf16[768,768]{1,0:T(8,128)(2,1)S(1)} %copy-done.8, bf16[768,768]{1,0:T(8,128)(2,1)S(1)} %copy-done.7, ...), custom_call_target="tpu_custom_call" | custom-call | flops 3623878656 | bytes 14680064 | tf_op jit(solution)/shard_map/pallas_call | solution.py:463
  394.7 7.5 %collective-permute-done.33 = bf16[96,1664]{1,0:T(8,128)(2,1)S(1)} collective-permute-done((bf16[96,1664]{1,0:T(8,128)(2,1)S(1)}, bf16[96,1664]{1,0:T(8,128)(2,1)S(1)}, u32[]{:S(2)}, u32[]{:S(2)}) %collective-permute-start.33) | collective-permute-done | bytes 319520 | tf_op jit(solution)/shard_map/ppermute | solution.py:59
  411.9 5.9 %collective-permute-done.38 = bf16[24,3328]{1,0:T(8,128)(2,1)S(1)} collective-permute-done((bf16[24,3328]{1,0:T(8,128)(2,1)S(1)}, bf16[24,3328]{1,0:T(8,128)(2,1)S(1)}, u32[]{:S(2)}, u32[]{:S(2)}) %collective-permute-start.38) | collective-permute-done | bytes 159776 | tf_op jit(solution)/shard_map/ppermute | solution.py:53
  (362 shorter events, 155.3 us)
Async XLA Ops:
  7.2 150.6 %all-gather.2.cloned.1.call-start = ((), (), s32[]{:S(2)}) async-start(), calls=%async_computation.1 | async-start | bytes 10616832 | tf_op jit(solution)/shard_map/all_gather | solution.py:736
  10.5 32.9 %collective-permute-start = (bf16[24,3200]{1,0:T(8,128)(2,1)S(1)}, bf16[24,3200]{1,0:T(8,128)(2,1)}, u32[]{:S(2)}, u32[]{:S(2)}) collective-permute-start(bf16[24,3200]{1,0:T(8,128)(2,1)S(1)} %concatenate.79), channel_id=1, source_target_pairs={{0,24},{1,25},{2,26},{3,27},{4,28},{5,29},{6,30},{7,31},{8,0},{9,1... | collective-permute-start | bytes 460808 | tf_op jit(solution)/shard_map/ppermute | solution.py:53
  15.6 31.6 %collective-permute-start.1 = (bf16[24,3200]{1,0:T(8,128)(2,1)S(1)}, bf16[24,3200]{1,0:T(8,128)(2,1)}, u32[]{:S(2)}, u32[]{:S(2)}) collective-permute-start(bf16[24,3200]{1,0:T(8,128)(2,1)S(1)} %concatenate.79), channel_id=1, source_target_pairs={{0,16},{1,17},{2,18},{3,19},{4,20},{5,21},{6,22},{7,23},{8,24},{9,... | collective-permute-start | bytes 460808 | tf_op jit(solution)/shard_map/ppermute | solution.py:53
  22.4 28.1 %collective-permute-start.5 = (bf16[2,96,768]{2,1,0:T(8,128)(2,1)}, bf16[2,96,768]{2,1,0:T(8,128)(2,1)}, u32[]{:S(2)}, u32[]{:S(2)}) collective-permute-start(bf16[2,96,768]{2,1,0:T(8,128)(2,1)} %pad_maximum_fusion.12), channel_id=1, source_target_pairs={{0,6},{1,7},{2,4},{3,5},{4,2},{5,3},{6,0},{7,1},{8,14},{9,15},{10,... | collective-permute-start | bytes 884744 | tf_op jit(solution)/shard_map/ppermute | solution.py:59
  25.7 24.9 %collective-permute-start.4 = (bf16[2,96,768]{2,1,0:T(8,128)(2,1)}, bf16[2,96,768]{2,1,0:T(8,128)(2,1)}, u32[]{:S(2)}, u32[]{:S(2)}) collective-permute-start(bf16[2,96,768]{2,1,0:T(8,128)(2,1)} %pad_maximum_fusion.11), channel_id=1, source_target_pairs={{0,4},{1,5},{2,6},{3,7},{4,0},{5,1},{6,2},{7,3},{8,12},{9,13},{10,... | collective-permute-start | bytes 884744 | tf_op jit(solution)/shard_map/ppermute | solution.py:59
  27.0 23.5 %collective-permute-start.3 = (bf16[2,96,768]{2,1,0:T(8,128)(2,1)}, bf16[2,96,768]{2,1,0:T(8,128)(2,1)}, u32[]{:S(2)}, u32[]{:S(2)}) collective-permute-start(bf16[2,96,768]{2,1,0:T(8,128)(2,1)} %pad_maximum_fusion.10), channel_id=1, source_target_pairs={{0,2},{1,3},{2,0},{3,1},{4,6},{5,7},{6,4},{7,5},{8,10},{9,11},{10,... | collective-permute-start | bytes 884744 | tf_op jit(solution)/shard_map/ppermute | solution.py:59
  53.0 312.1 %reduce-scatter.2.cloned.1.call-start = ((), (), s32[]{:S(2)}) async-start(), calls=%async_computation.2 | async-start | bytes 10616832 | tf_op jit(solution)/shard_map/reduce_scatter | solution.py:825
  56.1 26.2 %collective-permute-start.7 = (bf16[96,3200]{1,0:T(8,128)(2,1)S(1)}, bf16[96,3200]{1,0:T(8,128)(2,1)S(1)}, u32[]{:S(2)}, u32[]{:S(2)}) collective-permute-start(bf16[96,3200]{1,0:T(8,128)(2,1)S(1)} %pad_maximum_fusion.7), channel_id=1, source_target_pairs={{0,4},{1,5},{2,6},{3,7},{4,0},{5,1},{6,2},{7,3},{8,12},{9,13},{10,... | collective-permute-start | bytes 1843208 | tf_op jit(solution)/shard_map/ppermute | solution.py:59
  57.6 24.7 %collective-permute-start.8 = (bf16[96,3200]{1,0:T(8,128)(2,1)S(1)}, bf16[96,3200]{1,0:T(8,128)(2,1)S(1)}, u32[]{:S(2)}, u32[]{:S(2)}) collective-permute-start(bf16[96,3200]{1,0:T(8,128)(2,1)S(1)} %pad_maximum_fusion.7), channel_id=1, source_target_pairs={{0,6},{1,7},{2,4},{3,5},{4,2},{5,3},{6,0},{7,1},{8,14},{9,15},{10,... | collective-permute-start | bytes 1843208 | tf_op jit(solution)/shard_map/ppermute | solution.py:59
  94.0 35.5 %collective-permute-start.10 = (bf16[512,768]{1,0:T(8,128)(2,1)}, bf16[512,768]{1,0:T(8,128)(2,1)}, u32[]{:S(2)}, u32[]{:S(2)}) collective-permute-start(bf16[512,768]{1,0:T(8,128)(2,1)} %get-tuple-element.202), channel_id=1, source_target_pairs={{0,2},{1,3},{2,0},{3,1},{4,6},{5,7},{6,4},{7,5},{8,10},{9,11},{10,... | collective-permute-start | bytes 2359304 | tf_op jit(solution)/shard_map/ppermute | solution.py:59
  95.3 34.9 %collective-permute-start.11 = (bf16[512,768]{1,0:T(8,128)(2,1)}, bf16[512,768]{1,0:T(8,128)(2,1)}, u32[]{:S(2)}, u32[]{:S(2)}) collective-permute-start(bf16[512,768]{1,0:T(8,128)(2,1)} %get-tuple-element.203), channel_id=1, source_target_pairs={{0,4},{1,5},{2,6},{3,7},{4,0},{5,1},{6,2},{7,3},{8,12},{9,13},{10,... | collective-permute-start | bytes 2359304 | tf_op jit(solution)/shard_map/ppermute | solution.py:59
  96.1 35.6 %collective-permute-start.12 = (bf16[512,768]{1,0:T(8,128)(2,1)}, bf16[512,768]{1,0:T(8,128)(2,1)}, u32[]{:S(2)}, u32[]{:S(2)}) collective-permute-start(bf16[512,768]{1,0:T(8,128)(2,1)} %get-tuple-element.204), channel_id=1, source_target_pairs={{0,6},{1,7},{2,4},{3,5},{4,2},{5,3},{6,0},{7,1},{8,14},{9,15},{10,... | collective-permute-start | bytes 2359304 | tf_op jit(solution)/shard_map/ppermute | solution.py:59
  141.6 34.7 %collective-permute-start.18 = (bf16[512,768]{1,0:T(8,128)(2,1)}, bf16[512,768]{1,0:T(8,128)(2,1)}, u32[]{:S(2)}, u32[]{:S(2)}) collective-permute-start(bf16[512,768]{1,0:T(8,128)(2,1)} %get-tuple-element.218), channel_id=1, source_target_pairs={{0,4},{1,5},{2,6},{3,7},{4,0},{5,1},{6,2},{7,3},{8,12},{9,13},{10,... | collective-permute-start | bytes 2359304 | tf_op jit(solution)/shard_map/ppermute | solution.py:59
  156.2 42.2 %collective-permute-start.17 = (bf16[512,768]{1,0:T(8,128)(2,1)}, bf16[512,768]{1,0:T(8,128)(2,1)}, u32[]{:S(2)}, u32[]{:S(2)}) collective-permute-start(bf16[512,768]{1,0:T(8,128)(2,1)} %get-tuple-element.217), channel_id=1, source_target_pairs={{0,6},{1,7},{2,4},{3,5},{4,2},{5,3},{6,0},{7,1},{8,14},{9,15},{10,... | collective-permute-start | bytes 2359304 | tf_op jit(solution)/shard_map/ppermute | solution.py:59
  176.3 21.2 %collective-permute-start.19 = (bf16[512,768]{1,0:T(8,128)(2,1)S(1)}, bf16[512,768]{1,0:T(8,128)(2,1)S(1)}, u32[]{:S(2)}, u32[]{:S(2)}) collective-permute-start(bf16[512,768]{1,0:T(8,128)(2,1)S(1)} %get-tuple-element.231), channel_id=1, source_target_pairs={{0,2},{1,3},{2,0},{3,1},{4,6},{5,7},{6,4},{7,5},{8,10},{9,11},{10,... | collective-permute-start | bytes 2359304 | tf_op jit(solution)/shard_map/ppermute | solution.py:59
  194.8 20.5 %collective-permute-start.21 = (bf16[512,768]{1,0:T(8,128)(2,1)S(1)}, bf16[512,768]{1,0:T(8,128)(2,1)S(1)}, u32[]{:S(2)}, u32[]{:S(2)}) collective-permute-start(bf16[512,768]{1,0:T(8,128)(2,1)S(1)} %get-tuple-element.238), channel_id=1, source_target_pairs={{0,4},{1,5},{2,6},{3,7},{4,0},{5,1},{6,2},{7,3},{8,12},{9,13},{10,... | collective-permute-start | bytes 2359304 | tf_op jit(solution)/shard_map/ppermute | solution.py:59
  195.4 19.9 %collective-permute-start.20 = (bf16[512,768]{1,0:T(8,128)(2,1)S(1)}, bf16[512,768]{1,0:T(8,128)(2,1)S(1)}, u32[]{:S(2)}, u32[]{:S(2)}) collective-permute-start(bf16[512,768]{1,0:T(8,128)(2,1)S(1)} %get-tuple-element.237), channel_id=1, source_target_pairs={{0,2},{1,3},{2,0},{3,1},{4,6},{5,7},{6,4},{7,5},{8,10},{9,11},{10,... | collective-permute-start | bytes 2359304 | tf_op jit(solution)/shard_map/ppermute | solution.py:59
  196.6 38.0 %collective-permute-start.22 = (bf16[512,768]{1,0:T(8,128)(2,1)S(1)}, bf16[512,768]{1,0:T(8,128)(2,1)S(1)}, u32[]{:S(2)}, u32[]{:S(2)}) collective-permute-start(bf16[512,768]{1,0:T(8,128)(2,1)S(1)} %get-tuple-element.247), channel_id=1, source_target_pairs={{0,4},{1,5},{2,6},{3,7},{4,0},{5,1},{6,2},{7,3},{8,12},{9,13},{10,... | collective-permute-start | bytes 2359304 | tf_op jit(solution)/shard_map/ppermute | solution.py:59
  234.6 29.8 %collective-permute-start.23 = (bf16[512,768]{1,0:T(8,128)(2,1)}, bf16[512,768]{1,0:T(8,128)(2,1)}, u32[]{:S(2)}, u32[]{:S(2)}) collective-permute-start(bf16[512,768]{1,0:T(8,128)(2,1)} %get-tuple-element.260), channel_id=1, source_target_pairs={{0,6},{1,7},{2,4},{3,5},{4,2},{5,3},{6,0},{7,1},{8,14},{9,15},{10,... | collective-permute-start | bytes 2359304 | tf_op jit(solution)/shard_map/ppermute | solution.py:59
  236.0 31.4 %collective-permute-start.24 = (bf16[512,768]{1,0:T(8,128)(2,1)S(1)}, bf16[512,768]{1,0:T(8,128)(2,1)}, u32[]{:S(2)}, u32[]{:S(2)}) collective-permute-start(bf16[512,768]{1,0:T(8,128)(2,1)S(1)} %get-tuple-element.261), channel_id=1, source_target_pairs={{0,6},{1,7},{2,4},{3,5},{4,2},{5,3},{6,0},{7,1},{8,14},{9,15},{10,... | collective-permute-start | bytes 2359304 | tf_op jit(solution)/shard_map/ppermute | solution.py:59
  341.6 20.5 %collective-permute-start.29 = (bf16[384,768]{1,0:T(8,128)(2,1)}, bf16[384,768]{1,0:T(8,128)(2,1)}, u32[]{:S(2)}, u32[]{:S(2)}) collective-permute-start(bf16[384,768]{1,0:T(8,128)(2,1)} %get-tuple-element.294), channel_id=1, source_target_pairs={{0,1},{1,0},{2,3},{3,2},{4,5},{5,4},{6,7},{7,6},{8,9},{9,8},{10,11... | collective-permute-start | bytes 1769480 | tf_op jit(solution)/shard_map/ppermute | solution.py:63
  342.0 20.0 %collective-permute-start.26 = (bf16[96,1664]{1,0:T(8,128)(2,1)}, bf16[96,1664]{1,0:T(8,128)(2,1)}, u32[]{:S(2)}, u32[]{:S(2)}) collective-permute-start(bf16[96,1664]{1,0:T(8,128)(2,1)} %get-tuple-element.291), channel_id=1, source_target_pairs={{0,2},{1,3},{2,0},{3,1},{4,6},{5,7},{6,4},{7,5},{8,10},{9,11},{10,... | collective-permute-start | bytes 958472 | tf_op jit(solution)/shard_map/ppermute | solution.py:59
  373.1 20.7 %collective-permute-start.35 = (bf16[2,96,768]{2,1,0:T(8,128)(2,1)S(1)}, bf16[2,96,768]{2,1,0:T(8,128)(2,1)S(1)}, u32[]{:S(2)}, u32[]{:S(2)}) collective-permute-start(bf16[2,96,768]{2,1,0:T(8,128)(2,1)S(1)} %get-tuple-element.327), channel_id=1, source_target_pairs={{0,4},{1,5},{2,6},{3,7},{4,0},{5,1},{6,2},{7,3},{8,12},{9,13},{10,... | collective-permute-start | bytes 884744 | tf_op jit(solution)/shard_map/ppermute | solution.py:59
  374.6 19.2 %collective-permute-start.36 = (bf16[2,96,768]{2,1,0:T(8,128)(2,1)S(1)}, bf16[2,96,768]{2,1,0:T(8,128)(2,1)S(1)}, u32[]{:S(2)}, u32[]{:S(2)}) collective-permute-start(bf16[2,96,768]{2,1,0:T(8,128)(2,1)S(1)} %get-tuple-element.328), channel_id=1, source_target_pairs={{0,6},{1,7},{2,4},{3,5},{4,2},{5,3},{6,0},{7,1},{8,14},{9,15},{10,... | collective-permute-start | bytes 884744 | tf_op jit(solution)/shard_map/ppermute | solution.py:59
  (87 other events, 712.0 us)
Sparse Core Ops, SparseCore 0:
  53.2 89.4 all-gather.1
  267.5 97.6 reduce-scatter.1

commit v4 on v3

--- a/solution.py
+++ b/solution.py
@@ -534,8 +534,7 @@
 
 
 def finish_kernel(
-    slot_ref, attended_ref, upstream_ref, probs_ref, hot_ref, gate_ref, gain_ref, router_ref,
-    weight_ref, *refs,
+    slot_ref, attended_ref, upstream_ref, probs_ref, hot_ref, narrow_ref, weight_ref, *refs,
 ):
     pieces = refs[: 2 * EXPERTS]
     out_ref, rest_ref, low_ref, mixed_ref, logits_ref, gain_sum_ref = refs[2 * EXPERTS :]
@@ -551,7 +550,8 @@
             totals[which] = part if totals[which] is None else totals[which] + part
     expert_rows, back_rows = totals
     attended, upstream = attended_ref[...], upstream_ref[...].astype(F32)
-    gate = gate_ref[...]
+    gate = jnp.sum(probs_ref[...] * hot_ref[...], axis=1, keepdims=True)
+    narrow = narrow_ref[...].astype(F32)
     out_ref[...] = (attended + gate * expert_rows).astype(BF16)
     grad_gate = jnp.sum(upstream * expert_rows, axis=1, keepdims=True)
     grad_logits = probs_ref[...] * (grad_gate * hot_ref[...] - grad_gate * gate)
@@ -559,7 +559,7 @@
     grad_logits = grad_logits.astype(BF16).astype(F32)
     grad = back_rows
     for expert in range(EXPERTS):
-        grad = grad + grad_logits[:, expert : expert + 1] * router_ref[expert : expert + 1]
+        grad = grad + grad_logits[:, expert : expert + 1] * narrow[expert : expert + 1]
     inverse = lax.rsqrt(jnp.mean(attended * attended, axis=-1, keepdims=True) + norm_eps)
     gain_part = jnp.sum(grad * (attended * inverse), axis=0, keepdims=True)
 
@@ -571,7 +571,7 @@
     def _():
         gain_sum_ref[...] += gain_part
 
-    grad = grad * gain_ref[...]
+    grad = grad * narrow[EXPERTS + 1 : EXPERTS + 2]
     along = jnp.mean(attended * grad, axis=-1, keepdims=True)
     rest = upstream + inverse * (grad - attended * (inverse * inverse * along))
     rest_ref[...] = rest
@@ -582,7 +582,7 @@
     ).astype(BF16)
 
 
-def finish(slot_column, attended, upstream, probs, hot, gate, gain, router_t, weight, first, second):
+def finish(slot_column, attended, upstream, probs, hot, narrow, weight, first, second):
     rows = TOK_DEV // 4
 
     def part(width):
@@ -594,8 +594,8 @@
     return pl.pallas_call(
         finish_kernel,
         grid=(TOK_DEV // rows,),
-        in_specs=[part(1), part(D), part(D), part(EXPERTS), part(EXPERTS), part(1)]
-        + [whole((1, D)), whole((EXPERTS, D)), whole((D, D))]
+        in_specs=[part(1), part(D), part(D), part(EXPERTS), part(EXPERTS)]
+        + [whole((128, D)), whole((D, D))]
         + [whole((CAP, D))] * (2 * EXPERTS),
         out_specs=[part(D), part(D), part(D), part(D), part(EXPERTS), whole((1, D))],
         out_shape=[
@@ -611,8 +611,7 @@
             flops=4 * ROWS * TOK_DEV * D, bytes_accessed=20 << 20, transcendentals=0
         ),
     )(
-        slot_column, attended, upstream, probs, hot, gate, gain, router_t, weight,
-        *first, *second,
+        slot_column, attended, upstream, probs, hot, narrow, weight, *first, *second
     )
 
 
@@ -705,7 +704,9 @@
             ]
         )
 
-    arrived_weights = swap_rows([weights_for(flip) for flip in range(EXPERTS)], size)
+    offered = [weights_for(flip) for flip in range(EXPERTS)]
+    z_dense[0], offered[3] = lax.optimization_barrier((z_dense[0], offered[3]))
+    arrived_weights = swap_rows(offered, size)
     ends = jnp.cumsum(lengths[0])
     places = lax.iota(jnp.int32, TOK_DEV)
     doc_ids = jnp.sum((places[:, None] >= ends[None, :]).astype(jnp.int32), axis=1)
@@ -784,9 +785,13 @@
         ).astype(BF16)
         for part in range(PARTS)
     ]
-    router_t = router_w.astype(F32).T
-    rows[1], rows[3], gates, turned_mixed, qkv_parts, router_t = lax.optimization_barrier(
-        (rows[1], rows[3], gates, turned_mixed, qkv_parts, router_t)
+    narrow_t = lax.dot_general(
+        late_dense[:, 4 * D :], hand_on, (((0,), (1,)), ((), ())), preferred_element_type=F32
+    ).astype(BF16)
+    rows[1], rows[3], gates, turned_mixed, qkv_parts, narrow_t, out_w_late = (
+        lax.optimization_barrier(
+            (rows[1], rows[3], gates, turned_mixed, qkv_parts, narrow_t, out_w)
+        )
     )
     rows[3] = along_quad(rows[3], size, 3)
 
@@ -817,8 +822,7 @@
     )
     expert_grads, out_3, back_3 = lax.optimization_barrier((expert_grads, out_3, back_3))
     output, grad_res, grad_attn_out, grad_mixed, grad_logits, grad_gain_second = finish(
-        slot_column, attended, cotangent, probs_route, route_hot, gate, gain_second[None],
-        router_t, out_w,
+        slot_column, attended, cotangent, probs_route, route_hot, narrow_t, out_w_late,
         (passes[0][0], out_1, out_2, out_3),
         (passes[0][1], back_1, back_2, back_3),
     )
@@ -853,8 +857,8 @@
     )
     arrived_1 = along_core(other_1, size)
     arrived = [along_quad(low[flip - 1], size, flip) for flip in range(1, 4)]
-    (grads_2, table_2), arrived, arrived_1, expert_sums = lax.optimization_barrier(
-        (attend_part(2, logs), arrived, arrived_1, expert_sums)
+    (grads_2, table_2), arrived, arrived_1 = lax.optimization_barrier(
+        (attend_part(2, logs), arrived, arrived_1)
     )
     mine_2, other_2 = weight_halves(turned_normed, grads_2)
     table_grad = jnp.concatenate(
@@ -863,30 +867,27 @@
             for part in (table_0, table_1, table_2)
         ]
     ).reshape(-1, 128)
-    by_flip = [expert_sums[:, flip] for flip in range(EXPERTS)]
     table_low = table_grad.astype(BF16)
-    other_2, mine_2, table_low, by_flip = lax.optimization_barrier(
-        (with_table(other_2, table_low), mine_2, table_low, by_flip)
+    other_2, mine_2, table_low, late_grads = lax.optimization_barrier(
+        (with_table(other_2, table_low), mine_2, table_low, [grads_0, grads_1, grads_2])
     )
 
     arrived_2 = along_core(other_2, size)
-    by_flip = swap_rows(by_flip, size)
+    grad_tokens = token_grad(late_grads, qkv_parts, tokens, gain_first[None], grad_res)
+    arrived_2, grad_tokens = lax.optimization_barrier((arrived_2, grad_tokens))
     total = view[0] + sum(piece.astype(F32) for piece in arrived)
     late_1 = mine_1 + arrived_1.astype(F32)
-    arrived_2, total, late_1, by_flip[1] = lax.optimization_barrier(
-        (arrived_2, total, late_1, by_flip[1])
-    )
     table_low = (table_low.astype(F32) + arrived_2[:3, 3 * PART :].astype(F32)).astype(BF16)
     low, view = for_quad(
         jnp.concatenate([late_1, mine_2 + arrived_2[:, : 3 * PART].astype(F32)], axis=1)
     )
     low = [with_table(piece, table_low) for piece in low]
-    low, view, table_low, late_grads = lax.optimization_barrier(
-        (low, view, table_low, [grads_0, grads_1, grads_2])
-    )
+    by_flip = [expert_sums[:, flip] for flip in range(EXPERTS)]
+    low, view, table_low, by_flip = lax.optimization_barrier((low, view, table_low, by_flip))
     arrived = [along_quad(low[flip - 1], size, flip) for flip in range(1, 4)]
-    grad_tokens = token_grad(late_grads, qkv_parts, tokens, gain_first[None], grad_res)
-    arrived, grad_tokens, by_flip = lax.optimization_barrier((arrived, grad_tokens, by_flip))
+    by_flip[1] = along_quad(by_flip[1], size, 1)
+    arrived, by_flip = lax.optimization_barrier((arrived, by_flip))
+    by_flip[2:] = [along_quad(by_flip[flip], size, flip) for flip in range(2, EXPERTS)]
     table_low = sum_all(
         [table_low.astype(F32)] + [piece[:3, 6 * PART :].astype(F32) for piece in arrived]
     ).astype(BF16)

time: 437 us -> 437 us (level)
    ppermute x30, waiting for transfers between devices: 34.2 us -> 42.7 us  [along_quad(): return lax.ppermute(value, AXIS, [(i, i ^ flip << 1) for i in range(size)])]
    unnamed x155 -> x165, local copies, waits for them, and re-layouts: 30.6 us -> 30.6 us
  transfers between devices with their start and end apart: 42 -> 42, of which waited for: 17 -> 13; matrix products, arithmetic and copies ran while one was open for 18% -> 18% of each run, Pallas kernels for 48% -> 48%
where the time goes in v4:
time: 437 us; the launch traced here: 428 us
  Pallas kernels  206 us (47%)
  local copies, waits for them, and re-layouts  51.9 us (12%)
  waiting for transfers between devices  51.8 us (12%)
  starting transfers between devices  46.3 us (11%)
  other arithmetic  32.8 us (8%)
  matrix products  23.7 us (5%)
  between operations  15.5 us (4%)
    pallas_call x4, Pallas kernels, expert_pass(): pl.pallas_call(expert_kernel, grid=(steps,), in_specs=[whole, whole, pl.B...  65 us
    pallas_call x3, Pallas kernels, attend_back(): pl.pallas_call(attend_back_kernel, grid=(PART_PAIRS,), in_specs=[column(f...  45.8 us
    ppermute x30, waiting for transfers between devices, along_quad(): return lax.ppermute(value, AXIS, [(i, i ^ flip << 1) for i in range(size)])  42.7 us
    ppermute x30, starting transfers between devices, along_quad(): return lax.ppermute(value, AXIS, [(i, i ^ flip << 1) for i in range(size)])  33.2 us
    unnamed x165, local copies, waits for them, and re-layouts  30.6 us
    pallas_call x1, Pallas kernels, expert_weight_grads(): pl.pallas_call(expert_weight_kernel, grid=(steps,), in_specs=[whole] * (2...  26.8 us
    pallas_call x1, Pallas kernels, attend(): pl.pallas_call(attend_kernel, grid=(PAIRS,), in_specs=[column(0), column(...  24.2 us
    pallas_call x1, Pallas kernels, finish(): pl.pallas_call(finish_kernel, grid=(TOK_DEV // rows,), in_specs=[part(1),...  16.4 us
  transfers between devices with their start and end apart: 42, of which 13 were waited for; matrix products, arithmetic and copies ran while one was open for 18% of the time, Pallas kernels for 48%

profile of v4, /device:TPU:0, one launch (start us, length us, event | category | flops | bytes accessed | tf_op | source)
XLA Modules:
  0.0 428.4 jit_solution(8168122685526991519)
XLA Ops:
  10.5 5.1 %collective-permute-start = (bf16[24,3200]{1,0:T(8,128)(2,1)S(1)}, bf16[24,3200]{1,0:T(8,128)(2,1)}, u32[]{:S(2)}, u32[]{:S(2)}) collective-permute-start(bf16[24,3200]{1,0:T(8,128)(2,1)S(1)} %concatenate.79), channel_id=1, source_target_pairs={{0,24},{1,25},{2,26},{3,27},{4,28},{5,29},{6,30},{7,31},{8,0},{9,1... | collective-permute-start | bytes 460808 | tf_op jit(solution)/shard_map/ppermute | solution.py:53
  16.6 6.0 %constant_dynamic-slice_fusion.4 = (bf16[96,1,768]{2,1,0:T(2,128)(2,1)S(1)}, bf16[96,1,768]{2,1,0:T(2,128)(2,1)S(1)}, bf16[96,1,768]{2,1,0:T(2,128)(2,1)}, bf16[...) fusion(bf16[96,4,768]{2,1,0:T(4,128)(2,1)} %param.23, ...), kind=kLoop, calls=%fused_computation.222 | loop fusion | bytes 2359312 | tf_op jit(solution)/shard_map/jit(dynamic_index_in_dim)/dynamic_slice | solution.py:703
  31.3 3.1 fusion.3
  47.6 4.3 %collective-permute-done.5 = bf16[2,96,768]{2,1,0:T(8,128)(2,1)} collective-permute-done((bf16[2,96,768]{2,1,0:T(8,128)(2,1)}, bf16[2,96,768]{2,1,0:T(8,128)(2,1)}, u32[]{:S(2)}, u32[]{:S(2)}) %collective-permute-start.5) | collective-permute-done | bytes 294944 | tf_op jit(solution)/shard_map/ppermute | solution.py:59
  61.2 8.8 %shard_map.195 = (bf16[512,768]{1,0:T(8,128)(2,1)S(1)}, bf16[512,768]{1,0:T(8,128)(2,1)}, bf16[512,768]{1,0:T(8,128)(2,1)}, bf16[512,768]{1,0:T(8,128)(2,1)}, f32[12,3,128,128]{3,2,1,0:T(8,128)S(1)}) custom-call(s32[1,1024]{1,0:T(1,128)S(1)} %add.281.slot_ref, bf16[1024,768]{1,0:T(8,128)(2,1)S(1)} %copy-done.14, s32[3,128,128]{2,1,0:T(8,128)S(1)} %fusion.45.bucket_ref, ...), custom_call_target="tpu_custom_call" | custom-call | flops 12884901888 | bytes 6291456 | tf_op jit(solution)/shard_map/pallas_call | solution.py:497
  72.8 9.9 %collective-permute-done.7 = bf16[96,3200]{1,0:T(8,128)(2,1)S(1)} collective-permute-done((bf16[96,3200]{1,0:T(8,128)(2,1)S(1)}, bf16[96,3200]{1,0:T(8,128)(2,1)S(1)}, u32[]{:S(2)}, u32[]{:S(2)}) %collective-permute-start.7) | collective-permute-done | bytes 614432 | tf_op jit(solution)/shard_map/ppermute | solution.py:59
  85.0 2.9 collective-permute-done.9
  88.8 4.1 convolution_convert_fusion.q_ref.k_ref.v_ref
  98.8 24.2 %shard_map.196 = (bf16[1024,768]{1,0:T(8,128)(2,1)S(1)}, f32[6,2,1024]{2,1,0:T(2,128)S(1)}) custom-call(bf16[1024,2304]{1,0:T(8,128)(2,1)S(1)} %convolution_convert_fusion.q_ref.k_ref.v_ref, bf16[1024,2304]{1,0:T(8,128)(2,1)S(1)} %convolution_convert_fusion.q_ref.k_ref.v_ref, bf16[1024,2304]{1,0:T(8,128)(2,1)S(1)} %convolution_convert_fusion.q_ref.k_ref.v_ref, ...), custom_call_target="tpu_custom_call" | custom-call | flops 40000000000 | bytes 12582912 | tf_op jit(solution)/shard_map/pallas_call | solution.py:253
  132.4 4.7 %shard_map.197 = (bf16[512,768]{1,0:T(8,128)(2,1)S(1)}, bf16[512,768]{1,0:T(8,128)(2,1)S(1)}, bf16[512,768]{1,0:T(8,128)(2,1)}, bf16[512,768]{1,0:T(8,128)(2,1)}...) custom-call(s32[1,1024]{1,0:T(1,128)S(1)} %add.281.slot_ref, ...), custom_call_target="tpu_custom_call" | custom-call | flops 3221225472 | bytes 6291456 | tf_op jit(solution)/shard_map/pallas_call | solution.py:524
  158.1 16.4 %shard_map.198 = (bf16[512,768]{1,0:T(8,128)(2,1)S(1)}, bf16[512,768]{1,0:T(8,128)(2,1)S(1)}, bf16[512,768]{1,0:T(8,128)(2,1)S(1)}, bf16[512,3072]{1,0:T(8,128)(2,1)}, bf16[512,3072]{1,0:T(8,128)(2,1)}) custom-call(bf16[512,768]{1,0:T(8,128)(2,1)S(1)} %collective-permute-done.13.rows_ref.refs_1_, bf16[512,768]{1,0:T(8,128)(2,1)} %collective-permute-done.10.upstream_ref, ...), custom_call_target="tpu_custom_call" | custom-call | flops 9663676416 | bytes 20971520 | tf_op jit(solution)/shard_map/pallas_call | solution.py:633
  177.7 16.1 %shard_map.199 = (bf16[512,768]{1,0:T(8,128)(2,1)S(1)}, bf16[512,768]{1,0:T(8,128)(2,1)S(1)}, bf16[512,768]{1,0:T(8,128)(2,1)S(1)}, bf16[512,3072]{1,0:T(8,128)(2,1)}, bf16[512,3072]{1,0:T(8,128)(2,1)}) custom-call(bf16[512,768]{1,0:T(8,128)(2,1)S(1)} %collective-permute-done.18.rows_ref.refs_2_, bf16[512,768]{1,0:T(8,128)(2,1)} %collective-permute-done.11.upstream_ref, ...), custom_call_target="tpu_custom_call" | custom-call | flops 9663676416 | bytes 20971520 | tf_op jit(solution)/shard_map/pallas_call | solution.py:633
  198.4 16.4 %shard_map.200 = (bf16[512,768]{1,0:T(8,128)(2,1)S(1)}, bf16[512,768]{1,0:T(8,128)(2,1)S(1)}, bf16[512,768]{1,0:T(8,128)(2,1)S(1)}, bf16[512,3072]{1,0:T(8,128)(2,1)}, bf16[512,3072]{1,0:T(8,128)(2,1)}) custom-call(bf16[512,768]{1,0:T(8,128)(2,1)} %collective-permute-done.17.rows_ref.refs_3_, bf16[512,768]{1,0:T(8,128)(2,1)} %collective-permute-done.12.upstream_ref, ...), custom_call_target="tpu_custom_call" | custom-call | flops 9663676416 | bytes 20971520 | tf_op jit(solution)/shard_map/pallas_call | solution.py:633
  215.7 16.2 %shard_map.201 = (bf16[512,768]{1,0:T(8,128)(2,1)S(1)}, bf16[512,768]{1,0:T(8,128)(2,1)S(1)}, bf16[512,768]{1,0:T(8,128)(2,1)S(1)}, bf16[512,3072]{1,0:T(8,128)(2,1)}, bf16[512,3072]{1,0:T(8,128)(2,1)}) custom-call(bf16[512,768]{1,0:T(8,128)(2,1)S(1)} %copy-done.27, bf16[512,768]{1,0:T(8,128)(2,1)S(1)} %copy-done.29, ...), custom_call_target="tpu_custom_call" | custom-call | flops 9663676416 | bytes 20971520 | tf_op jit(solution)/shard_map/pallas_call | solution.py:633
  237.5 26.8 %shard_map.202 = bf16[8,2,384,768]{3,2,1,0:T(8,128)(2,1)} custom-call(bf16[512,768]{1,0:T(8,128)(2,1)} %copy-done.26, bf16[512,768]{1,0:T(8,128)(2,1)} %copy-done.15, bf16[512,768]{1,0:T(8,128)(2,1)} %copy-done.16, bf16[512,768]{1,0:T(8,128)(2,1)} %collective-permute-done.17.rows_ref.refs_3_, bf16[512,768]{1,0:T(8,128)(2,1)} %copy-done.33, ...), custom_call_target="tpu_custom_call" | custom-call | flops 19327352832 | bytes 41943040 | tf_op jit(solution)/shard_map/pallas_call | solution.py:650
  264.4 3.3 collective-permute-done.24.refs_7_
  268.9 16.4 %shard_map.203 = (bf16[1024,768]{1,0:T(8,128)(2,1)}, f32[1024,768]{1,0:T(8,128)}, bf16[1024,768]{1,0:T(8,128)(2,1)}, bf16[1024,768]{1,0:T(8,128)(2,1)}, f32[1024,4]{1,0:T(8,128)}, /*index=5*/f32[1,768]{1,0:T(1,128)}) custom-call(s32[1024,1]{1,0:T(8,128)} %get-tuple-element.451.slot_ref, f32[1024,768]{1,0:T(8,128)} %copy-done.42, ...), custom_call_target="tpu_custom_call" | custom-call | flops 6442450944 | bytes 20971520 | tf_op jit(solution)/shard_map/pallas_call | solution.py:594
  290.5 15.3 %shard_map.205 = (bf16[3,1024,256]{2,1,0:T(8,128)(2,1)S(1)}, f32[2,2,32,128]{3,2,1,0:T(8,128)S(1)}) custom-call(bf16[1024,2304]{1,0:T(8,128)(2,1)} %copy-done.21, bf16[1024,2304]{1,0:T(8,128)(2,1)} %copy-done.21, bf16[1024,2304]{1,0:T(8,128)(2,1)} %copy-done.21, bf16[1024,768]{1,0:T(8,128)(2,1)S(1)} %copy-done.22, ...), custom_call_target="tpu_custom_call" | custom-call | flops 26666665984 | bytes 8388608 | tf_op jit(solution)/shard_map/pallas_call | solution.py:276
  314.6 15.4 %shard_map.207 = (bf16[3,1024,256]{2,1,0:T(8,128)(2,1)S(1)}, f32[2,2,32,128]{3,2,1,0:T(8,128)S(1)}) custom-call(bf16[1024,2304]{1,0:T(8,128)(2,1)} %copy-done.21, bf16[1024,2304]{1,0:T(8,128)(2,1)} %copy-done.21, bf16[1024,2304]{1,0:T(8,128)(2,1)} %copy-done.21, bf16[1024,768]{1,0:T(8,128)(2,1)S(1)} %copy-done.23, ...), custom_call_target="tpu_custom_call" | custom-call | flops 26666665984 | bytes 8388608 | tf_op jit(solution)/shard_map/pallas_call | solution.py:276
  332.3 3.5 fusion.98
  340.9 15.1 %shard_map.209 = (bf16[3,1024,256]{2,1,0:T(8,128)(2,1)S(1)}, f32[2,2,32,128]{3,2,1,0:T(8,128)S(1)}) custom-call(bf16[1024,2304]{1,0:T(8,128)(2,1)} %copy-done.21, bf16[1024,2304]{1,0:T(8,128)(2,1)} %copy-done.21, bf16[1024,2304]{1,0:T(8,128)(2,1)} %copy-done.21, bf16[1024,768]{1,0:T(8,128)(2,1)S(1)} %copy-done.23, ...), custom_call_target="tpu_custom_call" | custom-call | flops 26666665984 | bytes 8388608 | tf_op jit(solution)/shard_map/pallas_call | solution.py:276
  362.7 8.1 %shard_map.211 = bf16[1024,768]{1,0:T(8,128)(2,1)} custom-call(bf16[3,1024,256]{2,1,0:T(8,128)(2,1)S(1)} %get-tuple-element.304.right_ref.grads_0, bf16[3,1024,256]{2,1,0:T(8,128)(2,1)} %copy-done.3, bf16[3,1024,256]{2,1,0:T(8,128)(2,1)} %copy-done.4, bf16[768,768]{1,0:T(8,128)(2,1)S(1)} %copy-done.8, bf16[768,768]{1,0:T(8,128)(2,1)S(1)} %copy-done.7, ...), custom_call_target="tpu_custom_call" | custom-call | flops 3623878656 | bytes 14680064 | tf_op jit(solution)/shard_map/pallas_call | solution.py:463
  379.7 16.9 %collective-permute-done.34 = bf16[2,96,768]{2,1,0:T(8,128)(2,1)S(1)} collective-permute-done((bf16[2,96,768]{2,1,0:T(8,128)(2,1)S(1)}, bf16[2,96,768]{2,1,0:T(8,128)(2,1)S(1)}, u32[]{:S(2)}, u32[]{:S(2)}) %collective-permute-start.34) | collective-permute-done | bytes 294944 | tf_op jit(solution)/shard_map/ppermute | solution.py:59
  406.8 4.7 %collective-permute-done.36 = bf16[24,3328]{1,0:T(8,128)(2,1)S(1)} collective-permute-done((bf16[24,3328]{1,0:T(8,128)(2,1)S(1)}, bf16[24,3328]{1,0:T(8,128)(2,1)S(1)}, u32[]{:S(2)}, u32[]{:S(2)}) %collective-permute-start.36) | collective-permute-done | bytes 159776 | tf_op jit(solution)/shard_map/ppermute | solution.py:53
  (369 shorter events, 149.0 us)
Async XLA Ops:
  7.2 150.9 %all-gather.2.cloned.1.call-start = ((), (), s32[]{:S(2)}) async-start(), calls=%async_computation.1 | async-start | bytes 10616832 | tf_op jit(solution)/shard_map/all_gather | solution.py:737
  10.5 32.9 %collective-permute-start = (bf16[24,3200]{1,0:T(8,128)(2,1)S(1)}, bf16[24,3200]{1,0:T(8,128)(2,1)}, u32[]{:S(2)}, u32[]{:S(2)}) collective-permute-start(bf16[24,3200]{1,0:T(8,128)(2,1)S(1)} %concatenate.79), channel_id=1, source_target_pairs={{0,24},{1,25},{2,26},{3,27},{4,28},{5,29},{6,30},{7,31},{8,0},{9,1... | collective-permute-start | bytes 460808 | tf_op jit(solution)/shard_map/ppermute | solution.py:53
  15.6 32.0 %collective-permute-start.1 = (bf16[24,3200]{1,0:T(8,128)(2,1)S(1)}, bf16[24,3200]{1,0:T(8,128)(2,1)}, u32[]{:S(2)}, u32[]{:S(2)}) collective-permute-start(bf16[24,3200]{1,0:T(8,128)(2,1)S(1)} %concatenate.79), channel_id=1, source_target_pairs={{0,16},{1,17},{2,18},{3,19},{4,20},{5,21},{6,22},{7,23},{8,24},{9,... | collective-permute-start | bytes 460808 | tf_op jit(solution)/shard_map/ppermute | solution.py:53
  15.6 32.0 %collective-permute-start.2 = (bf16[24,3200]{1,0:T(8,128)(2,1)S(1)}, bf16[24,3200]{1,0:T(8,128)(2,1)}, u32[]{:S(2)}, u32[]{:S(2)}) collective-permute-start(bf16[24,3200]{1,0:T(8,128)(2,1)S(1)} %concatenate.79), channel_id=1, source_target_pairs={{0,8},{1,9},{2,10},{3,11},{4,12},{5,13},{6,14},{7,15},{8,16},{9,17... | collective-permute-start | bytes 460808 | tf_op jit(solution)/shard_map/ppermute | solution.py:53
  23.4 24.2 %collective-permute-start.4 = (bf16[2,96,768]{2,1,0:T(8,128)(2,1)}, bf16[2,96,768]{2,1,0:T(8,128)(2,1)}, u32[]{:S(2)}, u32[]{:S(2)}) collective-permute-start(bf16[2,96,768]{2,1,0:T(8,128)(2,1)} %pad_maximum_fusion.12), channel_id=1, source_target_pairs={{0,4},{1,5},{2,6},{3,7},{4,0},{5,1},{6,2},{7,3},{8,12},{9,13},{10,... | collective-permute-start | bytes 884744 | tf_op jit(solution)/shard_map/ppermute | solution.py:59
  25.7 21.9 %collective-permute-start.3 = (bf16[2,96,768]{2,1,0:T(8,128)(2,1)}, bf16[2,96,768]{2,1,0:T(8,128)(2,1)}, u32[]{:S(2)}, u32[]{:S(2)}) collective-permute-start(bf16[2,96,768]{2,1,0:T(8,128)(2,1)} %pad_maximum_fusion.11), channel_id=1, source_target_pairs={{0,2},{1,3},{2,0},{3,1},{4,6},{5,7},{6,4},{7,5},{8,10},{9,11},{10,... | collective-permute-start | bytes 884744 | tf_op jit(solution)/shard_map/ppermute | solution.py:59
  54.4 317.9 %reduce-scatter.2.cloned.1.call-start = ((), (), s32[]{:S(2)}) async-start(), calls=%async_computation.2 | async-start | bytes 10616832 | tf_op jit(solution)/shard_map/reduce_scatter | solution.py:829
  56.5 26.2 %collective-permute-start.7 = (bf16[96,3200]{1,0:T(8,128)(2,1)S(1)}, bf16[96,3200]{1,0:T(8,128)(2,1)S(1)}, u32[]{:S(2)}, u32[]{:S(2)}) collective-permute-start(bf16[96,3200]{1,0:T(8,128)(2,1)S(1)} %pad_maximum_fusion.7), channel_id=1, source_target_pairs={{0,4},{1,5},{2,6},{3,7},{4,0},{5,1},{6,2},{7,3},{8,12},{9,13},{10,... | collective-permute-start | bytes 1843208 | tf_op jit(solution)/shard_map/ppermute | solution.py:59
  57.0 25.7 %collective-permute-start.8 = (bf16[96,3200]{1,0:T(8,128)(2,1)S(1)}, bf16[96,3200]{1,0:T(8,128)(2,1)S(1)}, u32[]{:S(2)}, u32[]{:S(2)}) collective-permute-start(bf16[96,3200]{1,0:T(8,128)(2,1)S(1)} %pad_maximum_fusion.7), channel_id=1, source_target_pairs={{0,6},{1,7},{2,4},{3,5},{4,2},{5,3},{6,0},{7,1},{8,14},{9,15},{10,... | collective-permute-start | bytes 1843208 | tf_op jit(solution)/shard_map/ppermute | solution.py:59
  94.4 35.4 %collective-permute-start.10 = (bf16[512,768]{1,0:T(8,128)(2,1)}, bf16[512,768]{1,0:T(8,128)(2,1)}, u32[]{:S(2)}, u32[]{:S(2)}) collective-permute-start(bf16[512,768]{1,0:T(8,128)(2,1)} %get-tuple-element.203), channel_id=1, source_target_pairs={{0,2},{1,3},{2,0},{3,1},{4,6},{5,7},{6,4},{7,5},{8,10},{9,11},{10,... | collective-permute-start | bytes 2359304 | tf_op jit(solution)/shard_map/ppermute | solution.py:59
  95.9 36.5 %collective-permute-start.11 = (bf16[512,768]{1,0:T(8,128)(2,1)}, bf16[512,768]{1,0:T(8,128)(2,1)}, u32[]{:S(2)}, u32[]{:S(2)}) collective-permute-start(bf16[512,768]{1,0:T(8,128)(2,1)} %get-tuple-element.204), channel_id=1, source_target_pairs={{0,4},{1,5},{2,6},{3,7},{4,0},{5,1},{6,2},{7,3},{8,12},{9,13},{10,... | collective-permute-start | bytes 2359304 | tf_op jit(solution)/shard_map/ppermute | solution.py:59
  96.5 36.0 %collective-permute-start.12 = (bf16[512,768]{1,0:T(8,128)(2,1)}, bf16[512,768]{1,0:T(8,128)(2,1)}, u32[]{:S(2)}, u32[]{:S(2)}) collective-permute-start(bf16[512,768]{1,0:T(8,128)(2,1)} %get-tuple-element.205), channel_id=1, source_target_pairs={{0,6},{1,7},{2,4},{3,5},{4,2},{5,3},{6,0},{7,1},{8,14},{9,15},{10,... | collective-permute-start | bytes 2359304 | tf_op jit(solution)/shard_map/ppermute | solution.py:59
  142.0 34.5 %collective-permute-start.18 = (bf16[512,768]{1,0:T(8,128)(2,1)}, bf16[512,768]{1,0:T(8,128)(2,1)S(1)}, u32[]{:S(2)}, u32[]{:S(2)}) collective-permute-start(bf16[512,768]{1,0:T(8,128)(2,1)} %get-tuple-element.220), channel_id=1, source_target_pairs={{0,4},{1,5},{2,6},{3,7},{4,0},{5,1},{6,2},{7,3},{8,12},{9,13},{10,... | collective-permute-start | bytes 2359304 | tf_op jit(solution)/shard_map/ppermute | solution.py:59
  156.6 41.8 %collective-permute-start.17 = (bf16[512,768]{1,0:T(8,128)(2,1)}, bf16[512,768]{1,0:T(8,128)(2,1)}, u32[]{:S(2)}, u32[]{:S(2)}) collective-permute-start(bf16[512,768]{1,0:T(8,128)(2,1)} %get-tuple-element.219), channel_id=1, source_target_pairs={{0,6},{1,7},{2,4},{3,5},{4,2},{5,3},{6,0},{7,1},{8,14},{9,15},{10,... | collective-permute-start | bytes 2359304 | tf_op jit(solution)/shard_map/ppermute | solution.py:59
  176.5 21.0 %collective-permute-start.19 = (bf16[512,768]{1,0:T(8,128)(2,1)S(1)}, bf16[512,768]{1,0:T(8,128)(2,1)S(1)}, u32[]{:S(2)}, u32[]{:S(2)}) collective-permute-start(bf16[512,768]{1,0:T(8,128)(2,1)S(1)} %get-tuple-element.233), channel_id=1, source_target_pairs={{0,2},{1,3},{2,0},{3,1},{4,6},{5,7},{6,4},{7,5},{8,10},{9,11},{10,... | collective-permute-start | bytes 2359304 | tf_op jit(solution)/shard_map/ppermute | solution.py:59
  194.7 21.0 %collective-permute-start.21 = (bf16[512,768]{1,0:T(8,128)(2,1)S(1)}, bf16[512,768]{1,0:T(8,128)(2,1)S(1)}, u32[]{:S(2)}, u32[]{:S(2)}) collective-permute-start(bf16[512,768]{1,0:T(8,128)(2,1)S(1)} %get-tuple-element.240), channel_id=1, source_target_pairs={{0,4},{1,5},{2,6},{3,7},{4,0},{5,1},{6,2},{7,3},{8,12},{9,13},{10,... | collective-permute-start | bytes 2359304 | tf_op jit(solution)/shard_map/ppermute | solution.py:59
  195.5 20.2 %collective-permute-start.20 = (bf16[512,768]{1,0:T(8,128)(2,1)S(1)}, bf16[512,768]{1,0:T(8,128)(2,1)S(1)}, u32[]{:S(2)}, u32[]{:S(2)}) collective-permute-start(bf16[512,768]{1,0:T(8,128)(2,1)S(1)} %get-tuple-element.239), channel_id=1, source_target_pairs={{0,2},{1,3},{2,0},{3,1},{4,6},{5,7},{6,4},{7,5},{8,10},{9,11},{10,... | collective-permute-start | bytes 2359304 | tf_op jit(solution)/shard_map/ppermute | solution.py:59
  196.9 37.7 %collective-permute-start.22 = (bf16[512,768]{1,0:T(8,128)(2,1)S(1)}, bf16[512,768]{1,0:T(8,128)(2,1)S(1)}, u32[]{:S(2)}, u32[]{:S(2)}) collective-permute-start(bf16[512,768]{1,0:T(8,128)(2,1)S(1)} %get-tuple-element.249), channel_id=1, source_target_pairs={{0,4},{1,5},{2,6},{3,7},{4,0},{5,1},{6,2},{7,3},{8,12},{9,13},{10,... | collective-permute-start | bytes 2359304 | tf_op jit(solution)/shard_map/ppermute | solution.py:59
  234.6 29.8 %collective-permute-start.23 = (bf16[512,768]{1,0:T(8,128)(2,1)S(1)}, bf16[512,768]{1,0:T(8,128)(2,1)}, u32[]{:S(2)}, u32[]{:S(2)}) collective-permute-start(bf16[512,768]{1,0:T(8,128)(2,1)S(1)} %get-tuple-element.262), channel_id=1, source_target_pairs={{0,6},{1,7},{2,4},{3,5},{4,2},{5,3},{6,0},{7,1},{8,14},{9,15},{10,... | collective-permute-start | bytes 2359304 | tf_op jit(solution)/shard_map/ppermute | solution.py:59
  236.1 31.6 %collective-permute-start.24 = (bf16[512,768]{1,0:T(8,128)(2,1)S(1)}, bf16[512,768]{1,0:T(8,128)(2,1)}, u32[]{:S(2)}, u32[]{:S(2)}) collective-permute-start(bf16[512,768]{1,0:T(8,128)(2,1)S(1)} %get-tuple-element.263), channel_id=1, source_target_pairs={{0,6},{1,7},{2,4},{3,5},{4,2},{5,3},{6,0},{7,1},{8,14},{9,15},{10,... | collective-permute-start | bytes 2359304 | tf_op jit(solution)/shard_map/ppermute | solution.py:59
  336.8 20.5 %collective-permute-start.29 = (bf16[384,768]{1,0:T(8,128)(2,1)}, bf16[384,768]{1,0:T(8,128)(2,1)}, u32[]{:S(2)}, u32[]{:S(2)}) collective-permute-start(bf16[384,768]{1,0:T(8,128)(2,1)} %get-tuple-element.296), channel_id=1, source_target_pairs={{0,1},{1,0},{2,3},{3,2},{4,5},{5,4},{6,7},{7,6},{8,9},{9,8},{10,11... | collective-permute-start | bytes 1769480 | tf_op jit(solution)/shard_map/ppermute | solution.py:63
  374.5 22.2 %collective-permute-start.31 = (bf16[96,1664]{1,0:T(8,128)(2,1)S(1)}, bf16[96,1664]{1,0:T(8,128)(2,1)S(1)}, u32[]{:S(2)}, u32[]{:S(2)}) collective-permute-start(bf16[96,1664]{1,0:T(8,128)(2,1)S(1)} %copy-done.53), channel_id=1, source_target_pairs={{0,2},{1,3},{2,0},{3,1},{4,6},{5,7},{6,4},{7,5},{8,10},{9,11},{10,... | collective-permute-start | bytes 958472 | tf_op jit(solution)/shard_map/ppermute | solution.py:59
  374.7 21.9 %collective-permute-start.32 = (bf16[96,1664]{1,0:T(8,128)(2,1)S(1)}, bf16[96,1664]{1,0:T(8,128)(2,1)S(1)}, u32[]{:S(2)}, u32[]{:S(2)}) collective-permute-start(bf16[96,1664]{1,0:T(8,128)(2,1)S(1)} %get-tuple-element.324), channel_id=1, source_target_pairs={{0,4},{1,5},{2,6},{3,7},{4,0},{5,1},{6,2},{7,3},{8,12},{9,13},{10,... | collective-permute-start | bytes 958472 | tf_op jit(solution)/shard_map/ppermute | solution.py:59
  375.9 20.8 %collective-permute-start.33 = (bf16[96,1664]{1,0:T(8,128)(2,1)S(1)}, bf16[96,1664]{1,0:T(8,128)(2,1)S(1)}, u32[]{:S(2)}, u32[]{:S(2)}) collective-permute-start(bf16[96,1664]{1,0:T(8,128)(2,1)S(1)} %get-tuple-element.325), channel_id=1, source_target_pairs={{0,6},{1,7},{2,4},{3,5},{4,2},{5,3},{6,0},{7,1},{8,14},{9,15},{10,... | collective-permute-start | bytes 958472 | tf_op jit(solution)/shard_map/ppermute | solution.py:59
  (92 other events, 707.9 us)
Sparse Core Ops, SparseCore 0:
  54.6 89.5 all-gather.1
  267.9 99.9 reduce-scatter.1
